TPU v7x, 32 devices: a whole 2x2x4 slice. The times are simulated.
32 devices in a mesh: seq: 32 (over z, y, x, core), tp: 1.
Axes of the slice: x: 2, y: 2, z: 4, core: 2. Of those that a mesh axis runs over, the one named last changes fastest.
Arguments:
- queries: bfloat16 [4096, 4096], P('seq', 'tp'), may hold values from -6 to 6
- keys: bfloat16 [4096, 4096], P('seq', 'tp'), may hold values from -6 to 6
- values: bfloat16 [4096, 4096], P('seq', 'tp'), may hold values from -6 to 6
- w_out: bfloat16 [4096, 4096], P('seq', 'tp'), may hold values from -0.09375 to 0.09375
- taps: bfloat16 [4096, 128], P('tp'), may hold values from -0.6 to 0.6, as said below
- seg_ids: int32 [32], replicated, may hold values from 0 to 3, never falling along the last dimension, each value on 1 to 16 neighbouring positions
- cotangent: bfloat16 [4096, 4096], P('seq', 'tp'), may hold values from -6 to 6
Outputs:
- outputs: bfloat16 [4096, 4096], P('seq', 'tp')
- grad_queries: bfloat16 [4096, 4096], P('seq', 'tp')
- grad_keys: bfloat16 [4096, 4096], P('seq', 'tp')
- grad_values: bfloat16 [4096, 4096], P('seq', 'tp')
- taps_grad: float32 [4096, 128], P(('tp', 'seq'))
Inputs may be any that keep to these rules, and one draw needn't show every extreme that they name: `seg_ids`: ids never fall along the pack, each segment covers 1 to 16 blocks. taps decay along the lag at a rate of each channel.
All inputs are finite; a program needn't handle non-finite values.
Results may differ from a plain program's by a relative error of at most 0.013.
Values may be sent and summed in bfloat16 or wider, within the bound.
No kernel may reach another device: no remote copies, remote signals or barrier semaphores. Data moves between devices by JAX's collectives and lax.ppermute only.
A program may use at most 128 MiB of HBM per device.

v0:
```python
import jax
import jax.numpy as jnp
from jax import lax
from jax.sharding import PartitionSpec as P


def lag_tables(length):
    rows = jnp.arange(length)[:, None]
    cols = jnp.arange(length)[None, :]
    lagged = (rows - cols).reshape(1, -1)
    shifts = jnp.arange(length)[:, None]
    inside = (lagged == shifts).astype(jnp.float32)
    across = (lagged + length == shifts).astype(jnp.float32)
    return (inside, across)


def build_taps(taps_grp, table):
    count, length = taps_grp.shape
    dense = jnp.dot(taps_grp, table.astype(jnp.bfloat16), preferred_element_type=jnp.float32)
    return dense.astype(jnp.bfloat16).reshape(count, length, length)


def to_groups(blocks, group):
    count, length, chans = blocks.shape
    return blocks.reshape(count, length, chans // group, group).transpose(2, 0, 1, 3)


def from_groups(grouped):
    parts, count, length, group = grouped.shape
    return grouped.transpose(1, 2, 0, 3).reshape(count, length, parts * group)


def filter_forward(taps, blocks, before, linked, group):
    length = blocks.shape[1]
    inside, across = lag_tables(length)

    def one_group(items):
        taps_grp, current, prior = items
        near = build_taps(taps_grp, inside)
        far = build_taps(taps_grp, across)
        own = jnp.einsum("cij,bjc->bic", near, current, preferred_element_type=jnp.float32)
        back = jnp.einsum("cij,bjc->bic", far, prior, preferred_element_type=jnp.float32)
        return (own + linked[:, None, None] * back).astype(jnp.bfloat16)

    taps_groups = taps.reshape(-1, group, length)
    result = lax.map(one_group, (taps_groups, to_groups(blocks, group), to_groups(before, group)))
    return from_groups(result)


def filter_backward(taps, grads, after, blocks, before, linked, linked_next, group):
    length = blocks.shape[1]
    inside, across = lag_tables(length)
    dims = (((1,), (1,)), ((), ()))

    def one_group(items):
        taps_grp, grad, later, current, prior = items
        near = build_taps(taps_grp, inside)
        far = build_taps(taps_grp, across)
        own = jnp.einsum("cij,bic->bjc", near, grad, preferred_element_type=jnp.float32)
        ahead = jnp.einsum("cij,bic->bjc", far, later, preferred_element_type=jnp.float32)
        back_grad = (own + linked_next[:, None, None] * ahead).astype(jnp.bfloat16)
        kept = grad * linked[:, None, None].astype(jnp.bfloat16)
        near_sum = jnp.einsum("bic,bjc->cij", grad, current, preferred_element_type=jnp.float32)
        far_sum = jnp.einsum("bic,bjc->cij", kept, prior, preferred_element_type=jnp.float32)
        width = near_sum.shape[0]
        taps_part = lax.dot_general(
            near_sum.reshape(width, -1), inside, dims, precision=lax.Precision.HIGHEST
        )
        taps_part = taps_part + lax.dot_general(
            far_sum.reshape(width, -1), across, dims, precision=lax.Precision.HIGHEST
        )
        return (back_grad, taps_part)

    taps_groups = taps.reshape(-1, group, length)
    back_grp, taps_parts = lax.map(
        one_group,
        (
            taps_groups,
            to_groups(grads, group),
            to_groups(after, group),
            to_groups(blocks, group),
            to_groups(before, group),
        ),
    )
    return (from_groups(back_grp), taps_parts.reshape(-1, length))


def to_channels(tensor):
    return lax.all_to_all(tensor, "seq", split_axis=1, concat_axis=0, tiled=True)


def to_sequence(tensor):
    return lax.all_to_all(tensor, "seq", split_axis=0, concat_axis=1, tiled=True)


def on_device(queries, keys, values, w_out, taps, seg_ids, cotangent):
    rows, chans = queries.shape
    length = taps.shape[1]
    nseq = lax.axis_size("seq")
    place = lax.axis_index("seq")
    weights = lax.all_gather(w_out, "seq", axis=0, tiled=True)
    product = (keys.astype(jnp.float32) * values.astype(jnp.float32)).astype(jnp.bfloat16)
    linked_all = jnp.concatenate(
        [jnp.zeros((1,), jnp.float32), (seg_ids[1:] == seg_ids[:-1]).astype(jnp.float32)]
    )
    linked_ext = jnp.concatenate([linked_all, jnp.zeros((1,), jnp.float32)])
    share = chans // nseq
    group = min(128, share)
    local_taps = lax.dynamic_slice_in_dim(taps, place * share, share, 0)
    spread = to_channels(product)
    blocks = spread.reshape(-1, length, share)
    before = jnp.concatenate([jnp.zeros_like(blocks[:1]), blocks[:-1]], 0)
    mixed = filter_forward(local_taps, blocks, before, linked_all, group)
    filtered = to_sequence(mixed.reshape(-1, share))
    gated = (queries.astype(jnp.float32) * filtered.astype(jnp.float32)).astype(jnp.bfloat16)
    outputs = jnp.dot(
        lax.all_gather(gated, "tp", axis=1, tiled=True), weights, preferred_element_type=jnp.float32
    ).astype(jnp.bfloat16)
    partial_value = lax.dot_general(
        cotangent, weights, (((1,), (1,)), ((), ())), preferred_element_type=jnp.float32
    )
    grad_gated = lax.psum_scatter(partial_value, "tp", scatter_dimension=1, tiled=True).astype(
        jnp.bfloat16
    )
    grad_filtered = (grad_gated.astype(jnp.float32) * queries.astype(jnp.float32)).astype(
        jnp.bfloat16
    )
    grad_queries = (grad_gated.astype(jnp.float32) * filtered.astype(jnp.float32)).astype(
        jnp.bfloat16
    )
    grads = to_channels(grad_filtered).reshape(-1, length, share)
    after = jnp.concatenate([grads[1:], jnp.zeros_like(grads[:1])], 0)
    back, taps_grad = filter_backward(
        local_taps, grads, after, blocks, before, linked_all, linked_ext[1:], group
    )
    grad_product = to_sequence(back.reshape(-1, share))
    grad_float = grad_product.astype(jnp.float32)
    grad_keys = (grad_float * values.astype(jnp.float32)).astype(jnp.bfloat16)
    grad_values = (grad_float * keys.astype(jnp.float32)).astype(jnp.bfloat16)
    return (outputs, grad_queries, grad_keys, grad_values, taps_grad)


def solution(mesh):
    in_specs = (
        P("seq", "tp"),
        P("seq", "tp"),
        P("seq", "tp"),
        P("seq", "tp"),
        P("tp", None),
        P(),
        P("seq", "tp"),
    )
    out_specs = (
        P("seq", "tp"),
        P("seq", "tp"),
        P("seq", "tp"),
        P("seq", "tp"),
        P(("tp", "seq"), None),
    )
    return jax.shard_map(
        on_device, mesh=mesh, in_specs=in_specs, out_specs=out_specs, check_vma=False
    )
```

profile of v0, /device:TPU:0, one launch (start us, length us, event | category | flops | bytes accessed | tf_op | source)
XLA Modules:
  0.0 361.8 jit_solution(222916393019825311)
XLA Ops:
  7.9 1.6 copy.24
  9.6 2.0 copy.23
  12.9 7.3 %all-to-all-start = ((bf16[128,32,128]{0,2,1:T(8,128)(2,1)}), bf16[128,32,128]{0,2,1:T(8,128)(2,1)S(1)}, u32[]{:S(2)}, u32[]{:S(2)}) async-start(bf16[128,32,128]{0,2,1:T(8,128)(2,1)} %bitcast.60), calls=%async_computation | async-start | bytes 2097152 | tf_op jit(solution)/shard_map/all_to_all | solution.py:89
  21.5 3.3 copy.39
  26.1 3.2 copy.40
  29.5 37.6 %all-to-all-done = bf16[128,32,128]{0,2,1:T(8,128)(2,1)S(1)} async-done(((bf16[128,32,128]{0,2,1:T(8,128)(2,1)}), bf16[128,32,128]{0,2,1:T(8,128)(2,1)S(1)}, u32[]{:S(2)}, u32[]{:S(2)}) %all-to-all-start) | async-done | bytes 1048608 | tf_op jit(solution)/shard_map/all_to_all | solution.py:89
  67.8 4.9 %fusion.34 = f32[128,32,128]{2,1,0:T(8,128)S(1)} fusion(bf16[128,128,128]{2,1,0:T(8,128)(2,1)} %bitcast.51, bf16[128,32,128]{0,2,1:T(8,128)(2,1)S(1)} %all-to-all-done), kind=kOutput, calls=%fused_computation.49 | convolution fusion | flops 134217728 | bytes 7340032 | tf_op jit(solution)/shard_map/while/body/eval_jaxpr/cij,bjc->bic/dot_general | solution.py:41
  72.7 2.3 fusion.18
  75.4 58.9 %all_to_all.52 = bf16[32,128,128]{1,2,0:T(8,128)(2,1)S(1)} all-to-all(bf16[32,128,128]{1,2,0:T(8,128)(2,1)S(1)} %copy.27), channel_id=1, replica_groups=mesh['seq'=32,'tp'=1] {'seq'}, dimensions={0} | all-to-all | bytes 2097152 | tf_op jit(solution)/shard_map/all_to_all | solution.py:93
  134.4 1.6 convert_element_type.149
  136.0 1.9 copy.28
  137.9 110.7 %all-gather.2.cloned.1.call-done = bf16[4096,4096]{1,0:T(8,128)(2,1)} async-done(((bf16[128,4096]{1,0:T(8,128)(2,1)}), bf16[4096,4096]{1,0:T(8,128)(2,1)}) %all-gather.2.cloned.1.call-update) | async-done | bytes 33554448 | tf_op jit(solution)/shard_map/all_gather | solution.py:101
  248.7 17.2 %fusion.14 = (bf16[128,4096]{1,0:T(8,128)(2,1)}, bf16[128,4096]{1,0:T(8,128)(2,1)}) fusion(bf16[128,4096]{1,0:T(8,128)(2,1)S(1)} %copy-done.13, f32[128,4096]{1,0:T(8,128)S(1)} %copy.28, bf16[128,4096]{1,0:T(8,128)(2,1)} %param.13, bf16[4096,4096]{1,0:T(8,128)(2,1)} %all-gather.2.cloned.1.call-done), kind=kOutput, calls=%fused_computation.27 | convolution fusion | flops 4298637312 | bytes 39845888 | tf_op jit(solution)/shard_map/dot_general | solution.py:119
  265.9 2.3 copy.38
  268.2 2.8 all-to-all-start.2
  271.0 26.2 %all-to-all-done.2 = bf16[128,32,128]{0,2,1:T(8,128)(2,1)S(1)} async-done(((bf16[128,32,128]{0,2,1:T(8,128)(2,1)}), bf16[128,32,128]{0,2,1:T(8,128)(2,1)S(1)}, u32[]{:S(2)}, u32[]{:S(2)}) %all-to-all-start.2) | async-done | bytes 1048608 | tf_op jit(solution)/shard_map/all_to_all | solution.py:89
  304.1 4.2 %all-to-all-start.3 = ((bf16[32,128,128]{1,2,0:T(8,128)(2,1)}), bf16[32,128,128]{1,2,0:T(8,128)(2,1)}, u32[]{:S(2)}, u32[]{:S(2)}) async-start(bf16[32,128,128]{1,2,0:T(8,128)(2,1)} %copy.33), calls=%async_computation.3 | async-start | bytes 2097152 | tf_op jit(solution)/shard_map/all_to_all | solution.py:93
  308.3 16.4 %convolution_convert_fusion.3 = bf16[128,4096]{1,0:T(8,128)(2,1)} fusion(bf16[4096,4096]{1,0:T(8,128)(2,1)} %all-gather.2.cloned.1.call-done, f32[128,4096]{1,0:T(8,128)S(1)} %copy.28, bf16[128,4096]{1,0:T(8,128)(2,1)} %param.7), kind=kOutput, calls=%fused_computation.14 | convolution fusion | flops 4297064448 | bytes 37748736 | tf_op jit(solution)/shard_map/dot_general | solution.py:116
  324.7 1.6 fusion.24
  326.3 9.2 %fusion = f32[128,128]{1,0:T(8,128)S(1)} fusion(f32[16,8,128,128]{3,2,1,0:T(8,128)S(1)} %bitcast.56, s32[16384]{0:T(1024)S(1)} %broadcast_add_fusion), kind=kOutput, calls=%fused_computation.2 | convolution fusion | flops 3223322624 | bytes 8519680 | tf_op jit(solution)/shard_map/while/body/eval_jaxpr/dot_general | solution.py:69
  337.1 10.1 %fusion.20 = f32[128,128]{1,0:T(8,128)} fusion(f32[128,128]{1,0:T(8,128)S(1)} %fusion, s32[16384]{0:T(1024)S(1)} %subtract_bitcast_fusion, f32[16,8,128,128]{3,2,1,0:T(8,128)S(1)} %bitcast.55), kind=kOutput, calls=%fused_computation.36 | convolution fusion | flops 3223339008 | bytes 8585216 | tf_op jit(solution)/shard_map/while/body/eval_jaxpr/dot_general | solution.py:66
  347.2 3.0 fusion.15
  350.2 2.3 copy.36
  352.5 2.3 copy.37
  (49 shorter events, 14.4 us)
Async XLA Ops:
  7.2 13.0 %copy-start = (bf16[4096,128]{1,0:T(8,128)(2,1)S(1)}, bf16[4096,128]{1,0:T(8,128)(2,1)}, u32[]{:S(2)}) copy-start(bf16[4096,128]{1,0:T(8,128)(2,1)} %param.11) | copy-start | bytes 3145732
  7.2 241.5 %all-gather.2.cloned.1.call-start = ((), (), s32[]{:S(2)}) async-start(), calls=%async_computation.4 | async-start | bytes 34603008 | tf_op jit(solution)/shard_map/all_gather | solution.py:101
  9.5 3.3 copy-start.7
  11.6 9.9 %copy-start.9 = (bf16[128,4096]{0,1:T(8,128)(2,1)}, bf16[128,4096]{0,1:T(8,128)(2,1)S(1)}, u32[]{:S(2)}) copy-start(bf16[128,4096]{0,1:T(8,128)(2,1)S(1)} %copy.23) | copy-start | bytes 3145732
  12.9 54.2 %all-to-all-start = ((bf16[128,32,128]{0,2,1:T(8,128)(2,1)}), bf16[128,32,128]{0,2,1:T(8,128)(2,1)S(1)}, u32[]{:S(2)}, u32[]{:S(2)}) async-start(bf16[128,32,128]{0,2,1:T(8,128)(2,1)} %bitcast.60), calls=%async_computation | async-start | bytes 2097152 | tf_op jit(solution)/shard_map/all_to_all | solution.py:89
  26.1 3.3 copy-start.14
  67.1 5.6 %copy-start.5 = (bf16[128,32,128]{0,2,1:T(8,128)(2,1)}, bf16[128,32,128]{0,2,1:T(8,128)(2,1)S(1)}, u32[]{:S(2)}) copy-start(bf16[128,32,128]{0,2,1:T(8,128)(2,1)S(1)} %all-to-all-done) | copy-start | bytes 3145732
  67.8 7.2 %copy-start.11 = (bf16[128,32,128]{0,1,2:T(8,128)(2,1)}, bf16[128,32,128]{0,1,2:T(8,128)(2,1)S(1)}, u32[]{:S(2)}) copy-start(bf16[128,32,128]{0,1,2:T(8,128)(2,1)S(1)} %copy.67) | copy-start | bytes 3145732
  67.8 4.9 %copy-start.3 = (bf16[16,8,128,128]{3,2,1,0:T(8,128)(2,1)S(1)}, bf16[16,8,128,128]{3,2,1,0:T(8,128)(2,1)}, u32[]{:S(2)}) copy-start(bf16[16,8,128,128]{3,2,1,0:T(8,128)(2,1)} %copy.40) | copy-start | bytes 12582916
  134.4 114.3 %copy-start.13 = (bf16[128,4096]{1,0:T(8,128)(2,1)S(1)}, bf16[128,4096]{1,0:T(8,128)(2,1)}, u32[]{:S(2)}) copy-start(bf16[128,4096]{1,0:T(8,128)(2,1)} %param.7) | copy-start | bytes 3145732
  268.2 29.0 %all-to-all-start.2 = ((bf16[128,32,128]{0,2,1:T(8,128)(2,1)}), bf16[128,32,128]{0,2,1:T(8,128)(2,1)S(1)}, u32[]{:S(2)}, u32[]{:S(2)}) async-start(bf16[128,32,128]{0,2,1:T(8,128)(2,1)} %bitcast.61), calls=%async_computation.2 | async-start | bytes 2097152 | tf_op jit(solution)/shard_map/all_to_all | solution.py:89
  297.2 2.2 copy-start.2
  299.4 2.2 copy-start.4
  304.1 43.0 %all-to-all-start.3 = ((bf16[32,128,128]{1,2,0:T(8,128)(2,1)}), bf16[32,128,128]{1,2,0:T(8,128)(2,1)}, u32[]{:S(2)}, u32[]{:S(2)}) async-start(bf16[32,128,128]{1,2,0:T(8,128)(2,1)} %copy.33), calls=%async_computation.3 | async-start | bytes 2097152 | tf_op jit(solution)/shard_map/all_to_all | solution.py:93
  308.3 16.4 %copy-start.12 = (bf16[128,32,128]{0,1,2:T(8,128)(2,1)S(1)}, bf16[128,32,128]{0,1,2:T(8,128)(2,1)}, u32[]{:S(2)}) copy-start(bf16[128,32,128]{0,1,2:T(8,128)(2,1)} %copy-done.11) | copy-start | bytes 3145732
  326.3 9.2 %copy-start.6 = (bf16[128,32,128]{0,2,1:T(8,128)(2,1)S(1)}, bf16[128,32,128]{0,2,1:T(8,128)(2,1)}, u32[]{:S(2)}) copy-start(bf16[128,32,128]{0,2,1:T(8,128)(2,1)} %copy-done.5) | copy-start | bytes 3145732
  337.1 10.1 %copy-start.8 = (bf16[128,4096]{0,1:T(8,128)(2,1)S(1)}, bf16[128,4096]{0,1:T(8,128)(2,1)}, u32[]{:S(2)}) copy-start(bf16[128,4096]{0,1:T(8,128)(2,1)} %copy-done.7) | copy-start | bytes 3145732
  337.1 10.1 %copy-start.10 = (bf16[128,4096]{0,1:T(8,128)(2,1)S(1)}, bf16[128,4096]{0,1:T(8,128)(2,1)}, u32[]{:S(2)}) copy-start(bf16[128,4096]{0,1:T(8,128)(2,1)} %copy-done.9) | copy-start | bytes 3145732
  337.1 17.6 %copy-start.1 = (bf16[4096,128]{1,0:T(8,128)(2,1)S(1)}, bf16[4096,128]{1,0:T(8,128)(2,1)}, u32[]{:S(2)}) copy-start(bf16[4096,128]{1,0:T(8,128)(2,1)} %param.11) | copy-start | bytes 3145732
Sparse Core Ops, SparseCore 0:
  10.9 237.7 all-gather.1
where the time goes:
time: 369 us; the launch traced here: 362 us
  waiting for transfers between devices  175 us (47%)
  matrix products  68.2 us (18%)
  blocking collectives  58.9 us (16%)
  local copies, waits for them, and re-layouts  24.5 us (7%)
  between operations  14.5 us (4%)
  starting transfers between devices  14.3 us (4%)
  other arithmetic  6.17 us (2%)
    all_gather x1, waiting for transfers between devices, on_device(): weights = lax.all_gather(w_out, 'seq', axis=0, tiled=True)  111 us
    all_to_all x2, waiting for transfers between devices, to_channels(): lax.all_to_all(tensor, 'seq', split_axis=1, concat_axis=0, tiled=True)  63.8 us
    all_to_all x1, blocking collectives, to_sequence(): lax.all_to_all(tensor, 'seq', split_axis=0, concat_axis=1, tiled=True)  58.9 us
    dot_general x1, matrix products, on_device(): lax.dot_general(cotangent, weights, (((1,), (1,)), ((), ())), preferred_e...  17.2 us
    unnamed x36, local copies, waits for them, and re-layouts  16.6 us
    dot_general x1, matrix products, on_device(): jnp.dot(lax.all_gather(gated, 'tp', axis=1, tiled=True), weights, preferr...  16.4 us
    all_to_all x2, starting transfers between devices, to_channels(): lax.all_to_all(tensor, 'seq', split_axis=1, concat_axis=0, tiled=True)  10.1 us
    dot_general x1, matrix products, one_group(): lax.dot_general(near_sum.reshape(width, -1), inside, dims, precision=lax....  10.1 us
  transfers between devices with their start and end apart: 4, of which 3 were waited for; matrix products, arithmetic and copies ran while one was open for 18% of the time, Pallas kernels for 0%

commit v1 on v0

v1 whole, which is shorter than its diff:
```python
import jax
import jax.numpy as jnp
import numpy as np
from jax import lax
from jax.sharding import PartitionSpec as P

F32 = jnp.float32
BF16 = jnp.bfloat16


def spectrum_table(length):
    angles = np.pi * (2 * np.arange(length)[:, None] + 1) * np.arange(-length, length)[None, :] / (2 * length)
    table = np.concatenate([np.cos(angles), -np.sin(angles)], 0).astype(np.float32)
    high = table.astype(BF16)
    low = (table - high.astype(np.float32)).astype(BF16)
    return table, high, low


def forward_dft(high, low, data, dims):
    first = lax.dot_general(high, data, (dims, ((), ())), preferred_element_type=F32)
    second = lax.dot_general(low, data, (dims, ((), ())), preferred_element_type=F32)
    return first + second


def times(a, b):
    half = a.shape[0] // 2
    ar, ai, br, bi = a[:half], a[half:], b[:half], b[half:]
    return jnp.concatenate([ar * br - ai * bi, ar * bi + ai * br], 0)


def times_conj(a, b):
    half = a.shape[0] // 2
    ar, ai, br, bi = a[:half], a[half:], b[:half], b[half:]
    return jnp.concatenate([ar * br + ai * bi, ai * br - ar * bi], 0)


def inverse_dft(table, spectrum, scale):
    done = lax.dot_general(
        table, spectrum, (((0,), (0,)), ((), ())), precision=lax.Precision.HIGH, preferred_element_type=F32
    )
    return done * scale


def mul(a, b):
    return (a.astype(F32) * b.astype(F32)).astype(BF16)


def scatter_sum(part, nseq, place):
    chans, lags = part.shape
    bits = nseq.bit_length() - 1
    if nseq != 1 << bits:
        return lax.psum_scatter(part, "seq", scatter_dimension=0, tiled=True)
    for step in range(bits):
        mine = (place >> step) & 1
        part = part.reshape(-1, 2, chans // nseq, lags)
        away = lax.dynamic_index_in_dim(part, 1 - mine, 1, False)
        kept = lax.dynamic_index_in_dim(part, mine, 1, False)
        part = kept + lax.ppermute(away, "seq", [(i, i ^ (1 << step)) for i in range(nseq)])
    return part.reshape(chans // nseq, lags)


def on_device(queries, keys, values, w_out, taps, seg_ids, cotangent):
    rows, chans = queries.shape
    length = taps.shape[1]
    assert rows == length
    nseq = lax.axis_size("seq")
    place = lax.axis_index("seq")
    table, high, low = spectrum_table(length)
    table_now, high_now, low_now = table[:, length:], high[:, length:], low[:, length:]
    scale = 1.0 / length
    weights = lax.all_gather(w_out, "seq", axis=0, tiled=True)
    later = [(i, i + 1) for i in range(nseq - 1)]
    earlier = [(i + 1, i) for i in range(nseq - 1)]
    own = lax.dynamic_index_in_dim(seg_ids, place, 0, False)
    prior = lax.dynamic_index_in_dim(seg_ids, jnp.maximum(place - 1, 0), 0, False)
    linked = (place > 0) & (own == prior)

    product = mul(keys, values)
    before = lax.ppermute(product, "seq", later)
    before = jnp.where(linked, before, jnp.zeros_like(before))
    data = forward_dft(high, low, jnp.concatenate([before, product], 0), ((1,), (0,)))
    filt = forward_dft(high_now, low_now, taps, ((1,), (1,)))
    filtered = inverse_dft(table_now, times(filt, data), scale).astype(BF16)
    gated = mul(queries, filtered)

    grad_gated = lax.dot_general(cotangent, weights, (((1,), (1,)), ((), ())), preferred_element_type=F32)
    grad_gated = lax.psum_scatter(grad_gated, "tp", scatter_dimension=1, tiled=True).astype(BF16)
    grad_queries = mul(grad_gated, filtered)
    grad_filtered = mul(grad_gated, queries)
    grads = forward_dft(high_now, low_now, grad_filtered, ((1,), (0,)))
    back = inverse_dft(table, times_conj(grads, filt), scale)
    across = jnp.where(linked, back[:length], 0.0).astype(BF16)
    ahead = lax.ppermute(across, "seq", earlier)
    taps_part = lax.dot_general(
        times_conj(grads, data), table_now, (((0,), (0,)), ((), ())),
        precision=lax.Precision.HIGH, preferred_element_type=F32,
    ) * scale
    taps_grad = scatter_sum(taps_part, nseq, place)
    outputs = jnp.dot(
        lax.all_gather(gated, "tp", axis=1, tiled=True), weights, preferred_element_type=F32
    ).astype(BF16)
    grad_product = (back[length:] + ahead.astype(F32)).astype(BF16)
    grad_keys = mul(grad_product, values)
    grad_values = mul(grad_product, keys)
    return (outputs, grad_queries, grad_keys, grad_values, taps_grad)


def solution(mesh):
    block = P("seq", "tp")
    return jax.shard_map(
        on_device,
        mesh=mesh,
        in_specs=(block, block, block, block, P("tp", None), P(), block),
        out_specs=(block, block, block, block, P(("tp", "seq"), None)),
        check_vma=False,
    )
```

time: 369 us -> 339 us (0.919); the launches traced: 362 us -> 338 us
  blocking collectives: 58.9 us -> 0 us
  waiting for transfers between devices: 175 us -> 205 us
  starting transfers between devices: 14.3 us -> 36.4 us
  matrix products: 68.2 us -> 52.1 us
  local copies, waits for them, and re-layouts: 24.5 us -> 20.7 us
    all_gather x1, waiting for transfers between devices: 111 us -> 193 us  [on_device(): weights = lax.all_gather(w_out, 'seq', axis=0, tiled=True)]
    all_to_all x3 -> x0, waiting for transfers between devices: 63.8 us -> none  [the longest x2 63.8 us: to_channels(): lax.all_to_all(tensor, 'seq', split_axis=1, concat_axis=0, tiled=True)]
    all_to_all x1 -> x0, blocking collectives: 58.9 us -> none  [to_sequence(): lax.all_to_all(tensor, 'seq', split_axis=0, concat_axis=1, tiled=True)]
    ppermute x0 -> x7, starting transfers between devices: none -> 36.4 us  [the longest x5 21.5 us: scatter_sum(): lax.ppermute(away, 'seq', [(i, i ^ 1 << step) for i in range(nseq)])]
    all_to_all x3 -> x0, starting transfers between devices: 14.2 us -> none  [the longest x2 10.1 us: to_channels(): lax.all_to_all(tensor, 'seq', split_axis=1, concat_axis=0, tiled=True)]
    ppermute x0 -> x7, waiting for transfers between devices: none -> 11.8 us  [the longest x5 11.8 us: scatter_sum(): lax.ppermute(away, 'seq', [(i, i ^ 1 << step) for i in range(nseq)])]
    dot_general x10 -> x14, matrix products: 34.6 us -> 23.5 us  [the longest x4 12 us: inverse_dft(): lax.dot_general(table, spectrum, (((0,), (0,)), ((), ())), precision=lax....]
    convert_element_type x3 -> x0, local copies, waits for them, and re-layouts: 3.73 us -> none  [the longest x1 1.93 us: on_device(): filtered.astype(jnp.float32)]
  transfers between devices with their start and end apart: 4 -> 8, of which waited for: 3 -> 5; matrix products, arithmetic and copies ran while one was open for 18% -> 12% of each run, Pallas kernels for 0% -> 0%
where the time goes in v1:
time: 339 us; the launch traced here: 338 us
  waiting for transfers between devices  205 us (60%)
  matrix products  52.1 us (15%)
  starting transfers between devices  36.4 us (11%)
  local copies, waits for them, and re-layouts  20.7 us (6%)
  between operations  15.7 us (5%)
  other arithmetic  8.25 us (2%)
    all_gather x1, waiting for transfers between devices, on_device(): weights = lax.all_gather(w_out, 'seq', axis=0, tiled=True)  193 us
    ppermute x5, starting transfers between devices, scatter_sum(): lax.ppermute(away, 'seq', [(i, i ^ 1 << step) for i in range(nseq)])  21.5 us
    unnamed x48, local copies, waits for them, and re-layouts  19.1 us
    dot_general x1, matrix products, on_device(): lax.dot_general(cotangent, weights, (((1,), (1,)), ((), ())), preferred_e...  14.4 us
    dot_general x1, matrix products, on_device(): jnp.dot(lax.all_gather(gated, 'tp', axis=1, tiled=True), weights, preferr...  14.2 us
    ppermute x1, starting transfers between devices, on_device(): before = lax.ppermute(product, 'seq', later)  13.5 us
    dot_general x4, matrix products, inverse_dft(): lax.dot_general(table, spectrum, (((0,), (0,)), ((), ())), precision=lax....  12 us
    ppermute x5, waiting for transfers between devices, scatter_sum(): lax.ppermute(away, 'seq', [(i, i ^ 1 << step) for i in range(nseq)])  11.8 us
  transfers between devices with their start and end apart: 8, of which 5 were waited for; matrix products, arithmetic and copies ran while one was open for 12% of the time, Pallas kernels for 0%

profile of v1, /device:TPU:0, one launch (start us, length us, event | category | flops | bytes accessed | tf_op | source)
XLA Modules:
  0.0 338.3 jit_solution(9864419733069532107)
XLA Ops:
  7.9 2.3 copy.57
  13.0 2.8 convolution_add_fusion.4
  15.8 192.7 %all-gather.2.cloned.1.call-done = bf16[4096,4096]{1,0:T(8,128)(2,1)} async-done(((bf16[128,4096]{1,0:T(8,128)(2,1)}), bf16[4096,4096]{1,0:T(8,128)(2,1)}) %all-gather.2.cloned.1.call-update) | async-done | bytes 33554448 | tf_op jit(solution)/shard_map/all_gather | solution.py:71
  208.4 14.4 %fusion.10 = f32[128,4096]{0,1:T(8,128)S(1)} fusion(bf16[128,4096]{1,0:T(8,128)(2,1)} %param.19, bf16[4096,4096]{1,0:T(8,128)(2,1)} %all-gather.2.cloned.1.call-done), kind=kOutput, calls=%fused_computation.18 | convolution fusion | flops 4296015872 | bytes 36700160 | tf_op jit(solution)/shard_map/dot_general | solution.py:86
  225.7 2.3 fusion.28
  228.1 2.3 fusion.1
  230.4 1.9 copy-done.10
  233.8 2.3 copy.58
  236.1 2.3 copy.59
  238.4 4.5 %fusion.15 = (bf16[128,4096]{0,1:T(8,128)(2,1)}, bf16[128,4096]{0,1:T(8,128)(2,1)}, bf16[128,4096]{0,1:T(8,128)(2,1)S(1)}) fusion(bf16[128,4096]{0,1:T(8,128)(2,1)} %copy.58, bf16[128,4096]{0,1:T(8,128)(2,1)} %collective-permute-done.1, f32[256,4096]{0,1:T(8,128)} %copy-done.10, bf16[128,4096]{0,1:T(8,128)(2,1)} %copy.59), kind=kLoop, calls=%fused_computation.29 | loop fusion | flops 6291456 | bytes 8388608 | tf_op jit(solution)/shard_map/convert_element_type | solution.py:45
  242.8 13.5 %collective-permute-start = (bf16[128,4096]{0,1:T(8,128)(2,1)S(1)}, bf16[128,4096]{0,1:T(8,128)(2,1)}, u32[]{:S(2)}, u32[]{:S(2)}) collective-permute-start(bf16[128,4096]{0,1:T(8,128)(2,1)S(1)} %get-tuple-element.27), channel_id=1, source_target_pairs={{0,1},{1,2},{2,3},{3,4},{4,5},{5,6},{6,7},{7,8},{8,9},{9,10},{10,1... | collective-permute-start | bytes 3145736 | tf_op jit(solution)/shard_map/ppermute | solution.py:79
  260.9 1.8 fusion.21
  262.9 1.9 fusion.5
  266.2 10.8 %collective-permute-start.2 = (f32[16,128,128]{2,1,0:T(8,128)S(1)}, f32[16,128,128]{2,1,0:T(8,128)}, u32[]{:S(2)}, u32[]{:S(2)}) collective-permute-start(f32[16,128,128]{2,1,0:T(8,128)S(1)} %dynamic-slice_bitcast_fusion), channel_id=1, source_target_pairs={{0,1},{1,0},{2,3},{3,2},{4,5},{5,4},{6,7},{7,6},{8,9},{9,8},{10,11... | collective-permute-start | bytes 3145736 | tf_op jit(solution)/shard_map/ppermute | solution.py:58
  277.0 2.4 collective-permute-done.2
  281.9 2.8 collective-permute-start.3
  284.7 2.3 copy.68
  287.0 2.3 copy.69
  289.3 8.0 %collective-permute-done.3 = f32[8,128,128]{2,1,0:T(8,128)} collective-permute-done((f32[8,128,128]{2,1,0:T(8,128)}, f32[8,128,128]{2,1,0:T(8,128)}, u32[]{:S(2)}, u32[]{:S(2)}) %collective-permute-start.3) | collective-permute-done | bytes 524320 | tf_op jit(solution)/shard_map/ppermute | solution.py:58
  298.6 3.6 %collective-permute-start.4 = (f32[4,128,128]{2,1,0:T(8,128)S(1)}, f32[4,128,128]{2,1,0:T(8,128)S(1)}, u32[]{:S(2)}, u32[]{:S(2)}) collective-permute-start(f32[4,128,128]{2,1,0:T(8,128)S(1)} %dynamic-slice_bitcast_fusion.2), channel_id=1, source_target_pairs={{0,4},{1,5},{2,6},{3,7},{4,0},{5,1},{6,2},{7,3},{8,12},{9,13},{10,... | collective-permute-start | bytes 786440 | tf_op jit(solution)/shard_map/ppermute | solution.py:58
  302.1 5.4 %fusion.35 = f32[4096,128]{1,0:T(8,128)S(1)} fusion(f32[128,128]{1,0:T(8,128)S(1)} %copy-done.15, f32[256,4096]{1,0:T(8,128)} %copy-done.4, f32[256,4096]{1,0:T(8,128)} %convolution_add_fusion.4), kind=kOutput, calls=%fused_computation.52 | convolution fusion | flops 404226048 | bytes 10551296 | tf_op jit(solution)/shard_map/dot_general | solution.py:38
  308.0 2.7 collective-permute-start.5
  310.7 1.9 multiply_convert_fusion
  315.3 14.2 %convolution_convert_fusion.1 = bf16[128,4096]{1,0:T(8,128)(2,1)} fusion(bf16[4096,4096]{1,0:T(8,128)(2,1)} %all-gather.2.cloned.1.call-done, f32[128,4096]{0,1:T(8,128)S(1)} %get-tuple-element.31, bf16[128,4096]{0,1:T(8,128)(2,1)S(1)} %copy-done.9), kind=kOutput, calls=%fused_computation.19 | convolution fusion | flops 4297064448 | bytes 37748736 | tf_op jit(solution)/shard_map/dot_general | solution.py:99
  (70 shorter events, 21.3 us)
Async XLA Ops:
  7.2 4.9 %copy-start = (bf16[4096,128]{1,0:T(8,128)(2,1)S(1)}, bf16[4096,128]{1,0:T(8,128)(2,1)}, u32[]{:S(2)}) copy-start(bf16[4096,128]{1,0:T(8,128)(2,1)} %param.17) | copy-start | bytes 3145732
  7.2 4.9 %copy-start.13 = (bf16[256,128]{1,0:T(8,128)(2,1)S(1)}, bf16[256,128]{1,0:T(8,128)(2,1)}, u32[]{:S(2)}) copy-start(bf16[256,128]{1,0:T(8,128)(2,1)} %constant.81.clone) | copy-start | bytes 196612
  7.2 3.0 copy-start.20
  7.2 201.2 %all-gather.2.cloned.1.call-start = ((), (), s32[]{:S(2)}) async-start(), calls=%async_computation | async-start | bytes 34603008 | tf_op jit(solution)/shard_map/all_gather | solution.py:71
  15.8 207.0 %copy-start.8 = (bf16[128,4096]{0,1:T(8,128)(2,1)S(1)}, bf16[128,4096]{0,1:T(8,128)(2,1)}, u32[]{:S(2)}) copy-start(bf16[128,4096]{0,1:T(8,128)(2,1)} %copy.57) | copy-start | bytes 3145732
  223.5 2.2 copy-start.2
  223.5 2.2 copy-start.17
  225.7 2.3 copy-start.6
  225.7 2.3 copy-start.16
  232.5 5.8 %collective-permute-start.1 = (bf16[128,4096]{0,1:T(8,128)(2,1)S(1)}, bf16[128,4096]{0,1:T(8,128)(2,1)}, u32[]{:S(2)}, u32[]{:S(2)}) collective-permute-start(bf16[128,4096]{0,1:T(8,128)(2,1)S(1)} %fusion.16), channel_id=1, source_target_pairs={{1,0},{2,1},{3,2},{4,3},{5,4},{6,5},{7,6},{8,7},{9,8},{10,9},{11,1... | collective-permute-start | bytes 3145736 | tf_op jit(solution)/shard_map/ppermute | solution.py:93
  242.8 15.0 %collective-permute-start = (bf16[128,4096]{0,1:T(8,128)(2,1)S(1)}, bf16[128,4096]{0,1:T(8,128)(2,1)}, u32[]{:S(2)}, u32[]{:S(2)}) collective-permute-start(bf16[128,4096]{0,1:T(8,128)(2,1)S(1)} %get-tuple-element.27), channel_id=1, source_target_pairs={{0,1},{1,2},{2,3},{3,4},{4,5},{5,6},{6,7},{7,8},{8,9},{9,10},{10,1... | collective-permute-start | bytes 3145736 | tf_op jit(solution)/shard_map/ppermute | solution.py:79
  258.7 2.2 copy-start.7
  258.7 2.2 copy-start.15
  260.8 2.0 copy-start.4
  260.8 2.0 copy-start.14
  266.2 13.2 %collective-permute-start.2 = (f32[16,128,128]{2,1,0:T(8,128)S(1)}, f32[16,128,128]{2,1,0:T(8,128)}, u32[]{:S(2)}, u32[]{:S(2)}) collective-permute-start(f32[16,128,128]{2,1,0:T(8,128)S(1)} %dynamic-slice_bitcast_fusion), channel_id=1, source_target_pairs={{0,1},{1,0},{2,3},{3,2},{4,5},{5,4},{6,7},{7,6},{8,9},{9,8},{10,11... | collective-permute-start | bytes 3145736 | tf_op jit(solution)/shard_map/ppermute | solution.py:58
  281.9 15.4 %collective-permute-start.3 = (f32[8,128,128]{2,1,0:T(8,128)}, f32[8,128,128]{2,1,0:T(8,128)}, u32[]{:S(2)}, u32[]{:S(2)}) collective-permute-start(f32[8,128,128]{2,1,0:T(8,128)} %dynamic-slice_bitcast_fusion.1), channel_id=1, source_target_pairs={{0,2},{1,3},{2,0},{3,1},{4,6},{5,7},{6,4},{7,5},{8,10},{9,11},{10,... | collective-permute-start | bytes 1572872 | tf_op jit(solution)/shard_map/ppermute | solution.py:58
  297.3 13.5 %copy-start.5 = (f32[256,4096]{1,0:T(8,128)S(1)}, f32[256,4096]{1,0:T(8,128)}, u32[]{:S(2)}) copy-start(f32[256,4096]{1,0:T(8,128)} %copy-done.4) | copy-start | bytes 12582916
  298.6 9.3 %collective-permute-start.4 = (f32[4,128,128]{2,1,0:T(8,128)S(1)}, f32[4,128,128]{2,1,0:T(8,128)S(1)}, u32[]{:S(2)}, u32[]{:S(2)}) collective-permute-start(f32[4,128,128]{2,1,0:T(8,128)S(1)} %dynamic-slice_bitcast_fusion.2), channel_id=1, source_target_pairs={{0,4},{1,5},{2,6},{3,7},{4,0},{5,1},{6,2},{7,3},{8,12},{9,13},{10,... | collective-permute-start | bytes 786440 | tf_op jit(solution)/shard_map/ppermute | solution.py:58
  302.1 8.6 %copy-start.3 = (f32[256,4096]{1,0:T(8,128)S(1)}, f32[256,4096]{1,0:T(8,128)}, u32[]{:S(2)}) copy-start(f32[256,4096]{1,0:T(8,128)} %convolution_add_fusion.4) | copy-start | bytes 12582916
  308.0 7.3 %copy-start.9 = (bf16[128,4096]{0,1:T(8,128)(2,1)S(1)}, bf16[128,4096]{0,1:T(8,128)(2,1)}, u32[]{:S(2)}) copy-start(bf16[128,4096]{0,1:T(8,128)(2,1)} %copy.57) | copy-start | bytes 3145732
  308.0 5.7 %collective-permute-start.5 = (f32[2,128,128]{2,1,0:T(8,128)S(1)}, f32[2,128,128]{2,1,0:T(8,128)S(1)}, u32[]{:S(2)}, u32[]{:S(2)}) collective-permute-start(f32[2,128,128]{2,1,0:T(8,128)S(1)} %dynamic-slice_bitcast_fusion.3), channel_id=1, source_target_pairs={{0,8},{1,9},{2,10},{3,11},{4,12},{5,13},{6,14},{7,15},{8,0},{9,1},... | collective-permute-start | bytes 393224 | tf_op jit(solution)/shard_map/ppermute | solution.py:58
  313.7 17.1 %collective-permute-start.6 = (f32[1,128,128]{2,1,0:T(8,128)S(1)}, f32[1,128,128]{2,1,0:T(8,128)S(1)}, u32[]{:S(2)}, u32[]{:S(2)}) collective-permute-start(f32[1,128,128]{2,1,0:T(8,128)S(1)} %constant_dynamic-slice_fusion), channel_id=1, source_target_pairs={{0,16},{1,17},{2,18},{3,19},{4,20},{5,21},{6,22},{7,23},{8,24},{9,... | collective-permute-start | bytes 196616 | tf_op jit(solution)/shard_map/ppermute | solution.py:58
  315.3 16.1 %copy-start.1 = (bf16[4096,128]{1,0:T(8,128)(2,1)S(1)}, bf16[4096,128]{1,0:T(8,128)(2,1)}, u32[]{:S(2)}) copy-start(bf16[4096,128]{1,0:T(8,128)(2,1)} %param.17) | copy-start | bytes 3145732
  (5 other events, 5.9 us)
Sparse Core Ops, SparseCore 0:
  10.9 197.4 all-gather.1

commit v2 on v1

--- a/solution.py
+++ b/solution.py
@@ -1,7 +1,11 @@
+import functools
+
 import jax
 import jax.numpy as jnp
 import numpy as np
 from jax import lax
+from jax.experimental import pallas as pl
+from jax.experimental.pallas import tpu as pltpu
 from jax.sharding import PartitionSpec as P
 
 F32 = jnp.float32
@@ -45,18 +49,197 @@
     return (a.astype(F32) * b.astype(F32)).astype(BF16)
 
 
-def scatter_sum(part, nseq, place):
-    chans, lags = part.shape
+def pick(data, width, side):
+    blocks = [data[:, i : i + width] for i in range(0, data.shape[1], width)]
+    return jnp.concatenate([jnp.where(side == 0, a, b) for a, b in zip(blocks[::2], blocks[1::2])], 1)
+
+
+def scatter_sum(part, nseq, place, order):
+    share = part.shape[1] // nseq
     bits = nseq.bit_length() - 1
     if nseq != 1 << bits:
-        return lax.psum_scatter(part, "seq", scatter_dimension=0, tiled=True)
-    for step in range(bits):
+        return lax.psum_scatter(part, "seq", scatter_dimension=1, tiled=True)
+    left = list(range(bits))
+    for step in [b for b in order if b < bits] + [b for b in range(bits) if b not in order]:
+        width = share << sum(b < step for b in left)
+        left.remove(step)
         mine = (place >> step) & 1
-        part = part.reshape(-1, 2, chans // nseq, lags)
-        away = lax.dynamic_index_in_dim(part, 1 - mine, 1, False)
-        kept = lax.dynamic_index_in_dim(part, mine, 1, False)
-        part = kept + lax.ppermute(away, "seq", [(i, i ^ (1 << step)) for i in range(nseq)])
-    return part.reshape(chans // nseq, lags)
+        away = pick(part, width, 1 - mine)
+        if step:
+            away = away.astype(BF16)
+        away = lax.ppermute(away, "seq", [(i, i ^ (1 << step)) for i in range(nseq)])
+        part = pick(part, width, mine) + away.astype(F32)
+    return part
+
+
+def links(seg_ids, place):
+    own = lax.dynamic_index_in_dim(seg_ids, place, 0, False)
+    prior = lax.dynamic_index_in_dim(seg_ids, jnp.maximum(place - 1, 0), 0, False)
+    return (place > 0) & (own == prior)
+
+
+def gathered_products(gated, cotangent, w_out):
+    weights = lax.all_gather(w_out, "seq", axis=0, tiled=True)
+    grad_gated = lax.dot_general(cotangent, weights, (((1,), (1,)), ((), ())), preferred_element_type=F32)
+    grad_gated = lax.psum_scatter(grad_gated, "tp", scatter_dimension=1, tiled=True).astype(BF16)
+    outputs = jnp.dot(
+        lax.all_gather(gated, "tp", axis=1, tiled=True), weights, preferred_element_type=F32
+    ).astype(BF16)
+    return grad_gated, outputs
+
+
+def ring_place(step, size):
+    half = (size + 1) // 2
+    return jnp.where(step < half, 2 * step, 2 * (size - 1 - step) + 1)
+
+
+def ring_step(row, size):
+    return jnp.where(row & 1 == 0, row >> 1, size - 1 - (row >> 1))
+
+
+def assemble_kernel(count, where_ref, *refs):
+    pieces, out_ref = refs[:-1], refs[-1]
+    width = out_ref.shape[0]
+    for i in range(count):
+        for half in range(2):
+            at = pl.ds(pl.multiple_of(where_ref[2 * i + half] * width, width), width)
+            out_ref[:, at] = pieces[i][:, half * width : (half + 1) * width]
+
+
+def assemble(where, pieces, chans):
+    rows = pieces[0].shape[0]
+    vmem = pl.BlockSpec(memory_space=pltpu.VMEM)
+    return pl.pallas_call(
+        functools.partial(assemble_kernel, len(pieces)),
+        out_shape=jax.ShapeDtypeStruct((rows, chans), pieces[0].dtype),
+        in_specs=[pl.BlockSpec(memory_space=pltpu.SMEM)] + [vmem] * len(pieces),
+        out_specs=vmem,
+        compiler_params=pltpu.CompilerParams(vmem_limit_bytes=16 << 20),
+        cost_estimate=pl.CostEstimate(flops=0, bytes_accessed=4 * rows * chans, transcendentals=0),
+    )(where, *pieces)
+
+
+def project_kernel(count, last, where_ref, gated_ref, *refs):
+    weights, refs = refs[: 2 * count], refs[2 * count :]
+    width = weights[0].shape[0]
+    total = None
+    for i in range(count):
+        left = jnp.concatenate(
+            [
+                gated_ref[:, pl.ds(pl.multiple_of(where_ref[2 * i + half] * width, width), width)]
+                for half in range(2)
+            ],
+            1,
+        )
+        right = jnp.concatenate([weights[2 * i][...], weights[2 * i + 1][...]], 0)
+        part = jnp.dot(left, right, preferred_element_type=F32)
+        total = part if total is None else total + part
+    if last:
+        before_ref, own_ref, away_ref = refs
+        total = total + before_ref[...]
+        rows = own_ref.shape[0]
+        own_ref[...] = total[:rows]
+        away_ref[...] = total[rows:].astype(BF16)
+    else:
+        refs[0][...] = total
+
+
+def project(where, gated, weights, before=None):
+    tokens = gated.shape[0]
+    depth, feats = weights[0].shape
+    tile = min(512, feats)
+    last = before is not None
+    whole = pl.BlockSpec((tokens, tile), lambda j, where: (0, j))
+    block = pl.BlockSpec((tokens // 2, tile), lambda j, where: (0, j))
+    split = tuple(jax.ShapeDtypeStruct((tokens // 2, feats), kind) for kind in (F32, BF16))
+    return pl.pallas_call(
+        functools.partial(project_kernel, len(weights) // 2, last),
+        out_shape=split if last else jax.ShapeDtypeStruct((tokens, feats), F32),
+        grid_spec=pltpu.PrefetchScalarGridSpec(
+            num_scalar_prefetch=1,
+            grid=(feats // tile,),
+            in_specs=[pl.BlockSpec(gated.shape, lambda j, where: (0, 0))]
+            + [pl.BlockSpec((depth, tile), lambda j, where: (0, j))] * len(weights)
+            + [whole] * last,
+            out_specs=(block, block) if last else whole,
+        ),
+        compiler_params=pltpu.CompilerParams(vmem_limit_bytes=32 << 20),
+        cost_estimate=pl.CostEstimate(
+            flops=2 * tokens * depth * len(weights) * feats,
+            bytes_accessed=2 * depth * feats * len(weights) + 2 * gated.size + 4 * tokens * feats,
+            transcendentals=0,
+        ),
+    )(where, gated, *weights, *([before] if last else []))
+
+
+def ring_products(gated, cotangent, w_out, place, nseq):
+    rows, chans = gated.shape
+    feats = cotangent.shape[1]
+    size = nseq // 4
+    core, pair, row = place & 1, (place >> 1) & 1, place >> 2
+    at = ring_step(row, size)
+    swap_core = [(i, i ^ 1) for i in range(nseq)]
+    swap_pair = [(i, i ^ 2) for i in range(nseq)]
+    walk = list(range(0, size, 2)) + list(range(1, size, 2))[::-1]
+    ahead = [
+        (4 * walk[i] + k, 4 * walk[(i + 1) % size] + k) for i in range(size) for k in range(4)
+    ]
+    behind = [(b, a) for a, b in ahead]
+    send = functools.partial(lax.ppermute, axis_name="seq")
+
+    half = feats // 2
+    kept = pick(w_out, half, core)
+    swapped = send(pick(w_out, half, 1 - core), perm=swap_core)
+    first = jnp.where(core == 0, kept, swapped)
+    second = jnp.where(core == 0, swapped, kept)
+
+    cot_away = send(cotangent, perm=swap_pair)
+    width = chans // (2 * size)
+    gated_away = send(pick(gated, width, 1 - pair), perm=swap_pair)
+    gated_pair = jnp.concatenate([pick(gated, width, pair), gated_away], 0)
+    cot_pair = jnp.concatenate([cotangent, cot_away], 0)
+    cot_mine, cot_other = pick(cot_pair, half, core), pick(cot_pair, half, 1 - core)
+
+    dims = (((1,), (1,)), ((), ()))
+    dot = functools.partial(lax.dot_general, dimension_numbers=dims, preferred_element_type=F32)
+    mine, other, pieces, columns, places = [], [], [], [], []
+    early = max(size - 2, 1)
+    for step in range(size):
+        first_row = ring_place(lax.rem(at - step + size, size), size)
+        second_row = ring_place(lax.rem(at + step, size), size)
+        columns += [2 * first_row, 2 * second_row + 1]
+        for side in (pair, 1 - pair):
+            places += [4 * first_row + 2 * side, 4 * second_row + 2 * side + 1]
+    columns = jnp.stack(columns).astype(jnp.int32)
+    for step in range(size):
+        if step:
+            if step >= 2:
+                first, second, pieces[2 * step - 4 : 2 * step - 2] = lax.optimization_barrier(
+                    (first, second, pieces[2 * step - 4 : 2 * step - 2])
+                )
+            if step == size - 2:
+                first, second, gated_pair = lax.optimization_barrier((first, second, gated_pair))
+            if step == size - 1:
+                sums = [project(columns[: 2 * early], gated_pair, w[: 2 * early]) for w in (mine, other)]
+                first, second, sums = lax.optimization_barrier((first, second, sums))
+            first, second = send(first, perm=ahead), send(second, perm=behind)
+        first_other, second_other = send(first, perm=swap_core), send(second, perm=swap_core)
+        mine += [first, second]
+        other += [first_other, second_other]
+        first_grad = (dot(cot_mine, first) + dot(cot_other, first_other)).astype(BF16)
+        second_grad = (dot(cot_mine, second) + dot(cot_other, second_other)).astype(BF16)
+        grad = jnp.concatenate([first_grad, second_grad], 1)
+        pieces += [grad[:rows], send(grad[rows:], perm=swap_pair)]
+    grad_gated = assemble(jnp.stack(places).astype(jnp.int32), pieces, chans)
+
+    outs = []
+    for w, total in zip((mine, other), sums):
+        own, away = project(columns[2 * early :], gated_pair, w[2 * early :], total)
+        outs.append((own + send(away, perm=swap_pair).astype(F32)).astype(BF16))
+    outputs = jnp.concatenate(
+        [jnp.where(core == 0, outs[0], outs[1]), jnp.where(core == 0, outs[1], outs[0])], 1
+    )
+    return grad_gated, outputs
 
 
 def on_device(queries, keys, values, w_out, taps, seg_ids, cotangent):
@@ -68,12 +251,9 @@
     table, high, low = spectrum_table(length)
     table_now, high_now, low_now = table[:, length:], high[:, length:], low[:, length:]
     scale = 1.0 / length
-    weights = lax.all_gather(w_out, "seq", axis=0, tiled=True)
     later = [(i, i + 1) for i in range(nseq - 1)]
     earlier = [(i + 1, i) for i in range(nseq - 1)]
-    own = lax.dynamic_index_in_dim(seg_ids, place, 0, False)
-    prior = lax.dynamic_index_in_dim(seg_ids, jnp.maximum(place - 1, 0), 0, False)
-    linked = (place > 0) & (own == prior)
+    linked = links(seg_ids, place)
 
     product = mul(keys, values)
     before = lax.ppermute(product, "seq", later)
@@ -83,22 +263,18 @@
     filtered = inverse_dft(table_now, times(filt, data), scale).astype(BF16)
     gated = mul(queries, filtered)
 
-    grad_gated = lax.dot_general(cotangent, weights, (((1,), (1,)), ((), ())), preferred_element_type=F32)
-    grad_gated = lax.psum_scatter(grad_gated, "tp", scatter_dimension=1, tiled=True).astype(BF16)
+    if lax.axis_size("tp") == 1 and nseq % 4 == 0 and nseq > 4 and rows * nseq == chans:
+        grad_gated, outputs = ring_products(gated, cotangent, w_out, place, nseq)
+    else:
+        grad_gated, outputs = gathered_products(gated, cotangent, w_out)
     grad_queries = mul(grad_gated, filtered)
     grad_filtered = mul(grad_gated, queries)
     grads = forward_dft(high_now, low_now, grad_filtered, ((1,), (0,)))
     back = inverse_dft(table, times_conj(grads, filt), scale)
     across = jnp.where(linked, back[:length], 0.0).astype(BF16)
     ahead = lax.ppermute(across, "seq", earlier)
-    taps_part = lax.dot_general(
-        times_conj(grads, data), table_now, (((0,), (0,)), ((), ())),
-        precision=lax.Precision.HIGH, preferred_element_type=F32,
-    ) * scale
-    taps_grad = scatter_sum(taps_part, nseq, place)
-    outputs = jnp.dot(
-        lax.all_gather(gated, "tp", axis=1, tiled=True), weights, preferred_element_type=F32
-    ).astype(BF16)
+    taps_part = inverse_dft(table_now, times_conj(grads, data), scale)
+    taps_grad = scatter_sum(taps_part, nseq, place, (0, 2, 3, 4, 1)).T
     grad_product = (back[length:] + ahead.astype(F32)).astype(BF16)
     grad_keys = mul(grad_product, values)
     grad_values = mul(grad_product, keys)

time: 339 us -> 229 us (0.68)
  waiting for transfers between devices: 205 us -> 75.2 us
  starting transfers between devices: 36.4 us -> 71 us
  matrix products: 52.1 us -> 35.9 us
  Pallas kernels: 0 us -> 12.7 us
  between operations: 15.7 us -> 3.48 us
  local copies, waits for them, and re-layouts: 20.7 us -> 16.4 us
    all_gather x1 -> x0, waiting for transfers between devices: 193 us -> none  [on_device(): weights = lax.all_gather(w_out, 'seq', axis=0, tiled=True)]
    ppermute x5 -> x48, waiting for transfers between devices: 11.8 us -> 75.1 us  [the longest x14 47.1 us: ring_products(): first, second = (send(first, perm=ahead), send(second, perm=behind))]
    ppermute x5 -> x48, starting transfers between devices: 21.5 us -> 66.2 us  [the longest x14 25.6 us: ring_products(): first, second = (send(first, perm=ahead), send(second, perm=behind))]
    dot_general x4 -> x32, matrix products: 32.3 us -> 14 us  [the longest x8 3.54 us: ring_products(): dot(cot_other, first_other)]
    pallas_call x0 -> x5, Pallas kernels: none -> 12.7 us  [the longest x4 11.9 us: project(): pl.pallas_call(functools.partial(project_kernel, len(weights) // 2, last)...]
    ppermute x1, starting transfers between devices: 13.5 us -> 3.34 us  [on_device(): before = lax.ppermute(product, 'seq', later)]
    unnamed x48 -> x44, local copies, waits for them, and re-layouts: 19.1 us -> 14.3 us
    select_n x0 -> x6, other arithmetic: none -> 4.05 us  [the longest x4 2.29 us: pick(): jnp.where(side == 0, a, b)]
  transfers between devices with their start and end apart: 8 -> 50, of which waited for: 5 -> 22; matrix products, arithmetic and copies ran while one was open for 12% -> 23% of each run, Pallas kernels for 0% -> 6%
where the time goes in v2:
time: 229 us; the launch traced here: 225 us
  waiting for transfers between devices  75.2 us (33%)
  starting transfers between devices  71 us (31%)
  matrix products  35.9 us (16%)
  local copies, waits for them, and re-layouts  16.4 us (7%)
  Pallas kernels  12.7 us (6%)
  other arithmetic  10.7 us (5%)
  between operations  3.48 us (2%)
    ppermute x14, waiting for transfers between devices, ring_products(): first, second = (send(first, perm=ahead), send(second, perm=behind))  47.1 us
    ppermute x14, starting transfers between devices, ring_products(): first, second = (send(first, perm=ahead), send(second, perm=behind))  25.6 us
    unnamed x44, local copies, waits for them, and re-layouts  14.3 us
    pallas_call x4, Pallas kernels, project(): pl.pallas_call(functools.partial(project_kernel, len(weights) // 2, last)...  11.9 us
    ppermute x5, starting transfers between devices, scatter_sum(): away = lax.ppermute(away, 'seq', [(i, i ^ 1 << step) for i in range(nseq)])  11.9 us
    ppermute x2, waiting for transfers between devices, ring_products(): outs.append((own + send(away, perm=swap_pair).astype(F32)).astype(BF16))  10.8 us
    ppermute x8, starting transfers between devices, ring_products(): send(first, perm=swap_core)  10.4 us
    ppermute x8, starting transfers between devices, ring_products(): pieces += [grad[:rows], send(grad[rows:], perm=swap_pair)]  10.2 us
  transfers between devices with their start and end apart: 50, of which 22 were waited for; matrix products, arithmetic and copies ran while one was open for 23% of the time, Pallas kernels for 6%

profile of v2, /device:TPU:0, one launch (start us, length us, event | category | flops | bytes accessed | tf_op | source)
XLA Modules:
  0.0 225.5 jit_solution(9801180512061142735)
XLA Ops:
  5.3 3.3 %collective-permute-start.27 = (bf16[128,4096]{0,1:T(8,128)(2,1)S(1)}, bf16[128,4096]{0,1:T(8,128)(2,1)}, u32[]{:S(2)}, u32[]{:S(2)}) collective-permute-start(bf16[128,4096]{0,1:T(8,128)(2,1)S(1)} %fusion.12), channel_id=1, source_target_pairs={{0,1},{1,2},{2,3},{3,4},{4,5},{5,6},{6,7},{7,8},{8,9},{9,10},{10,1... | collective-permute-start | bytes 3145736 | tf_op jit(solution)/shard_map/ppermute | solution.py:259
  13.6 2.7 %fusion.108 = f32[4096,256]{0,1:T(8,128)} fusion(bf16[128,4096]{0,1:T(8,128)(2,1)S(1)} %fusion.12, bf16[256,128]{1,0:T(8,128)(2,1)S(1)} %copy-done.10), kind=kOutput, calls=%fused_computation.245 | convolution fusion | flops 268435456 | bytes 5308416 | tf_op jit(solution)/shard_map/dot_general | solution.py:25
  16.3 2.8 %fusion.107 = f32[4096,256]{0,1:T(8,128)} fusion(bf16[128,4096]{0,1:T(8,128)(2,1)S(1)} %fusion.12, bf16[256,128]{1,0:T(8,128)(2,1)S(1)} %copy-done.11), kind=kOutput, calls=%fused_computation.244 | convolution fusion | flops 268435456 | bytes 5308416 | tf_op jit(solution)/shard_map/dot_general | solution.py:24
  19.8 2.7 %convolution_add_fusion.4 = f32[256,4096]{1,0:T(8,128)} fusion(f32[256,4096]{1,0:T(8,128)S(1)} %fusion.106, bf16[256,128]{1,0:T(8,128)(2,1)S(1)} %copy-done.10, bf16[4096,128]{1,0:T(8,128)(2,1)S(1)} %copy-done), kind=kOutput, calls=%fused_computation.9 | convolution fusion | flops 269484032 | bytes 9502720 | tf_op jit(solution)/shard_map/dot_general | solution.py:25
  29.5 5.3 %collective-permute-done.3 = bf16[128,4096]{1,0:T(8,128)(2,1)} collective-permute-done((bf16[128,4096]{1,0:T(8,128)(2,1)}, bf16[128,4096]{1,0:T(8,128)(2,1)}, u32[]{:S(2)}, u32[]{:S(2)}) %collective-permute-start.3) | collective-permute-done | bytes 1048608 | tf_op jit(solution)/shard_map/ppermute | solution.py:196
  49.5 10.3 %collective-permute-start.9 = (bf16[128,2048]{1,0:T(8,128)(2,1)S(1)}, bf16[128,2048]{1,0:T(8,128)(2,1)S(1)}, u32[]{:S(2)}, u32[]{:S(2)}) collective-permute-start(bf16[128,2048]{1,0:T(8,128)(2,1)S(1)} %collective-permute-done.1.refs_2_), channel_id=1, source_target_pairs={{0,1},{1,0},{2,3},{3,2},{4,5},{5,4},{6,7},{7,6},{8,9},{9,8},{10,11... | collective-permute-start | bytes 1572872 | tf_op jit(solution)/shard_map/ppermute | solution.py:226
  62.5 10.9 %collective-permute-start.8 = (bf16[128,2048]{1,0:T(8,128)(2,1)S(1)}, bf16[128,2048]{1,0:T(8,128)(2,1)S(1)}, u32[]{:S(2)}, u32[]{:S(2)}) collective-permute-start(bf16[128,2048]{1,0:T(8,128)(2,1)S(1)} %collective-permute-done.2.refs_3_), channel_id=1, source_target_pairs={{8,0},{9,1},{10,2},{11,3},{16,8},{17,9},{18,10},{19,11},{24,16},{2... | collective-permute-start | bytes 1572872 | tf_op jit(solution)/shard_map/ppermute | solution.py:225
  76.5 9.3 %collective-permute-done.8.refs_5_ = bf16[128,2048]{1,0:T(8,128)(2,1)S(1)} collective-permute-done((bf16[128,2048]{1,0:T(8,128)(2,1)S(1)}, bf16[128,2048]{1,0:T(8,128)(2,1)S(1)}, u32[]{:S(2)}, u32[]{:S(2)}) %collective-permute-start.8) | collective-permute-done | bytes 524320 | tf_op jit(solution)/shard_map/ppermute | solution.py:225
  92.0 7.0 %collective-permute-done.12.refs_6_ = bf16[128,2048]{1,0:T(8,128)(2,1)S(1)} collective-permute-done((bf16[128,2048]{1,0:T(8,128)(2,1)S(1)}, bf16[128,2048]{1,0:T(8,128)(2,1)S(1)}, u32[]{:S(2)}, u32[]{:S(2)}) %collective-permute-start.12) | collective-permute-done | bytes 524320 | tf_op jit(solution)/shard_map/ppermute | solution.py:225
  105.5 10.2 %collective-permute-done.17.refs_8_ = bf16[128,2048]{1,0:T(8,128)(2,1)S(1)} collective-permute-done((bf16[128,2048]{1,0:T(8,128)(2,1)S(1)}, bf16[128,2048]{1,0:T(8,128)(2,1)S(1)}, u32[]{:S(2)}, u32[]{:S(2)}) %collective-permute-start.17) | collective-permute-done | bytes 524320 | tf_op jit(solution)/shard_map/ppermute | solution.py:225
  123.3 6.9 %collective-permute-done.22.refs_10_ = bf16[128,2048]{1,0:T(8,128)(2,1)S(1)} collective-permute-done((bf16[128,2048]{1,0:T(8,128)(2,1)S(1)}, bf16[128,2048]{1,0:T(8,128)(2,1)S(1)}, u32[]{:S(2)}, u32[]{:S(2)}) %collective-permute-start.22) | collective-permute-done | bytes 524320 | tf_op jit(solution)/shard_map/ppermute | solution.py:225
  134.1 3.6 %shard_map.164.refs_4_ = f32[256,2048]{1,0:T(8,128)S(1)} custom-call(s32[12]{0:T(128)S(1)} %stack.169.where_ref, bf16[256,2048]{1,0:T(8,128)(2,1)S(1)} %pad_maximum_fusion.gated_ref, bf16[128,2048]{1,0:T(8,128)(2,1)S(1)} %get-tuple-element.119.refs_0_, bf16[128,2048]{1,0:T(8,128)(2,1)S(1)} %get-tuple-element.118.refs_1_, ...), custom_call_target="tpu_custom_call" | custom-call | flops 1610612736 | bytes 9437184 | tf_op jit(solution)/shard_map/pallas_call | solution.py:155
  139.7 3.6 %shard_map.165.refs_4_ = f32[256,2048]{1,0:T(8,128)S(1)} custom-call(s32[12]{0:T(128)S(1)} %stack.169.where_ref, bf16[256,2048]{1,0:T(8,128)(2,1)S(1)} %pad_maximum_fusion.gated_ref, bf16[128,2048]{1,0:T(8,128)(2,1)S(1)} %collective-permute-done.4.refs_0_, bf16[128,2048]{1,0:T(8,128)(2,1)S(1)} %collective-permute-done.5.refs_1_, ...), custom_call_target="tpu_custom_call" | custom-call | flops 1610612736 | bytes 9437184 | tf_op jit(solution)/shard_map/pallas_call | solution.py:155
  143.4 3.0 %collective-permute-done.29.refs_0_ = bf16[128,2048]{1,0:T(8,128)(2,1)S(1)} collective-permute-done((bf16[128,2048]{1,0:T(8,128)(2,1)S(1)}, bf16[128,2048]{1,0:T(8,128)(2,1)S(1)}, u32[]{:S(2)}, u32[]{:S(2)}) %collective-permute-start.29) | collective-permute-done | bytes 524320 | tf_op jit(solution)/shard_map/ppermute | solution.py:225
  153.3 6.6 %collective-permute-done.34.refs_2_ = bf16[128,2048]{1,0:T(8,128)(2,1)S(1)} collective-permute-done((bf16[128,2048]{1,0:T(8,128)(2,1)S(1)}, bf16[128,2048]{1,0:T(8,128)(2,1)S(1)}, u32[]{:S(2)}, u32[]{:S(2)}) %collective-permute-start.34) | collective-permute-done | bytes 524320 | tf_op jit(solution)/shard_map/ppermute | solution.py:225
  164.2 2.4 %shard_map.166 = (f32[128,2048]{1,0:T(8,128)S(1)}, bf16[128,2048]{1,0:T(8,128)(2,1)S(1)}) custom-call(s32[4]{0:T(128)S(1)} %pad_add_fusion.where_ref, bf16[256,2048]{1,0:T(8,128)(2,1)S(1)} %pad_maximum_fusion.gated_ref, bf16[128,2048]{1,0:T(8,128)(2,1)S(1)} %collective-permute-done.29.refs_0_, bf16[128,2048]{1,0:T(8,128)(2,1)S(1)} %collective-permute-done.30.refs_1_, ...), custom_call_target="tpu_custom_call" | custom-call | flops 536870912 | bytes 5242880 | tf_op jit(solution)/shard_map/pallas_call | solution.py:155
  178.4 2.3 %fusion.29 = f32[4096,256]{1,0:T(8,128)S(1)} fusion(f32[128,256]{1,0:T(8,128)S(1)} %copy-done.15, f32[256,4096]{1,0:T(8,128)S(1)} %fusion.2, f32[256,4096]{1,0:T(8,128)S(1)} %copy-done.2), kind=kOutput, calls=%fused_computation.44 | convolution fusion | flops 806879232 | bytes 12713984 | tf_op jit(solution)/shard_map/dot_general | solution.py:42
  180.7 2.3 %fusion.1 = f32[256,4096]{0,1:T(8,128)S(1)} fusion(f32[4096,256]{1,0:T(8,128)S(1)} %fusion.29, f32[128,256]{1,0:T(8,128)S(1)} %copy-done.14, f32[256,4096]{1,0:T(8,128)S(1)} %fusion.2, f32[256,4096]{1,0:T(8,128)S(1)} %copy-done.2), kind=kOutput, calls=%fused_computation.2 | convolution fusion | flops 808976384 | bytes 16908288 | tf_op jit(solution)/shard_map/dot_general | solution.py:42
  186.2 2.8 %collective-permute-start.46 = (bf16[128,1024]{1,0:T(8,128)(2,1)S(1)}, bf16[128,1024]{1,0:T(8,128)(2,1)S(1)}, u32[]{:S(2)}, u32[]{:S(2)}) collective-permute-start(bf16[128,1024]{1,0:T(8,128)(2,1)S(1)} %pad_maximum_fusion.2), channel_id=1, source_target_pairs={{0,4},{1,5},{2,6},{3,7},{4,0},{5,1},{6,2},{7,3},{8,12},{9,13},{10,... | collective-permute-start | bytes 786440 | tf_op jit(solution)/shard_map/ppermute | solution.py:70
  189.0 10.8 %collective-permute-done.41 = bf16[128,2048]{1,0:T(8,128)(2,1)S(1)} collective-permute-done((bf16[128,2048]{1,0:T(8,128)(2,1)S(1)}, bf16[128,2048]{1,0:T(8,128)(2,1)S(1)}, u32[]{:S(2)}, u32[]{:S(2)}) %collective-permute-start.41) | collective-permute-done | bytes 524320 | tf_op jit(solution)/shard_map/ppermute | solution.py:238
  202.3 3.8 %collective-permute-done.47 = bf16[128,512]{1,0:T(8,128)(2,1)S(1)} collective-permute-done((bf16[128,512]{1,0:T(8,128)(2,1)S(1)}, bf16[128,512]{1,0:T(8,128)(2,1)S(1)}, u32[]{:S(2)}, u32[]{:S(2)}) %collective-permute-start.47) | collective-permute-done | bytes 131104 | tf_op jit(solution)/shard_map/ppermute | solution.py:70
  207.2 4.8 %collective-permute-done.48 = bf16[128,256]{1,0:T(8,128)(2,1)S(1)} collective-permute-done((bf16[128,256]{1,0:T(8,128)(2,1)S(1)}, bf16[128,256]{1,0:T(8,128)(2,1)S(1)}, u32[]{:S(2)}, u32[]{:S(2)}) %collective-permute-start.48) | collective-permute-done | bytes 65568 | tf_op jit(solution)/shard_map/ppermute | solution.py:70
  212.1 7.0 %collective-permute-start.49 = (bf16[128,128]{1,0:T(8,128)(2,1)S(1)}, bf16[128,128]{1,0:T(8,128)(2,1)S(1)}, u32[]{:S(2)}, u32[]{:S(2)}) collective-permute-start(bf16[128,128]{1,0:T(8,128)(2,1)S(1)} %select_convert_fusion.7), channel_id=1, source_target_pairs={{0,2},{1,3},{2,0},{3,1},{4,6},{5,7},{6,4},{7,5},{8,10},{9,11},{10,... | collective-permute-start | bytes 98312 | tf_op jit(solution)/shard_map/ppermute | solution.py:70
  220.6 2.4 %copy.62 = bf16[128,4096]{1,0:T(8,128)(2,1)} copy(bf16[128,4096]{0,1:T(8,128)(2,1)} %get-tuple-element.81) | data formatting | bytes 2097152
  (231 shorter events, 95.0 us)
Async XLA Ops:
  5.3 36.2 %collective-permute-start.27 = (bf16[128,4096]{0,1:T(8,128)(2,1)S(1)}, bf16[128,4096]{0,1:T(8,128)(2,1)}, u32[]{:S(2)}, u32[]{:S(2)}) collective-permute-start(bf16[128,4096]{0,1:T(8,128)(2,1)S(1)} %fusion.12), channel_id=1, source_target_pairs={{0,1},{1,2},{2,3},{3,4},{4,5},{5,6},{6,7},{7,8},{8,9},{9,10},{10,1... | collective-permute-start | bytes 3145736 | tf_op jit(solution)/shard_map/ppermute | solution.py:259
  8.6 26.2 %collective-permute-start.3 = (bf16[128,4096]{1,0:T(8,128)(2,1)}, bf16[128,4096]{1,0:T(8,128)(2,1)}, u32[]{:S(2)}, u32[]{:S(2)}) collective-permute-start(bf16[128,4096]{1,0:T(8,128)(2,1)} %param.19), channel_id=1, source_target_pairs={{0,2},{1,3},{2,0},{3,1},{4,6},{5,7},{6,4},{7,5},{8,10},{9,11},{10,... | collective-permute-start | bytes 3145736 | tf_op jit(solution)/shard_map/ppermute | solution.py:196
  12.3 13.9 %collective-permute-start = (bf16[128,2048]{1,0:T(8,128)(2,1)}, bf16[128,2048]{1,0:T(8,128)(2,1)}, u32[]{:S(2)}, u32[]{:S(2)}) collective-permute-start(bf16[128,2048]{1,0:T(8,128)(2,1)} %broadcast_select_fusion.5), channel_id=1, source_target_pairs={{0,1},{1,0},{2,3},{3,2},{4,5},{5,4},{6,7},{7,6},{8,9},{9,8},{10,11... | collective-permute-start | bytes 1572872 | tf_op jit(solution)/shard_map/ppermute | solution.py:192
  27.7 21.8 %collective-permute-start.1 = (bf16[128,2048]{1,0:T(8,128)(2,1)S(1)}, bf16[128,2048]{1,0:T(8,128)(2,1)S(1)}, u32[]{:S(2)}, u32[]{:S(2)}) collective-permute-start(bf16[128,2048]{1,0:T(8,128)(2,1)S(1)} %get-tuple-element.119.refs_0_), channel_id=1, source_target_pairs={{0,8},{1,9},{2,10},{3,11},{8,16},{9,17},{10,18},{11,19},{16,24},{1... | collective-permute-start | bytes 1572872 | tf_op jit(solution)/shard_map/ppermute | solution.py:225
  34.8 25.5 %collective-permute-start.2 = (bf16[128,2048]{1,0:T(8,128)(2,1)S(1)}, bf16[128,2048]{1,0:T(8,128)(2,1)S(1)}, u32[]{:S(2)}, u32[]{:S(2)}) collective-permute-start(bf16[128,2048]{1,0:T(8,128)(2,1)S(1)} %get-tuple-element.118.refs_1_), channel_id=1, source_target_pairs={{8,0},{9,1},{10,2},{11,3},{16,8},{17,9},{18,10},{19,11},{24,16},{2... | collective-permute-start | bytes 1572872 | tf_op jit(solution)/shard_map/ppermute | solution.py:225
  39.4 21.5 %collective-permute-start.6 = (bf16[128,256]{1,0:T(8,128)(2,1)S(1)}, bf16[128,256]{1,0:T(8,128)(2,1)S(1)}, u32[]{:S(2)}, u32[]{:S(2)}) collective-permute-start(bf16[128,256]{1,0:T(8,128)(2,1)S(1)} %get-tuple-element.162), channel_id=1, source_target_pairs={{0,2},{1,3},{2,0},{3,1},{4,6},{5,7},{6,4},{7,5},{8,10},{9,11},{10,... | collective-permute-start | bytes 196616 | tf_op jit(solution)/shard_map/ppermute | solution.py:232
  49.5 23.9 %collective-permute-start.9 = (bf16[128,2048]{1,0:T(8,128)(2,1)S(1)}, bf16[128,2048]{1,0:T(8,128)(2,1)S(1)}, u32[]{:S(2)}, u32[]{:S(2)}) collective-permute-start(bf16[128,2048]{1,0:T(8,128)(2,1)S(1)} %collective-permute-done.1.refs_2_), channel_id=1, source_target_pairs={{0,1},{1,0},{2,3},{3,2},{4,5},{5,4},{6,7},{7,6},{8,9},{9,8},{10,11... | collective-permute-start | bytes 1572872 | tf_op jit(solution)/shard_map/ppermute | solution.py:226
  60.8 13.1 %collective-permute-start.10 = (bf16[128,2048]{1,0:T(8,128)(2,1)S(1)}, bf16[128,2048]{1,0:T(8,128)(2,1)S(1)}, u32[]{:S(2)}, u32[]{:S(2)}) collective-permute-start(bf16[128,2048]{1,0:T(8,128)(2,1)S(1)} %collective-permute-done.2.refs_3_), channel_id=1, source_target_pairs={{0,1},{1,0},{2,3},{3,2},{4,5},{5,4},{6,7},{7,6},{8,9},{9,8},{10,11... | collective-permute-start | bytes 1572872 | tf_op jit(solution)/shard_map/ppermute | solution.py:226
  60.9 15.6 %collective-permute-start.7 = (bf16[128,2048]{1,0:T(8,128)(2,1)S(1)}, bf16[128,2048]{1,0:T(8,128)(2,1)S(1)}, u32[]{:S(2)}, u32[]{:S(2)}) collective-permute-start(bf16[128,2048]{1,0:T(8,128)(2,1)S(1)} %collective-permute-done.1.refs_2_), channel_id=1, source_target_pairs={{0,8},{1,9},{2,10},{3,11},{8,16},{9,17},{10,18},{11,19},{16,24},{1... | collective-permute-start | bytes 1572872 | tf_op jit(solution)/shard_map/ppermute | solution.py:225
  62.5 23.3 %collective-permute-start.8 = (bf16[128,2048]{1,0:T(8,128)(2,1)S(1)}, bf16[128,2048]{1,0:T(8,128)(2,1)S(1)}, u32[]{:S(2)}, u32[]{:S(2)}) collective-permute-start(bf16[128,2048]{1,0:T(8,128)(2,1)S(1)} %collective-permute-done.2.refs_3_), channel_id=1, source_target_pairs={{8,0},{9,1},{10,2},{11,3},{16,8},{17,9},{18,10},{19,11},{24,16},{2... | collective-permute-start | bytes 1572872 | tf_op jit(solution)/shard_map/ppermute | solution.py:225
  75.7 29.7 %collective-permute-start.28 = (bf16[128,2048]{1,0:T(8,128)(2,1)S(1)}, bf16[128,2048]{1,0:T(8,128)(2,1)S(1)}, u32[]{:S(2)}, u32[]{:S(2)}) collective-permute-start(bf16[128,2048]{1,0:T(8,128)(2,1)S(1)} %get-tuple-element.129), channel_id=1, source_target_pairs={{0,2},{1,3},{2,0},{3,1},{4,6},{5,7},{6,4},{7,5},{8,10},{9,11},{10,... | collective-permute-start | bytes 1572872 | tf_op jit(solution)/shard_map/ppermute | solution.py:198
  85.8 13.2 %collective-permute-start.12 = (bf16[128,2048]{1,0:T(8,128)(2,1)S(1)}, bf16[128,2048]{1,0:T(8,128)(2,1)S(1)}, u32[]{:S(2)}, u32[]{:S(2)}) collective-permute-start(bf16[128,2048]{1,0:T(8,128)(2,1)S(1)} %collective-permute-done.7.refs_4_), channel_id=1, source_target_pairs={{0,8},{1,9},{2,10},{3,11},{8,16},{9,17},{10,18},{11,19},{16,24},{1... | collective-permute-start | bytes 1572872 | tf_op jit(solution)/shard_map/ppermute | solution.py:225
  101.3 14.4 %collective-permute-start.17 = (bf16[128,2048]{1,0:T(8,128)(2,1)S(1)}, bf16[128,2048]{1,0:T(8,128)(2,1)S(1)}, u32[]{:S(2)}, u32[]{:S(2)}) collective-permute-start(bf16[128,2048]{1,0:T(8,128)(2,1)S(1)} %collective-permute-done.12.refs_6_), channel_id=1, source_target_pairs={{0,8},{1,9},{2,10},{3,11},{8,16},{9,17},{10,18},{11,19},{16,24},{1... | collective-permute-start | bytes 1572872 | tf_op jit(solution)/shard_map/ppermute | solution.py:225
  102.8 14.1 %collective-permute-start.18 = (bf16[128,2048]{1,0:T(8,128)(2,1)S(1)}, bf16[128,2048]{1,0:T(8,128)(2,1)S(1)}, u32[]{:S(2)}, u32[]{:S(2)}) collective-permute-start(bf16[128,2048]{1,0:T(8,128)(2,1)S(1)} %collective-permute-done.13.refs_7_), channel_id=1, source_target_pairs={{8,0},{9,1},{10,2},{11,3},{16,8},{17,9},{18,10},{19,11},{24,16},{2... | collective-permute-start | bytes 1572872 | tf_op jit(solution)/shard_map/ppermute | solution.py:225
  116.9 13.2 %collective-permute-start.22 = (bf16[128,2048]{1,0:T(8,128)(2,1)S(1)}, bf16[128,2048]{1,0:T(8,128)(2,1)S(1)}, u32[]{:S(2)}, u32[]{:S(2)}) collective-permute-start(bf16[128,2048]{1,0:T(8,128)(2,1)S(1)} %collective-permute-done.17.refs_8_), channel_id=1, source_target_pairs={{0,8},{1,9},{2,10},{3,11},{8,16},{9,17},{10,18},{11,19},{16,24},{1... | collective-permute-start | bytes 1572872 | tf_op jit(solution)/shard_map/ppermute | solution.py:225
  118.6 13.0 %collective-permute-start.23 = (bf16[128,2048]{1,0:T(8,128)(2,1)S(1)}, bf16[128,2048]{1,0:T(8,128)(2,1)S(1)}, u32[]{:S(2)}, u32[]{:S(2)}) collective-permute-start(bf16[128,2048]{1,0:T(8,128)(2,1)S(1)} %collective-permute-done.18.refs_9_), channel_id=1, source_target_pairs={{8,0},{9,1},{10,2},{11,3},{16,8},{17,9},{18,10},{19,11},{24,16},{2... | collective-permute-start | bytes 1572872 | tf_op jit(solution)/shard_map/ppermute | solution.py:225
  132.0 14.4 %collective-permute-start.29 = (bf16[128,2048]{1,0:T(8,128)(2,1)S(1)}, bf16[128,2048]{1,0:T(8,128)(2,1)S(1)}, u32[]{:S(2)}, u32[]{:S(2)}) collective-permute-start(bf16[128,2048]{1,0:T(8,128)(2,1)S(1)} %collective-permute-done.22.refs_10_), channel_id=1, source_target_pairs={{0,8},{1,9},{2,10},{3,11},{8,16},{9,17},{10,18},{11,19},{16,24},{1... | collective-permute-start | bytes 1572872 | tf_op jit(solution)/shard_map/ppermute | solution.py:225
  133.4 13.6 %collective-permute-start.30 = (bf16[128,2048]{1,0:T(8,128)(2,1)S(1)}, bf16[128,2048]{1,0:T(8,128)(2,1)S(1)}, u32[]{:S(2)}, u32[]{:S(2)}) collective-permute-start(bf16[128,2048]{1,0:T(8,128)(2,1)S(1)} %collective-permute-done.23.refs_11_), channel_id=1, source_target_pairs={{8,0},{9,1},{10,2},{11,3},{16,8},{17,9},{18,10},{19,11},{24,16},{2... | collective-permute-start | bytes 1572872 | tf_op jit(solution)/shard_map/ppermute | solution.py:225
  146.9 13.0 %collective-permute-start.34 = (bf16[128,2048]{1,0:T(8,128)(2,1)S(1)}, bf16[128,2048]{1,0:T(8,128)(2,1)S(1)}, u32[]{:S(2)}, u32[]{:S(2)}) collective-permute-start(bf16[128,2048]{1,0:T(8,128)(2,1)S(1)} %collective-permute-done.29.refs_0_), channel_id=1, source_target_pairs={{0,8},{1,9},{2,10},{3,11},{8,16},{9,17},{10,18},{11,19},{16,24},{1... | collective-permute-start | bytes 1572872 | tf_op jit(solution)/shard_map/ppermute | solution.py:225
  152.1 18.9 %collective-permute-start.42 = (bf16[128,256]{1,0:T(8,128)(2,1)S(1)}, bf16[128,256]{1,0:T(8,128)(2,1)S(1)}, u32[]{:S(2)}, u32[]{:S(2)}) collective-permute-start(bf16[128,256]{1,0:T(8,128)(2,1)S(1)} %get-tuple-element.150), channel_id=1, source_target_pairs={{0,2},{1,3},{2,0},{3,1},{4,6},{5,7},{6,4},{7,5},{8,10},{9,11},{10,... | collective-permute-start | bytes 196616 | tf_op jit(solution)/shard_map/ppermute | solution.py:232
  166.6 22.4 %collective-permute-start.36 = (bf16[128,2048]{1,0:T(8,128)(2,1)S(1)}, bf16[128,2048]{1,0:T(8,128)(2,1)S(1)}, u32[]{:S(2)}, u32[]{:S(2)}) collective-permute-start(bf16[128,2048]{1,0:T(8,128)(2,1)S(1)} %get-tuple-element.59), channel_id=1, source_target_pairs={{0,2},{1,3},{2,0},{3,1},{4,6},{5,7},{6,4},{7,5},{8,10},{9,11},{10,... | collective-permute-start | bytes 1572872 | tf_op jit(solution)/shard_map/ppermute | solution.py:238
  169.9 29.9 %collective-permute-start.41 = (bf16[128,2048]{1,0:T(8,128)(2,1)S(1)}, bf16[128,2048]{1,0:T(8,128)(2,1)S(1)}, u32[]{:S(2)}, u32[]{:S(2)}) collective-permute-start(bf16[128,2048]{1,0:T(8,128)(2,1)S(1)} %get-tuple-element.62), channel_id=1, source_target_pairs={{0,2},{1,3},{2,0},{3,1},{4,6},{5,7},{6,4},{7,5},{8,10},{9,11},{10,... | collective-permute-start | bytes 1572872 | tf_op jit(solution)/shard_map/ppermute | solution.py:238
  183.2 35.9 %collective-permute-start.44 = (bf16[128,4096]{0,1:T(8,128)(2,1)S(1)}, bf16[128,4096]{0,1:T(8,128)(2,1)S(1)}, u32[]{:S(2)}, u32[]{:S(2)}) collective-permute-start(bf16[128,4096]{0,1:T(8,128)(2,1)S(1)} %fusion.17), channel_id=1, source_target_pairs={{1,0},{2,1},{3,2},{4,3},{5,4},{6,5},{7,6},{8,7},{9,8},{10,9},{11,1... | collective-permute-start | bytes 3145736 | tf_op jit(solution)/shard_map/ppermute | solution.py:275
  186.2 14.0 %collective-permute-start.46 = (bf16[128,1024]{1,0:T(8,128)(2,1)S(1)}, bf16[128,1024]{1,0:T(8,128)(2,1)S(1)}, u32[]{:S(2)}, u32[]{:S(2)}) collective-permute-start(bf16[128,1024]{1,0:T(8,128)(2,1)S(1)} %pad_maximum_fusion.2), channel_id=1, source_target_pairs={{0,4},{1,5},{2,6},{3,7},{4,0},{5,1},{6,2},{7,3},{8,12},{9,13},{10,... | collective-permute-start | bytes 786440 | tf_op jit(solution)/shard_map/ppermute | solution.py:70
  (45 other events, 260.0 us)

commit v3 on v1

v3 whole, which is shorter than its diff:
```python
import functools

import jax
import jax.numpy as jnp
import numpy as np
from jax import lax
from jax.experimental import pallas as pl
from jax.experimental.pallas import tpu as pltpu
from jax.sharding import PartitionSpec as P

F32 = jnp.float32
BF16 = jnp.bfloat16


def spectrum_table(length):
    angles = np.pi * (2 * np.arange(length)[:, None] + 1) * np.arange(-length, length)[None, :] / (2 * length)
    table = np.concatenate([np.cos(angles), -np.sin(angles)], 0).astype(np.float32)
    high = table.astype(BF16)
    low = (table - high.astype(np.float32)).astype(BF16)
    return table, high, low


def forward_dft(high, low, data, dims):
    first = lax.dot_general(high, data, (dims, ((), ())), preferred_element_type=F32)
    second = lax.dot_general(low, data, (dims, ((), ())), preferred_element_type=F32)
    return first + second


def times(a, b):
    half = a.shape[0] // 2
    ar, ai, br, bi = a[:half], a[half:], b[:half], b[half:]
    return jnp.concatenate([ar * br - ai * bi, ar * bi + ai * br], 0)


def times_conj(a, b):
    half = a.shape[0] // 2
    ar, ai, br, bi = a[:half], a[half:], b[:half], b[half:]
    return jnp.concatenate([ar * br + ai * bi, ai * br - ar * bi], 0)


def inverse_dft(table, spectrum, scale):
    done = lax.dot_general(
        table, spectrum, (((0,), (0,)), ((), ())), precision=lax.Precision.HIGH, preferred_element_type=F32
    )
    return done * scale


def mul(a, b):
    return (a.astype(F32) * b.astype(F32)).astype(BF16)


def pick(data, width, side):
    blocks = [data[:, i : i + width] for i in range(0, data.shape[1], width)]
    return jnp.concatenate([jnp.where(side == 0, a, b) for a, b in zip(blocks[::2], blocks[1::2])], 1)


def scatter_sum(part, nseq, place, order):
    share = part.shape[1] // nseq
    bits = nseq.bit_length() - 1
    if nseq != 1 << bits:
        return lax.psum_scatter(part, "seq", scatter_dimension=1, tiled=True)
    left = list(range(bits))
    for step in [b for b in order if b < bits] + [b for b in range(bits) if b not in order]:
        width = share << sum(b < step for b in left)
        left.remove(step)
        mine = (place >> step) & 1
        away = pick(part, width, 1 - mine)
        if step:
            away = away.astype(BF16)
        away = lax.ppermute(away, "seq", [(i, i ^ (1 << step)) for i in range(nseq)])
        part = pick(part, width, mine) + away.astype(F32)
    return part


def links(seg_ids, place):
    own = lax.dynamic_index_in_dim(seg_ids, place, 0, False)
    prior = lax.dynamic_index_in_dim(seg_ids, jnp.maximum(place - 1, 0), 0, False)
    return (place > 0) & (own == prior)


def gathered_products(gated, cotangent, w_out):
    weights = lax.all_gather(w_out, "seq", axis=0, tiled=True)
    grad_gated = lax.dot_general(cotangent, weights, (((1,), (1,)), ((), ())), preferred_element_type=F32)
    grad_gated = lax.psum_scatter(grad_gated, "tp", scatter_dimension=1, tiled=True).astype(BF16)
    outputs = jnp.dot(
        lax.all_gather(gated, "tp", axis=1, tiled=True), weights, preferred_element_type=F32
    ).astype(BF16)
    return grad_gated, outputs


def ring_place(step, size):
    half = (size + 1) // 2
    return jnp.where(step < half, 2 * step, 2 * (size - 1 - step) + 1)


def ring_step(row, size):
    return jnp.where(row & 1 == 0, row >> 1, size - 1 - (row >> 1))


def split(data):
    high = data.astype(BF16)
    return high, (data - high.astype(F32)).astype(BF16)


def dot(a, b):
    return jnp.dot(a, b, preferred_element_type=F32)


def dot_three(high, low, data):
    data_high, data_low = split(data)
    return dot(high, data_high) + (dot(high, data_low) + dot(low, data_high))


def forward_kernel(linked_ref, fwd_hi, fwd_lo, inv_hi, inv_lo, before, product, taps, queries, *outs):
    data_ref, filt_ref, filtered_ref, gated_ref = outs
    length = product.shape[0]
    past = jnp.where(linked_ref[0] == 1, before[...].astype(F32), 0.0).astype(BF16)
    window = jnp.concatenate([past, product[...]], 0)
    data = dot(fwd_hi[...], window) + dot(fwd_lo[...], window)
    dims = (((1,), (1,)), ((), ()))
    filt = lax.dot_general(fwd_hi[:, length:], taps[...], dims, preferred_element_type=F32)
    filt = filt + lax.dot_general(fwd_lo[:, length:], taps[...], dims, preferred_element_type=F32)
    data_ref[...] = data
    filt_ref[...] = filt
    filtered = dot_three(inv_hi[length:], inv_lo[length:], times(filt, data)) * (1.0 / length)
    filtered = filtered.astype(BF16)
    filtered_ref[...] = filtered
    gated_ref[...] = mul(queries[...], filtered)


def tables(length):
    table, high, low = spectrum_table(length)
    return tuple(jnp.asarray(t) for t in (high, low, high.T, low.T))


def forward_filter(linked, before, product, taps, queries):
    length, chans = product.shape
    width = min(512, chans)
    fixed = pl.BlockSpec((2 * length, 2 * length), lambda j: (0, 0))
    block = pl.BlockSpec((length, width), lambda j: (0, j))
    spectrum = pl.BlockSpec((2 * length, width), lambda j: (0, j))
    wide = jax.ShapeDtypeStruct((2 * length, chans), F32)
    narrow = jax.ShapeDtypeStruct((length, chans), BF16)
    return pl.pallas_call(
        forward_kernel,
        out_shape=(wide, wide, narrow, narrow),
        grid=(chans // width,),
        in_specs=[pl.BlockSpec(memory_space=pltpu.SMEM)]
        + [fixed] * 4
        + [block, block, pl.BlockSpec((width, length), lambda j: (j, 0)), block],
        out_specs=(spectrum, spectrum, block, block),
        compiler_params=pltpu.CompilerParams(vmem_limit_bytes=32 << 20),
        cost_estimate=pl.CostEstimate(
            flops=24 * length * length * chans, bytes_accessed=28 * length * chans, transcendentals=0
        ),
    )(linked.astype(jnp.int32).reshape(1), *tables(length), before, product, taps, queries)


def grad_kernel(scalars, cot, first, first_other, second, second_other, own_ref, away_ref, total):
    @pl.when(pl.program_id(0) == 0)
    def _():
        total[...] = jnp.zeros_like(total)

    def add(refs):
        rows = jnp.concatenate([ref[...] for ref in refs], 0)
        dims = (((1,), (1,)), ((), ()))
        total[...] += lax.dot_general(cot[...], rows, dims, preferred_element_type=F32)

    @pl.when(scalars[0] == 0)
    def _():
        add((first, first_other, second, second_other))

    @pl.when(scalars[0] != 0)
    def _():
        add((first_other, first, second_other, second))

    @pl.when(pl.program_id(0) == pl.num_programs(0) - 1)
    def _():
        rows = own_ref.shape[0]
        own_ref[...] = total[:rows].astype(BF16)
        away_ref[...] = total[rows:].astype(BF16)


def grad_product(core, cot, weights):
    tokens, feats = cot.shape
    depth = weights[0].shape[0]
    tile = min(1024, feats)
    out = jax.ShapeDtypeStruct((tokens // 2, 4 * depth), BF16)
    whole = pl.BlockSpec(out.shape, lambda j, core: (0, 0))
    return pl.pallas_call(
        grad_kernel,
        out_shape=(out, out),
        grid_spec=pltpu.PrefetchScalarGridSpec(
            num_scalar_prefetch=1,
            grid=(feats // tile,),
            in_specs=[pl.BlockSpec((tokens, tile), lambda j, core: (0, j))]
            + [pl.BlockSpec((depth, tile), lambda j, core: (0, j))] * 4,
            out_specs=(whole, whole),
            scratch_shapes=[pltpu.VMEM((tokens, 4 * depth), F32)],
        ),
        compiler_params=pltpu.CompilerParams(vmem_limit_bytes=16 << 20),
        cost_estimate=pl.CostEstimate(
            flops=8 * tokens * depth * feats, bytes_accessed=(2 * tokens + 8 * depth) * feats, transcendentals=0
        ),
    )(core, cot, *weights)


def project_kernel(count, first, last, scalars, gated_ref, *refs):
    weights, refs = refs[: 4 * count], refs[4 * count :]
    width = 4 * weights[0].shape[0]
    total = refs[-1]
    total[...] = jnp.zeros_like(total) if first else refs[0][...]

    def add(order):
        for i in range(count):
            left = gated_ref[:, pl.ds(pl.multiple_of(scalars[1 + i] * width, width), width)]
            right = jnp.concatenate([weights[4 * i + k][...] for k in order], 0)
            total[...] += dot(left, right)

    @pl.when(scalars[0] == 0)
    def _():
        add((0, 1, 2, 3))

    @pl.when(scalars[0] != 0)
    def _():
        add((2, 3, 0, 1))

    if last:
        own_ref, away_ref = refs[-3:-1]
        rows = own_ref.shape[0]
        own_ref[...] = total[:rows]
        away_ref[...] = total[rows:].astype(BF16)
    else:
        refs[-2][...] = total[...]


def project(scalars, gated, groups, before=None, last=False):
    tokens = gated.shape[0]
    depth, feats = groups[0][0].shape
    tile = min(512, feats)
    weights = [w for group in groups for w in group]
    whole = pl.BlockSpec((tokens, tile), lambda j, s: (0, j))
    block = pl.BlockSpec((tokens // 2, tile), lambda j, s: (0, j))
    halves = tuple(jax.ShapeDtypeStruct((tokens // 2, feats), kind) for kind in (F32, BF16))
    return pl.pallas_call(
        functools.partial(project_kernel, len(groups), before is None, last),
        out_shape=halves if last else jax.ShapeDtypeStruct((tokens, feats), F32),
        grid_spec=pltpu.PrefetchScalarGridSpec(
            num_scalar_prefetch=1,
            grid=(feats // tile,),
            in_specs=[pl.BlockSpec(gated.shape, lambda j, s: (0, 0))]
            + [pl.BlockSpec((depth, tile), lambda j, s: (0, j))] * len(weights)
            + [whole] * (before is not None),
            out_specs=(block, block) if last else whole,
            scratch_shapes=[pltpu.VMEM((tokens, tile), F32)],
        ),
        compiler_params=pltpu.CompilerParams(vmem_limit_bytes=32 << 20),
        cost_estimate=pl.CostEstimate(
            flops=2 * tokens * depth * len(weights) * feats,
            bytes_accessed=2 * depth * feats * len(weights) + 2 * gated.size + 4 * tokens * feats,
            transcendentals=0,
        ),
    )(scalars, gated, *weights, *([] if before is None else [before]))


def backward_kernel(count, scalars, fwd_hi, fwd_lo, inv_hi, inv_lo, queries, filtered, data, filt, *refs):
    grads, refs = refs[: 4 * count], refs[-5:]
    grad_queries_ref, near_ref, across_ref, taps_ref, grad = refs
    length = queries.shape[0]
    depth = length // 2

    def side(first, second):
        return [ref[:, k * depth : (k + 1) * depth] for k in (0, 1) for ref in (first[:, : 2 * depth], second[:, 2 * depth :])]

    for i in range(count):
        own, away = [side(grads[4 * i + k], grads[4 * i + k + 2]) for k in (0, 1)]

        @pl.when((pl.program_id(0) == i) & (scalars[0] == 0))
        def _(own=own, away=away):
            grad[...] = jnp.concatenate(own + away, 1)

        @pl.when((pl.program_id(0) == i) & (scalars[0] != 0))
        def _(own=own, away=away):
            grad[...] = jnp.concatenate(away + own, 1)

    grad_gated = grad[...]
    grad_queries_ref[...] = mul(grad_gated, filtered[...])
    grad_filtered = mul(grad_gated, queries[...])
    grads = dot(fwd_hi[:, length:], grad_filtered) + dot(fwd_lo[:, length:], grad_filtered)
    back = dot_three(inv_hi[...], inv_lo[...], times_conj(grads, filt[...])) * (1.0 / length)
    across_ref[...] = jnp.where(scalars[1] == 1, back[:length], 0.0).astype(BF16)
    near_ref[...] = back[length:]
    taps_ref[...] = dot_three(inv_hi[length:], inv_lo[length:], times_conj(grads, data[...])) * (1.0 / length)


def backward_filter(scalars, groups, queries, filtered, data, filt, before=None):
    length, chans = queries.shape
    width = 4 * length
    count = len(groups)
    pieces = [p for group in groups for p in group]
    fixed = pl.BlockSpec((2 * length, 2 * length), lambda j, s: (0, 0))
    block = pl.BlockSpec((length, width), lambda j, s: (0, s[2 + j]))
    spectrum = pl.BlockSpec((2 * length, width), lambda j, s: (0, s[2 + j]))
    piece = pl.BlockSpec((length, 2 * length), lambda j, s: (0, 0))
    before = [] if before is None else list(before)
    inputs = 9 + len(pieces)
    return pl.pallas_call(
        functools.partial(backward_kernel, count),
        out_shape=tuple(jax.ShapeDtypeStruct((length, chans), kind) for kind in (BF16, F32, BF16, F32)),
        grid_spec=pltpu.PrefetchScalarGridSpec(
            num_scalar_prefetch=1,
            grid=(count,),
            in_specs=[fixed] * 4
            + [block, block, spectrum, spectrum]
            + [piece] * len(pieces)
            + [pl.BlockSpec(memory_space=pl.ANY)] * len(before),
            out_specs=(block,) * 4,
            scratch_shapes=[pltpu.VMEM((length, width), BF16)],
        ),
        input_output_aliases={inputs + i: i for i in range(len(before))},
        compiler_params=pltpu.CompilerParams(vmem_limit_bytes=32 << 20),
        cost_estimate=pl.CostEstimate(
            flops=28 * length * length * width * count, bytes_accessed=34 * length * width * count, transcendentals=0
        ),
    )(scalars, *tables(length), queries, filtered, data, filt, *pieces, *before)


def on_ring(queries, keys, values, w_out, taps, seg_ids, cotangent):
    rows, chans = queries.shape
    nseq = lax.axis_size("seq")
    place = lax.axis_index("seq")
    size = nseq // 4
    core, pair, row = place & 1, (place >> 1) & 1, place >> 2
    at = ring_step(row, size)
    swap_core = [(i, i ^ 1) for i in range(nseq)]
    swap_pair = [(i, i ^ 2) for i in range(nseq)]
    walk = list(range(0, size, 2)) + list(range(1, size, 2))[::-1]
    onward = [(4 * walk[i] + k, 4 * walk[(i + 1) % size] + k) for i in range(size) for k in range(4)]
    backward = [(b, a) for a, b in onward]
    later = [(i, i + 1) for i in range(nseq - 1)]
    earlier = [(i + 1, i) for i in range(nseq - 1)]
    send = functools.partial(lax.ppermute, axis_name="seq")
    linked = links(seg_ids, place)

    first, second = w_out[: rows // 2], w_out[rows // 2 :]
    cot_pair = jnp.concatenate([cotangent, send(cotangent, perm=swap_pair)], 0)
    product = mul(keys, values)
    before = send(product, perm=later)
    data, filt, filtered, gated = forward_filter(linked, before, product, taps, queries)
    width = 2 * rows
    gated_away = send(pick(gated, width, 1 - pair), perm=swap_pair)
    gated_pair = jnp.concatenate([pick(gated, width, pair), gated_away], 0)

    ready = [max(s, size - s) if s else 0 for s in range(size)]
    groups_at = {t: [s for s in range(size) if ready[s] == t] for t in range(size)}
    early = max(size - 3, 0)
    stages = {early: [s for s in range(size) if ready[s] <= early]}
    for t in range(early + 1, size):
        stages[t] = groups_at[t]
    block = [ring_place(lax.rem(at - s + size, size), size).astype(jnp.int32) for s in range(size)]
    core = core.astype(jnp.int32)
    core_only = core.reshape(1)
    firsts, seconds, own, away = [], [], [], []
    sums = back = None
    for step in range(size):
        if step:
            if step >= 2:
                first, second, own[step - 2], away[step - 2] = lax.optimization_barrier(
                    (first, second, own[step - 2], away[step - 2])
                )
            if step == 2:
                first, second, gated = lax.optimization_barrier((first, second, gated))
            if step - 2 in stages and step - 2 < size - 1:
                first, second, sums, back = lax.optimization_barrier((first, second, sums, back))
            first, second = send(first, perm=onward), send(second, perm=backward)
        firsts.append((first, send(first, perm=swap_core)))
        seconds.append((second, send(second, perm=swap_core)))
        mine, theirs = grad_product(core_only, cot_pair, firsts[step] + seconds[step])
        own.append(mine)
        away.append(send(theirs, perm=swap_pair))
        if step in stages and stages[step]:
            sets = stages[step]
            blocks = [block[s] for s in sets]
            mirror = [(size - s) % size for s in sets]
            groups = [
                (firsts[s][0], seconds[m][0], firsts[s][1], seconds[m][1]) for s, m in zip(sets, mirror)
            ]
            sums = project(
                jnp.stack([core] + blocks), gated_pair, groups, sums, step == size - 1
            )
            groups = [(own[s], away[s], own[m], away[m]) for s, m in zip(sets, mirror)]
            scalars = jnp.stack([pair.astype(jnp.int32), linked.astype(jnp.int32)] + blocks)
            back = backward_filter(scalars, groups, queries, filtered, data, filt, back)
    grad_queries, near, across, taps_part = back
    ahead = send(across, perm=earlier)
    taps_grad = scatter_sum(taps_part, nseq, place, (0, 2, 3, 4, 1)).T
    out_own, out_away = sums
    outputs = (out_own + send(out_away, perm=swap_pair).astype(F32)).astype(BF16)
    grad_product_ = (near + ahead.astype(F32)).astype(BF16)
    grad_keys = mul(grad_product_, values)
    grad_values = mul(grad_product_, keys)
    return (outputs, grad_queries, grad_keys, grad_values, taps_grad)


def on_device(queries, keys, values, w_out, taps, seg_ids, cotangent):
    rows, chans = queries.shape
    length = taps.shape[1]
    assert rows == length
    nseq = lax.axis_size("seq")
    place = lax.axis_index("seq")
    table, high, low = spectrum_table(length)
    table_now, high_now, low_now = table[:, length:], high[:, length:], low[:, length:]
    scale = 1.0 / length
    later = [(i, i + 1) for i in range(nseq - 1)]
    earlier = [(i + 1, i) for i in range(nseq - 1)]
    linked = links(seg_ids, place)

    product = mul(keys, values)
    before = lax.ppermute(product, "seq", later)
    before = jnp.where(linked, before, jnp.zeros_like(before))
    data = forward_dft(high, low, jnp.concatenate([before, product], 0), ((1,), (0,)))
    filt = forward_dft(high_now, low_now, taps, ((1,), (1,)))
    filtered = inverse_dft(table_now, times(filt, data), scale).astype(BF16)
    gated = mul(queries, filtered)

    grad_gated, outputs = gathered_products(gated, cotangent, w_out)
    grad_queries = mul(grad_gated, filtered)
    grad_filtered = mul(grad_gated, queries)
    grads = forward_dft(high_now, low_now, grad_filtered, ((1,), (0,)))
    back = inverse_dft(table, times_conj(grads, filt), scale)
    across = jnp.where(linked, back[:length], 0.0).astype(BF16)
    ahead = lax.ppermute(across, "seq", earlier)
    taps_part = inverse_dft(table_now, times_conj(grads, data), scale)
    taps_grad = scatter_sum(taps_part, nseq, place, (0, 2, 3, 4, 1)).T
    grad_product = (back[length:] + ahead.astype(F32)).astype(BF16)
    grad_keys = mul(grad_product, values)
    grad_values = mul(grad_product, keys)
    return (outputs, grad_queries, grad_keys, grad_values, taps_grad)


def solution(mesh):
    block = P("seq", "tp")
    ring = mesh.shape["tp"] == 1 and mesh.shape["seq"] % 4 == 0 and mesh.shape["seq"] > 4

    def run(queries, keys, values, w_out, taps, seg_ids, cotangent):
        rows, chans = queries.shape
        place = on_ring if ring and rows * lax.axis_size("seq") == chans else on_device
        return place(queries, keys, values, w_out, taps, seg_ids, cotangent)

    return jax.shard_map(
        run,
        mesh=mesh,
        in_specs=(block, block, block, block, P("tp", None), P(), block),
        out_specs=(block, block, block, block, P(("tp", "seq"), None)),
        check_vma=False,
    )
```

time: 339 us -> 307 us (0.906)
  waiting for transfers between devices: 205 us -> 112 us
  Pallas kernels: 0 us -> 69.9 us
  matrix products: 52.1 us -> 0 us
  starting transfers between devices: 36.4 us -> 55.6 us
  other arithmetic: 8.25 us -> 26.3 us
  local copies, waits for them, and re-layouts: 20.7 us -> 37.9 us
  between operations: 15.7 us -> 3 us
    all_gather x1 -> x0, waiting for transfers between devices: 193 us -> none  [on_device(): weights = lax.all_gather(w_out, 'seq', axis=0, tiled=True)]
    ppermute x7 -> x48, waiting for transfers between devices: 11.8 us -> 112 us  [the longest x14 53.4 us: on_ring(): first, second = (send(first, perm=onward), send(second, perm=backward))]
    pallas_call x0 -> x15, Pallas kernels: none -> 69.9 us  [the longest x8 26 us: grad_product(): pl.pallas_call(grad_kernel, out_shape=(out, out), grid_spec=pltpu.Prefetc...]
    dot_general x16 -> x0, matrix products: 52.1 us -> none  [the longest x1 14.4 us: on_device(): lax.dot_general(cotangent, weights, (((1,), (1,)), ((), ())), preferred_e...]
    ppermute x7 -> x48, starting transfers between devices: 36.4 us -> 55.6 us  [the longest x14 24.4 us: on_ring(): first, second = (send(first, perm=onward), send(second, perm=backward))]
    unnamed x48 -> x184, local copies, waits for them, and re-layouts: 19.1 us -> 35.8 us
    unnamed x0 -> x22, other arithmetic: none -> 15.1 us
  transfers between devices with their start and end apart: 8 -> 48, of which waited for: 5 -> 20; matrix products, arithmetic and copies ran while one was open for 12% -> 5% of each run, Pallas kernels for 0% -> 18%
where the time goes in v3:
time: 307 us; the launch traced here: 305 us
  waiting for transfers between devices  112 us (36%)
  Pallas kernels  69.9 us (23%)
  starting transfers between devices  55.6 us (18%)
  local copies, waits for them, and re-layouts  37.9 us (12%)
  other arithmetic  26.3 us (9%)
    ppermute x14, waiting for transfers between devices, on_ring(): first, second = (send(first, perm=onward), send(second, perm=backward))  53.4 us
    unnamed x184, local copies, waits for them, and re-layouts  35.8 us
    pallas_call x8, Pallas kernels, grad_product(): pl.pallas_call(grad_kernel, out_shape=(out, out), grid_spec=pltpu.Prefetc...  26 us
    ppermute x14, starting transfers between devices, on_ring(): first, second = (send(first, perm=onward), send(second, perm=backward))  24.4 us
    pallas_call x3, Pallas kernels, project(): pl.pallas_call(functools.partial(project_kernel, len(groups), before is N...  21.7 us
    ppermute x5, waiting for transfers between devices, scatter_sum(): away = lax.ppermute(away, 'seq', [(i, i ^ 1 << step) for i in range(nseq)])  18.7 us
    ppermute x1, waiting for transfers between devices, on_ring(): cot_pair = jnp.concatenate([cotangent, send(cotangent, perm=swap_pair)], 0)  18.4 us
    unnamed x22, other arithmetic  15.1 us
  transfers between devices with their start and end apart: 48, of which 20 were waited for; matrix products, arithmetic and copies ran while one was open for 5% of the time, Pallas kernels for 18%

profile of v3, /device:TPU:0, one launch (start us, length us, event | category | flops | bytes accessed | tf_op | source)
XLA Modules:
  0.0 304.9 jit_solution(6779785505089612132)
XLA Ops:
  3.5 3.4 %collective-permute-start = (bf16[128,4096]{1,0:T(8,128)(2,1)}, bf16[128,4096]{1,0:T(8,128)(2,1)}, u32[]{:S(2)}, u32[]{:S(2)}) collective-permute-start(bf16[128,4096]{1,0:T(8,128)(2,1)} %fusion.product), channel_id=1, source_target_pairs={{0,1},{1,2},{2,3},{3,4},{4,5},{5,6},{6,7},{7,8},{8,9},{9,10},{10,1... | collective-permute-start | bytes 3145736 | tf_op jit(solution)/shard_map/ppermute | solution.py:348
  14.5 18.4 %collective-permute-done.4 = bf16[128,4096]{1,0:T(8,128)(2,1)} collective-permute-done((bf16[128,4096]{1,0:T(8,128)(2,1)}, bf16[128,4096]{1,0:T(8,128)(2,1)}, u32[]{:S(2)}, u32[]{:S(2)}) %collective-permute-start.4) | collective-permute-done | bytes 1048608 | tf_op jit(solution)/shard_map/ppermute | solution.py:346
  35.8 3.4 %shard_map.255 = (bf16[128,256]{1,0:T(8,128)(2,1)S(1)}, bf16[128,256]{1,0:T(8,128)(2,1)S(1)}) custom-call(s32[1]{0:T(128)} %bitcast.scalars, bf16[256,4096]{1,0:T(8,128)(2,1)S(1)} %constant_dynamic-update-slice_fusion.16.cot, bf16[64,4096]{1,0:T(8,128)(2,1)S(1)} %get-tuple-element.179.first.refs_0_, ...), custom_call_target="tpu_custom_call" | custom-call | flops 536870912 | bytes 4194304 | tf_op jit(solution)/shard_map/pallas_call | solution.py:190
  41.9 8.4 %shard_map.254 = (f32[256,4096]{1,0:T(8,128)S(1)}, f32[256,4096]{1,0:T(8,128)S(1)}, bf16[128,4096]{1,0:T(8,128)(2,1)S(1)}, bf16[128,4096]{1,0:T(8,128)(2,1)S(1)}) custom-call(s32[1]{0:T(128)} %bitcast.4.linked_ref, bf16[256,256]{1,0:T(8,128)(2,1)S(1)} %copy-done.57, bf16[256,256]{1,0:T(8,128)(2,1)S(1)} %copy-done.58, bf16[256,256]{1,0:T(8,128)(2,1)S(1)} %copy-done.59, ...), custom_call_target="tpu_custom_call" | custom-call | flops 1610612736 | bytes 14680064 | tf_op jit(solution)/shard_map/pallas_call | solution.py:144
  55.5 10.6 %collective-permute-start.9 = (bf16[64,4096]{1,0:T(8,128)(2,1)S(1)}, bf16[64,4096]{1,0:T(8,128)(2,1)S(1)}, u32[]{:S(2)}, u32[]{:S(2)}) collective-permute-start(bf16[64,4096]{1,0:T(8,128)(2,1)S(1)} %collective-permute-done.3.second.refs_5_), channel_id=1, source_target_pairs={{8,0},{9,1},{10,2},{11,3},{16,8},{17,9},{18,10},{19,11},{24,16},{2... | collective-permute-start | bytes 1572872 | tf_op jit(solution)/shard_map/ppermute | solution.py:375
  66.6 12.3 %collective-permute-done.8.first.refs_0_ = bf16[64,4096]{1,0:T(8,128)(2,1)S(1)} collective-permute-done((bf16[64,4096]{1,0:T(8,128)(2,1)}, bf16[64,4096]{1,0:T(8,128)(2,1)S(1)}, u32[]{:S(2)}, u32[]{:S(2)}) %collective-permute-start.8) | collective-permute-done | bytes 524320 | tf_op jit(solution)/shard_map/ppermute | solution.py:375
  92.5 3.3 %shard_map.257 = (bf16[128,256]{1,0:T(8,128)(2,1)S(1)}, bf16[128,256]{1,0:T(8,128)(2,1)S(1)}) custom-call(s32[1]{0:T(128)} %bitcast.scalars, bf16[256,4096]{1,0:T(8,128)(2,1)S(1)} %constant_dynamic-update-slice_fusion.16.cot, bf16[64,4096]{1,0:T(8,128)(2,1)S(1)} %collective-permute-done.8.first.refs_0_, ...), custom_call_target="tpu_custom_call" | custom-call | flops 536870912 | bytes 4194304 | tf_op jit(solution)/shard_map/pallas_call | solution.py:190
  99.1 4.1 %collective-permute-done.13.first.refs_4_ = bf16[64,4096]{1,0:T(8,128)(2,1)} collective-permute-done((bf16[64,4096]{1,0:T(8,128)(2,1)S(1)}, bf16[64,4096]{1,0:T(8,128)(2,1)}, u32[]{:S(2)}, u32[]{:S(2)}) %collective-permute-start.13) | collective-permute-done | bytes 524320 | tf_op jit(solution)/shard_map/ppermute | solution.py:375
  109.4 3.6 %shard_map.258 = (bf16[128,256]{1,0:T(8,128)(2,1)S(1)}, bf16[128,256]{1,0:T(8,128)(2,1)S(1)}) custom-call(s32[1]{0:T(128)} %bitcast.scalars, bf16[256,4096]{1,0:T(8,128)(2,1)S(1)} %constant_dynamic-update-slice_fusion.16.cot, bf16[64,4096]{1,0:T(8,128)(2,1)} %collective-permute-done.13.first.refs_4_, ...), custom_call_target="tpu_custom_call" | custom-call | flops 536870912 | bytes 4194304 | tf_op jit(solution)/shard_map/pallas_call | solution.py:190
  114.6 5.2 %collective-permute-done.18.first.refs_8_ = bf16[64,4096]{1,0:T(8,128)(2,1)S(1)} collective-permute-done((bf16[64,4096]{1,0:T(8,128)(2,1)}, bf16[64,4096]{1,0:T(8,128)(2,1)S(1)}, u32[]{:S(2)}, u32[]{:S(2)}) %collective-permute-start.18) | collective-permute-done | bytes 524320 | tf_op jit(solution)/shard_map/ppermute | solution.py:375
  129.6 6.8 %collective-permute-done.23.first.refs_12_ = bf16[64,4096]{1,0:T(8,128)(2,1)} collective-permute-done((bf16[64,4096]{1,0:T(8,128)(2,1)S(1)}, bf16[64,4096]{1,0:T(8,128)(2,1)}, u32[]{:S(2)}, u32[]{:S(2)}) %collective-permute-start.23) | collective-permute-done | bytes 524320 | tf_op jit(solution)/shard_map/ppermute | solution.py:375
  142.2 8.8 %collective-permute-done.29.refs_1_.second = bf16[64,4096]{1,0:T(8,128)(2,1)} collective-permute-done((bf16[64,4096]{1,0:T(8,128)(2,1)}, bf16[64,4096]{1,0:T(8,128)(2,1)}, u32[]{:S(2)}, u32[]{:S(2)}) %collective-permute-start.29) | collective-permute-done | bytes 524320 | tf_op jit(solution)/shard_map/ppermute | solution.py:375
  153.9 3.6 %shard_map.260 = (bf16[128,256]{1,0:T(8,128)(2,1)S(1)}, bf16[128,256]{1,0:T(8,128)(2,1)S(1)}) custom-call(s32[1]{0:T(128)} %bitcast.scalars, bf16[256,4096]{1,0:T(8,128)(2,1)S(1)} %constant_dynamic-update-slice_fusion.16.cot, bf16[64,4096]{1,0:T(8,128)(2,1)} %collective-permute-done.23.first.refs_12_, ...), custom_call_target="tpu_custom_call" | custom-call | flops 536870912 | bytes 4194304 | tf_op jit(solution)/shard_map/pallas_call | solution.py:190
  159.5 8.3 %shard_map.261.refs_8_ = f32[256,4096]{1,0:T(8,128)S(1)} custom-call(s32[5]{0:T(128)S(1)} %stack.74.scalars, bf16[256,2048]{1,0:T(8,128)(2,1)S(1)} %pad_maximum_fusion.gated_ref, bf16[64,4096]{1,0:T(8,128)(2,1)S(1)} %copy-done.26, bf16[64,4096]{1,0:T(8,128)(2,1)S(1)} %copy-done.24, bf16[64,4096]{1,0:T(8,128)(2,1)} %collective-permute-done.5.first_other.refs_2_, ...), custom_call_target="tpu_custom_call" | custom-call | flops 2147483648 | bytes 13631488 | tf_op jit(solution)/shard_map/pallas_call | solution.py:245
  170.0 6.6 %shard_map.264 = (bf16[128,4096]{1,0:T(8,128)(2,1)}, f32[128,4096]{1,0:T(8,128)S(1)}, bf16[128,4096]{1,0:T(8,128)(2,1)S(1)}, f32[128,4096]{1,0:T(8,128)S(1)}) custom-call(s32[6]{0:T(128)S(1)} %stack.77.scalars, bf16[256,256]{1,0:T(8,128)(2,1)S(1)} %copy-done.57, bf16[256,256]{1,0:T(8,128)(2,1)S(1)} %copy-done.58, bf16[256,256]{1,0:T(8,128)(2,1)S(1)} %copy-done.59, ...), custom_call_target="tpu_custom_call" | custom-call | flops 939524096 | bytes 8912896 | tf_op jit(solution)/shard_map/pallas_call | solution.py:307
  176.6 3.7 %shard_map.263 = (bf16[128,256]{1,0:T(8,128)(2,1)S(1)}, bf16[128,256]{1,0:T(8,128)(2,1)S(1)}) custom-call(s32[1]{0:T(128)} %bitcast.scalars, bf16[256,4096]{1,0:T(8,128)(2,1)S(1)} %constant_dynamic-update-slice_fusion.16.cot, bf16[64,4096]{1,0:T(8,128)(2,1)} %collective-permute-done.28.refs_4_.first, ...), custom_call_target="tpu_custom_call" | custom-call | flops 536870912 | bytes 4194304 | tf_op jit(solution)/shard_map/pallas_call | solution.py:190
  183.0 6.7 %shard_map.262.refs_8_ = f32[256,4096]{1,0:T(8,128)S(1)} custom-call(s32[3]{0:T(128)S(1)} %pad_add_fusion.1.scalars, bf16[256,2048]{1,0:T(8,128)(2,1)S(1)} %pad_maximum_fusion.gated_ref, bf16[64,4096]{1,0:T(8,128)(2,1)S(1)} %copy-done.38, bf16[64,4096]{1,0:T(8,128)(2,1)} %collective-permute-done.29.refs_1_.second, ...), custom_call_target="tpu_custom_call" | custom-call | flops 1073741824 | bytes 9437184 | tf_op jit(solution)/shard_map/pallas_call | solution.py:245
  192.9 3.7 %shard_map.265 = (bf16[128,4096]{1,0:T(8,128)(2,1)}, f32[128,4096]{1,0:T(8,128)S(1)}, bf16[128,4096]{1,0:T(8,128)(2,1)S(1)}, f32[128,4096]{1,0:T(8,128)S(1)}) custom-call(s32[4]{0:T(128)S(1)} %pad_add_fusion.2.scalars, bf16[256,256]{1,0:T(8,128)(2,1)S(1)} %copy-done.57, ...), custom_call_target="tpu_custom_call", output_to_operand_aliasing={{0}: (17, {}), {1}: (18, {}), {2}: (19, {}), {3}: (20, {})} | custom-call | flops 469762048 | bytes 4456448 | tf_op jit(solution)/shard_map/pallas_call | solution.py:307
  202.3 11.2 %collective-permute-done.36.refs_1_.second = bf16[64,4096]{1,0:T(8,128)(2,1)} collective-permute-done((bf16[64,4096]{1,0:T(8,128)(2,1)}, bf16[64,4096]{1,0:T(8,128)(2,1)}, u32[]{:S(2)}, u32[]{:S(2)}) %collective-permute-start.36) | collective-permute-done | bytes 524320 | tf_op jit(solution)/shard_map/ppermute | solution.py:375
  216.4 3.4 %shard_map.267 = (bf16[128,256]{1,0:T(8,128)(2,1)S(1)}, bf16[128,256]{1,0:T(8,128)(2,1)S(1)}) custom-call(s32[1]{0:T(128)} %bitcast.scalars, bf16[256,4096]{1,0:T(8,128)(2,1)S(1)} %constant_dynamic-update-slice_fusion.16.cot, bf16[64,4096]{1,0:T(8,128)(2,1)} %collective-permute-done.38.refs_4_.first, ...), custom_call_target="tpu_custom_call" | custom-call | flops 536870912 | bytes 4194304 | tf_op jit(solution)/shard_map/pallas_call | solution.py:190
  235.8 3.7 %shard_map.268 = (bf16[128,4096]{1,0:T(8,128)(2,1)}, f32[128,4096]{1,0:T(8,128)S(1)}, bf16[128,4096]{1,0:T(8,128)(2,1)S(1)}, f32[128,4096]{1,0:T(8,128)S(1)}) custom-call(s32[4]{0:T(128)S(1)} %pad_add_fusion.4.scalars, bf16[256,256]{1,0:T(8,128)(2,1)S(1)} %copy-done.57, ...), custom_call_target="tpu_custom_call", output_to_operand_aliasing={{0}: (17, {}), {1}: (18, {}), {2}: (19, {}), {3}: (20, {})} | custom-call | flops 469762048 | bytes 4456448 | tf_op jit(solution)/shard_map/pallas_call | solution.py:307
  256.3 6.7 %shard_map.266 = (f32[128,4096]{1,0:T(8,128)S(1)}, bf16[128,4096]{1,0:T(8,128)(2,1)S(1)}) custom-call(s32[3]{0:T(128)S(1)} %pad_add_fusion.scalars, bf16[256,2048]{1,0:T(8,128)(2,1)S(1)} %pad_maximum_fusion.gated_ref, bf16[64,4096]{1,0:T(8,128)(2,1)} %collective-permute-done.2.first.refs_0_, bf16[64,4096]{1,0:T(8,128)(2,1)} %collective-permute-done.36.refs_1_.second, ...), custom_call_target="tpu_custom_call" | custom-call | flops 1073741824 | bytes 9437184 | tf_op jit(solution)/shard_map/pallas_call | solution.py:245
  268.6 15.8 %collective-permute-done.45 = bf16[128,512]{1,0:T(8,128)(2,1)S(1)} collective-permute-done((bf16[128,512]{1,0:T(8,128)(2,1)S(1)}, bf16[128,512]{1,0:T(8,128)(2,1)S(1)}, u32[]{:S(2)}, u32[]{:S(2)}) %collective-permute-start.45) | collective-permute-done | bytes 131104 | tf_op jit(solution)/shard_map/ppermute | solution.py:70
  286.5 11.8 %collective-permute-done.40 = bf16[128,4096]{1,0:T(8,128)(2,1)S(1)} collective-permute-done((bf16[128,4096]{1,0:T(8,128)(2,1)S(1)}, bf16[128,4096]{1,0:T(8,128)(2,1)S(1)}, u32[]{:S(2)}, u32[]{:S(2)}) %collective-permute-start.40) | collective-permute-done | bytes 1048608 | tf_op jit(solution)/shard_map/ppermute | solution.py:398
  (321 shorter events, 128.5 us)
Async XLA Ops:
  3.5 38.3 %collective-permute-start = (bf16[128,4096]{1,0:T(8,128)(2,1)}, bf16[128,4096]{1,0:T(8,128)(2,1)}, u32[]{:S(2)}, u32[]{:S(2)}) collective-permute-start(bf16[128,4096]{1,0:T(8,128)(2,1)} %fusion.product), channel_id=1, source_target_pairs={{0,1},{1,2},{2,3},{3,4},{4,5},{5,6},{6,7},{7,8},{8,9},{9,10},{10,1... | collective-permute-start | bytes 3145736 | tf_op jit(solution)/shard_map/ppermute | solution.py:348
  6.9 26.0 %collective-permute-start.4 = (bf16[128,4096]{1,0:T(8,128)(2,1)}, bf16[128,4096]{1,0:T(8,128)(2,1)}, u32[]{:S(2)}, u32[]{:S(2)}) collective-permute-start(bf16[128,4096]{1,0:T(8,128)(2,1)} %param.29), channel_id=1, source_target_pairs={{0,2},{1,3},{2,0},{3,1},{4,6},{5,7},{6,4},{7,5},{8,10},{9,11},{10,... | collective-permute-start | bytes 3145736 | tf_op jit(solution)/shard_map/ppermute | solution.py:346
  8.7 45.6 %collective-permute-start.2 = (bf16[64,4096]{1,0:T(8,128)(2,1)S(1)}, bf16[64,4096]{1,0:T(8,128)(2,1)}, u32[]{:S(2)}, u32[]{:S(2)}) collective-permute-start(bf16[64,4096]{1,0:T(8,128)(2,1)S(1)} %get-tuple-element.179.first.refs_0_), channel_id=1, source_target_pairs={{0,8},{1,9},{2,10},{3,11},{8,16},{9,17},{10,18},{11,19},{16,24},{1... | collective-permute-start | bytes 1572872 | tf_op jit(solution)/shard_map/ppermute | solution.py:375
  10.3 25.4 %collective-permute-start.5 = (bf16[64,4096]{1,0:T(8,128)(2,1)S(1)}, bf16[64,4096]{1,0:T(8,128)(2,1)}, u32[]{:S(2)}, u32[]{:S(2)}) collective-permute-start(bf16[64,4096]{1,0:T(8,128)(2,1)S(1)} %get-tuple-element.179.first.refs_0_), channel_id=1, source_target_pairs={{0,1},{1,0},{2,3},{3,2},{4,5},{5,4},{6,7},{7,6},{8,9},{9,8},{10,11... | collective-permute-start | bytes 1572872 | tf_op jit(solution)/shard_map/ppermute | solution.py:376
  11.3 24.3 %collective-permute-start.6 = (bf16[64,4096]{1,0:T(8,128)(2,1)S(1)}, bf16[64,4096]{1,0:T(8,128)(2,1)}, u32[]{:S(2)}, u32[]{:S(2)}) collective-permute-start(bf16[64,4096]{1,0:T(8,128)(2,1)S(1)} %get-tuple-element.178.second.refs_1_), channel_id=1, source_target_pairs={{0,1},{1,0},{2,3},{3,2},{4,5},{5,4},{6,7},{7,6},{8,9},{9,8},{10,11... | collective-permute-start | bytes 1572872 | tf_op jit(solution)/shard_map/ppermute | solution.py:377
  33.0 21.3 %collective-permute-start.3 = (bf16[64,4096]{1,0:T(8,128)(2,1)S(1)}, bf16[64,4096]{1,0:T(8,128)(2,1)S(1)}, u32[]{:S(2)}, u32[]{:S(2)}) collective-permute-start(bf16[64,4096]{1,0:T(8,128)(2,1)S(1)} %get-tuple-element.178.second.refs_1_), channel_id=1, source_target_pairs={{8,0},{9,1},{10,2},{11,3},{16,8},{17,9},{18,10},{19,11},{24,16},{2... | collective-permute-start | bytes 1572872 | tf_op jit(solution)/shard_map/ppermute | solution.py:375
  39.8 14.4 %collective-permute-start.7 = (bf16[128,256]{1,0:T(8,128)(2,1)S(1)}, bf16[128,256]{1,0:T(8,128)(2,1)S(1)}, u32[]{:S(2)}, u32[]{:S(2)}) collective-permute-start(bf16[128,256]{1,0:T(8,128)(2,1)S(1)} %get-tuple-element.70), channel_id=1, source_target_pairs={{0,2},{1,3},{2,0},{3,1},{4,6},{5,7},{6,4},{7,5},{8,10},{9,11},{10,... | collective-permute-start | bytes 196616 | tf_op jit(solution)/shard_map/ppermute | solution.py:380
  54.9 23.9 %collective-permute-start.8 = (bf16[64,4096]{1,0:T(8,128)(2,1)}, bf16[64,4096]{1,0:T(8,128)(2,1)S(1)}, u32[]{:S(2)}, u32[]{:S(2)}) collective-permute-start(bf16[64,4096]{1,0:T(8,128)(2,1)} %collective-permute-done.2.first.refs_0_), channel_id=1, source_target_pairs={{0,8},{1,9},{2,10},{3,11},{8,16},{9,17},{10,18},{11,19},{16,24},{1... | collective-permute-start | bytes 1572872 | tf_op jit(solution)/shard_map/ppermute | solution.py:375
  55.5 23.4 %collective-permute-start.9 = (bf16[64,4096]{1,0:T(8,128)(2,1)S(1)}, bf16[64,4096]{1,0:T(8,128)(2,1)S(1)}, u32[]{:S(2)}, u32[]{:S(2)}) collective-permute-start(bf16[64,4096]{1,0:T(8,128)(2,1)S(1)} %collective-permute-done.3.second.refs_5_), channel_id=1, source_target_pairs={{8,0},{9,1},{10,2},{11,3},{16,8},{17,9},{18,10},{19,11},{24,16},{2... | collective-permute-start | bytes 1572872 | tf_op jit(solution)/shard_map/ppermute | solution.py:375
  66.1 13.3 %collective-permute-start.10 = (bf16[64,4096]{1,0:T(8,128)(2,1)}, bf16[64,4096]{1,0:T(8,128)(2,1)S(1)}, u32[]{:S(2)}, u32[]{:S(2)}) collective-permute-start(bf16[64,4096]{1,0:T(8,128)(2,1)} %collective-permute-done.2.first.refs_0_), channel_id=1, source_target_pairs={{0,1},{1,0},{2,3},{3,2},{4,5},{5,4},{6,7},{7,6},{8,9},{9,8},{10,11... | collective-permute-start | bytes 1572872 | tf_op jit(solution)/shard_map/ppermute | solution.py:376
  78.9 13.6 %collective-permute-start.15 = (bf16[64,4096]{1,0:T(8,128)(2,1)S(1)}, bf16[64,4096]{1,0:T(8,128)(2,1)}, u32[]{:S(2)}, u32[]{:S(2)}) collective-permute-start(bf16[64,4096]{1,0:T(8,128)(2,1)S(1)} %collective-permute-done.8.first.refs_0_), channel_id=1, source_target_pairs={{0,1},{1,0},{2,3},{3,2},{4,5},{5,4},{6,7},{7,6},{8,9},{9,8},{10,11... | collective-permute-start | bytes 1572872 | tf_op jit(solution)/shard_map/ppermute | solution.py:376
  78.9 13.6 %collective-permute-start.16 = (bf16[64,4096]{1,0:T(8,128)(2,1)S(1)}, bf16[64,4096]{1,0:T(8,128)(2,1)}, u32[]{:S(2)}, u32[]{:S(2)}) collective-permute-start(bf16[64,4096]{1,0:T(8,128)(2,1)S(1)} %collective-permute-done.9.second.refs_5_), channel_id=1, source_target_pairs={{0,1},{1,0},{2,3},{3,2},{4,5},{5,4},{6,7},{7,6},{8,9},{9,8},{10,11... | collective-permute-start | bytes 1572872 | tf_op jit(solution)/shard_map/ppermute | solution.py:377
  90.4 14.8 %collective-permute-start.14 = (bf16[64,4096]{1,0:T(8,128)(2,1)S(1)}, bf16[64,4096]{1,0:T(8,128)(2,1)}, u32[]{:S(2)}, u32[]{:S(2)}) collective-permute-start(bf16[64,4096]{1,0:T(8,128)(2,1)S(1)} %collective-permute-done.9.second.refs_5_), channel_id=1, source_target_pairs={{8,0},{9,1},{10,2},{11,3},{16,8},{17,9},{18,10},{19,11},{24,16},{2... | collective-permute-start | bytes 1572872 | tf_op jit(solution)/shard_map/ppermute | solution.py:375
  105.3 14.5 %collective-permute-start.18 = (bf16[64,4096]{1,0:T(8,128)(2,1)}, bf16[64,4096]{1,0:T(8,128)(2,1)S(1)}, u32[]{:S(2)}, u32[]{:S(2)}) collective-permute-start(bf16[64,4096]{1,0:T(8,128)(2,1)} %collective-permute-done.13.first.refs_4_), channel_id=1, source_target_pairs={{0,8},{1,9},{2,10},{3,11},{8,16},{9,17},{10,18},{11,19},{16,24},{1... | collective-permute-start | bytes 1572872 | tf_op jit(solution)/shard_map/ppermute | solution.py:375
  107.1 14.2 %collective-permute-start.19 = (bf16[64,4096]{1,0:T(8,128)(2,1)}, bf16[64,4096]{1,0:T(8,128)(2,1)S(1)}, u32[]{:S(2)}, u32[]{:S(2)}) collective-permute-start(bf16[64,4096]{1,0:T(8,128)(2,1)} %collective-permute-done.14.second.refs_13_), channel_id=1, source_target_pairs={{8,0},{9,1},{10,2},{11,3},{16,8},{17,9},{18,10},{19,11},{24,16},{2... | collective-permute-start | bytes 1572872 | tf_op jit(solution)/shard_map/ppermute | solution.py:375
  122.0 14.4 %collective-permute-start.23 = (bf16[64,4096]{1,0:T(8,128)(2,1)S(1)}, bf16[64,4096]{1,0:T(8,128)(2,1)}, u32[]{:S(2)}, u32[]{:S(2)}) collective-permute-start(bf16[64,4096]{1,0:T(8,128)(2,1)S(1)} %collective-permute-done.18.first.refs_8_), channel_id=1, source_target_pairs={{0,8},{1,9},{2,10},{3,11},{8,16},{9,17},{10,18},{11,19},{16,24},{1... | collective-permute-start | bytes 1572872 | tf_op jit(solution)/shard_map/ppermute | solution.py:375
  123.3 14.1 %collective-permute-start.24 = (bf16[64,4096]{1,0:T(8,128)(2,1)S(1)}, bf16[64,4096]{1,0:T(8,128)(2,1)}, u32[]{:S(2)}, u32[]{:S(2)}) collective-permute-start(bf16[64,4096]{1,0:T(8,128)(2,1)S(1)} %collective-permute-done.19.second.refs_9_), channel_id=1, source_target_pairs={{8,0},{9,1},{10,2},{11,3},{16,8},{17,9},{18,10},{19,11},{24,16},{2... | collective-permute-start | bytes 1572872 | tf_op jit(solution)/shard_map/ppermute | solution.py:375
  137.4 13.5 %collective-permute-start.29 = (bf16[64,4096]{1,0:T(8,128)(2,1)}, bf16[64,4096]{1,0:T(8,128)(2,1)}, u32[]{:S(2)}, u32[]{:S(2)}) collective-permute-start(bf16[64,4096]{1,0:T(8,128)(2,1)} %collective-permute-done.24.second.refs_5_), channel_id=1, source_target_pairs={{8,0},{9,1},{10,2},{11,3},{16,8},{17,9},{18,10},{19,11},{24,16},{2... | collective-permute-start | bytes 1572872 | tf_op jit(solution)/shard_map/ppermute | solution.py:375
  151.0 25.6 %collective-permute-start.33 = (bf16[64,4096]{1,0:T(8,128)(2,1)}, bf16[64,4096]{1,0:T(8,128)(2,1)S(1)}, u32[]{:S(2)}, u32[]{:S(2)}) collective-permute-start(bf16[64,4096]{1,0:T(8,128)(2,1)} %collective-permute-done.29.refs_1_.second), channel_id=1, source_target_pairs={{0,1},{1,0},{2,3},{3,2},{4,5},{5,4},{6,7},{7,6},{8,9},{9,8},{10,11... | collective-permute-start | bytes 1572872 | tf_op jit(solution)/shard_map/ppermute | solution.py:377
  151.4 25.2 %collective-permute-start.34 = (bf16[64,4096]{1,0:T(8,128)(2,1)}, bf16[64,4096]{1,0:T(8,128)(2,1)S(1)}, u32[]{:S(2)}, u32[]{:S(2)}) collective-permute-start(bf16[64,4096]{1,0:T(8,128)(2,1)} %collective-permute-done.28.refs_4_.first), channel_id=1, source_target_pairs={{0,1},{1,0},{2,3},{3,2},{4,5},{5,4},{6,7},{7,6},{8,9},{9,8},{10,11... | collective-permute-start | bytes 1572872 | tf_op jit(solution)/shard_map/ppermute | solution.py:376
  263.0 35.3 %collective-permute-start.40 = (bf16[128,4096]{1,0:T(8,128)(2,1)S(1)}, bf16[128,4096]{1,0:T(8,128)(2,1)S(1)}, u32[]{:S(2)}, u32[]{:S(2)}) collective-permute-start(bf16[128,4096]{1,0:T(8,128)(2,1)S(1)} %get-tuple-element.118), channel_id=1, source_target_pairs={{0,2},{1,3},{2,0},{3,1},{4,6},{5,7},{6,4},{7,5},{8,10},{9,11},{10,... | collective-permute-start | bytes 3145736 | tf_op jit(solution)/shard_map/ppermute | solution.py:398
  264.4 37.7 %collective-permute-start.42 = (bf16[128,4096]{1,0:T(8,128)(2,1)S(1)}, bf16[128,4096]{1,0:T(8,128)(2,1)S(1)}, u32[]{:S(2)}, u32[]{:S(2)}) collective-permute-start(bf16[128,4096]{1,0:T(8,128)(2,1)S(1)} %copy-done.30), channel_id=1, source_target_pairs={{1,0},{2,1},{3,2},{4,3},{5,4},{6,5},{7,6},{8,7},{9,8},{10,9},{11,1... | collective-permute-start | bytes 3145736 | tf_op jit(solution)/shard_map/ppermute | solution.py:395
  265.9 18.6 %collective-permute-start.45 = (bf16[128,512]{1,0:T(8,128)(2,1)S(1)}, bf16[128,512]{1,0:T(8,128)(2,1)S(1)}, u32[]{:S(2)}, u32[]{:S(2)}) collective-permute-start(bf16[128,512]{1,0:T(8,128)(2,1)S(1)} %pad_maximum_fusion.2), channel_id=1, source_target_pairs={{0,8},{1,9},{2,10},{3,11},{4,12},{5,13},{6,14},{7,15},{8,0},{9,1},... | collective-permute-start | bytes 393224 | tf_op jit(solution)/shard_map/ppermute | solution.py:70
  284.5 15.0 %collective-permute-start.46 = (bf16[128,256]{1,0:T(8,128)(2,1)S(1)}, bf16[128,256]{1,0:T(8,128)(2,1)S(1)}, u32[]{:S(2)}, u32[]{:S(2)}) collective-permute-start(bf16[128,256]{1,0:T(8,128)(2,1)S(1)} %select_convert_fusion), channel_id=1, source_target_pairs={{0,16},{1,17},{2,18},{3,19},{4,20},{5,21},{6,22},{7,23},{8,24},{9,... | collective-permute-start | bytes 196616 | tf_op jit(solution)/shard_map/ppermute | solution.py:70
  (115 other events, 780.4 us)

commit v4 on v3

--- a/solution.py
+++ b/solution.py
@@ -49,27 +49,44 @@
     return (a.astype(F32) * b.astype(F32)).astype(BF16)
 
 
-def pick(data, width, side):
-    blocks = [data[:, i : i + width] for i in range(0, data.shape[1], width)]
-    return jnp.concatenate([jnp.where(side == 0, a, b) for a, b in zip(blocks[::2], blocks[1::2])], 1)
-
-
-def scatter_sum(part, nseq, place, order):
-    share = part.shape[1] // nseq
+def scatter_sum(part, nseq, place):
     bits = nseq.bit_length() - 1
-    if nseq != 1 << bits:
-        return lax.psum_scatter(part, "seq", scatter_dimension=1, tiled=True)
-    left = list(range(bits))
-    for step in [b for b in order if b < bits] + [b for b in range(bits) if b not in order]:
-        width = share << sum(b < step for b in left)
-        left.remove(step)
+    lags = part.shape[-2]
+    chans = part.shape[-1]
+    for step in range(bits):
         mine = (place >> step) & 1
-        away = pick(part, width, 1 - mine)
+        part = part.reshape(-1, 2, lags, chans)
+        away = lax.dynamic_index_in_dim(part, 1 - mine, 1, False)
+        kept = lax.dynamic_index_in_dim(part, mine, 1, False)
         if step:
             away = away.astype(BF16)
         away = lax.ppermute(away, "seq", [(i, i ^ (1 << step)) for i in range(nseq)])
-        part = pick(part, width, mine) + away.astype(F32)
-    return part
+        part = kept + away.astype(F32)
+    return part[0]
+
+
+def sum_over_ring(part, nseq, place):
+    core, pair, row = place & 1, (place >> 1) & 1, place >> 2
+    four, size, lags, chans = part.shape
+
+    def halve(part, bit, mine, kind):
+        away = lax.dynamic_index_in_dim(part, 1 - mine, 1, False).astype(kind)
+        away = lax.ppermute(away, "seq", [(i, i ^ bit) for i in range(nseq)])
+        return lax.dynamic_index_in_dim(part, mine, 1, False) + away.astype(F32)
+
+    part = halve(part.reshape(2, 2, size, lags, chans), 1, core, F32)
+    part = halve(part.reshape(1, 2, size, lags, chans), 2, pair, BF16).reshape(size, lags, chans)
+    if size & (size - 1):
+        return lax.psum_scatter(
+            part, "seq", scatter_dimension=0,
+            axis_index_groups=[[4 * r + k for r in range(size)] for k in range(4)],
+        )
+    left = size
+    while left > 1:
+        bit = size // left
+        part = halve(part.reshape(left // 2, 2, lags, chans), 4 * bit, (row // bit) & 1, BF16)
+        left //= 2
+    return part.reshape(lags, chans)
 
 
 def links(seg_ids, place):
@@ -125,7 +142,10 @@
     filtered = dot_three(inv_hi[length:], inv_lo[length:], times(filt, data)) * (1.0 / length)
     filtered = filtered.astype(BF16)
     filtered_ref[...] = filtered
-    gated_ref[...] = mul(queries[...], filtered)
+    gated = mul(queries[...], filtered)
+    half = gated.shape[1] // 2
+    gated_ref[0] = gated[:, :half]
+    gated_ref[1] = gated[:, half:]
 
 
 def tables(length):
@@ -135,7 +155,7 @@
 
 def forward_filter(linked, before, product, taps, queries):
     length, chans = product.shape
-    width = min(512, chans)
+    width = 4 * length
     fixed = pl.BlockSpec((2 * length, 2 * length), lambda j: (0, 0))
     block = pl.BlockSpec((length, width), lambda j: (0, j))
     spectrum = pl.BlockSpec((2 * length, width), lambda j: (0, j))
@@ -143,20 +163,20 @@
     narrow = jax.ShapeDtypeStruct((length, chans), BF16)
     return pl.pallas_call(
         forward_kernel,
-        out_shape=(wide, wide, narrow, narrow),
+        out_shape=(wide, wide, narrow, jax.ShapeDtypeStruct((2, length, chans // 2), BF16)),
         grid=(chans // width,),
         in_specs=[pl.BlockSpec(memory_space=pltpu.SMEM)]
         + [fixed] * 4
         + [block, block, pl.BlockSpec((width, length), lambda j: (j, 0)), block],
-        out_specs=(spectrum, spectrum, block, block),
-        compiler_params=pltpu.CompilerParams(vmem_limit_bytes=32 << 20),
+        out_specs=(spectrum, spectrum, block, pl.BlockSpec((2, length, width // 2), lambda j: (0, 0, j))),
+        compiler_params=pltpu.CompilerParams(vmem_limit_bytes=12 << 20),
         cost_estimate=pl.CostEstimate(
             flops=24 * length * length * chans, bytes_accessed=28 * length * chans, transcendentals=0
         ),
     )(linked.astype(jnp.int32).reshape(1), *tables(length), before, product, taps, queries)
 
 
-def grad_kernel(scalars, cot, first, first_other, second, second_other, own_ref, away_ref, total):
+def grad_kernel(scalars, cot_own, cot_away, first, first_other, second, second_other, own_ref, away_ref, total):
     @pl.when(pl.program_id(0) == 0)
     def _():
         total[...] = jnp.zeros_like(total)
@@ -164,7 +184,8 @@
     def add(refs):
         rows = jnp.concatenate([ref[...] for ref in refs], 0)
         dims = (((1,), (1,)), ((), ()))
-        total[...] += lax.dot_general(cot[...], rows, dims, preferred_element_type=F32)
+        cot = jnp.concatenate([cot_own[...], cot_away[...]], 0)
+        total[...] += lax.dot_general(cot, rows, dims, preferred_element_type=F32)
 
     @pl.when(scalars[0] == 0)
     def _():
@@ -181,11 +202,12 @@
         away_ref[...] = total[rows:].astype(BF16)
 
 
-def grad_product(core, cot, weights):
-    tokens, feats = cot.shape
+def grad_product(core, cot_own, cot_away, weights):
+    rows, feats = cot_own.shape
+    tokens = 2 * rows
     depth = weights[0].shape[0]
     tile = min(1024, feats)
-    out = jax.ShapeDtypeStruct((tokens // 2, 4 * depth), BF16)
+    out = jax.ShapeDtypeStruct((rows, 4 * depth), BF16)
     whole = pl.BlockSpec(out.shape, lambda j, core: (0, 0))
     return pl.pallas_call(
         grad_kernel,
@@ -193,29 +215,43 @@
         grid_spec=pltpu.PrefetchScalarGridSpec(
             num_scalar_prefetch=1,
             grid=(feats // tile,),
-            in_specs=[pl.BlockSpec((tokens, tile), lambda j, core: (0, j))]
+            in_specs=[pl.BlockSpec((rows, tile), lambda j, core: (0, j))] * 2
             + [pl.BlockSpec((depth, tile), lambda j, core: (0, j))] * 4,
             out_specs=(whole, whole),
             scratch_shapes=[pltpu.VMEM((tokens, 4 * depth), F32)],
         ),
-        compiler_params=pltpu.CompilerParams(vmem_limit_bytes=16 << 20),
+        compiler_params=pltpu.CompilerParams(vmem_limit_bytes=8 << 20),
         cost_estimate=pl.CostEstimate(
             flops=8 * tokens * depth * feats, bytes_accessed=(2 * tokens + 8 * depth) * feats, transcendentals=0
         ),
-    )(core, cot, *weights)
-
-
-def project_kernel(count, first, last, scalars, gated_ref, *refs):
+    )(core, cot_own, cot_away, *weights)
+
+
+def project_kernel(count, first, last, scalars, gated_own, gated_away, *refs):
     weights, refs = refs[: 4 * count], refs[4 * count :]
-    width = 4 * weights[0].shape[0]
-    total = refs[-1]
+    depth = weights[0].shape[0]
+    width = 4 * depth
+    left, total = refs[-2:]
+
+    @pl.when(pl.program_id(0) == 0)
+    def _():
+        for i in range(count):
+            for part, ref in enumerate((gated_own, gated_away)):
+                blocks = [
+                    ref[:, pl.ds(pl.multiple_of(scalars[1 + 2 * i + way] * width, width), width)] for way in (0, 1)
+                ]
+                rows = ref.shape[0]
+                left[i, part * rows : (part + 1) * rows] = jnp.concatenate(
+                    [blocks[way][:, (2 * k + way) * depth : (2 * k + way + 1) * depth] for way in (0, 1) for k in (0, 1)],
+                    1,
+                )
+
     total[...] = jnp.zeros_like(total) if first else refs[0][...]
 
     def add(order):
         for i in range(count):
-            left = gated_ref[:, pl.ds(pl.multiple_of(scalars[1 + i] * width, width), width)]
             right = jnp.concatenate([weights[4 * i + k][...] for k in order], 0)
-            total[...] += dot(left, right)
+            total[...] += dot(left[i], right)
 
     @pl.when(scalars[0] == 0)
     def _():
@@ -223,44 +259,47 @@
 
     @pl.when(scalars[0] != 0)
     def _():
-        add((2, 3, 0, 1))
+        add((1, 0, 3, 2))
 
     if last:
-        own_ref, away_ref = refs[-3:-1]
+        own_ref, away_ref = refs[-4:-2]
         rows = own_ref.shape[0]
         own_ref[...] = total[:rows]
         away_ref[...] = total[rows:].astype(BF16)
     else:
-        refs[-2][...] = total[...]
-
-
-def project(scalars, gated, groups, before=None, last=False):
-    tokens = gated.shape[0]
+        refs[-3][...] = total[...]
+
+
+def project(scalars, gated_own, gated_away, groups, before=None, last=False):
+    rows, chans = gated_own.shape
     depth, feats = groups[0][0].shape
-    tile = min(512, feats)
+    tile = min(1024, feats)
     weights = [w for group in groups for w in group]
-    whole = pl.BlockSpec((tokens, tile), lambda j, s: (0, j))
-    block = pl.BlockSpec((tokens // 2, tile), lambda j, s: (0, j))
-    halves = tuple(jax.ShapeDtypeStruct((tokens // 2, feats), kind) for kind in (F32, BF16))
+    whole = pl.BlockSpec((2 * rows, tile), lambda j, s: (0, j))
+    block = pl.BlockSpec((rows, tile), lambda j, s: (0, j))
+    halves = tuple(jax.ShapeDtypeStruct((rows, feats), kind) for kind in (F32, BF16))
     return pl.pallas_call(
         functools.partial(project_kernel, len(groups), before is None, last),
-        out_shape=halves if last else jax.ShapeDtypeStruct((tokens, feats), F32),
+        out_shape=halves if last else jax.ShapeDtypeStruct((2 * rows, feats), F32),
         grid_spec=pltpu.PrefetchScalarGridSpec(
             num_scalar_prefetch=1,
             grid=(feats // tile,),
-            in_specs=[pl.BlockSpec(gated.shape, lambda j, s: (0, 0))]
+            in_specs=[pl.BlockSpec(gated_own.shape, lambda j, s: (0, 0))] * 2
             + [pl.BlockSpec((depth, tile), lambda j, s: (0, j))] * len(weights)
             + [whole] * (before is not None),
             out_specs=(block, block) if last else whole,
-            scratch_shapes=[pltpu.VMEM((tokens, tile), F32)],
-        ),
-        compiler_params=pltpu.CompilerParams(vmem_limit_bytes=32 << 20),
+            scratch_shapes=[
+                pltpu.VMEM((len(groups), 2 * rows, 4 * depth), BF16),
+                pltpu.VMEM((2 * rows, tile), F32),
+            ],
+        ),
+        compiler_params=pltpu.CompilerParams(vmem_limit_bytes=16 << 20),
         cost_estimate=pl.CostEstimate(
-            flops=2 * tokens * depth * len(weights) * feats,
-            bytes_accessed=2 * depth * feats * len(weights) + 2 * gated.size + 4 * tokens * feats,
+            flops=4 * rows * depth * len(weights) * feats,
+            bytes_accessed=2 * depth * feats * len(weights) + 4 * rows * chans + 8 * rows * feats,
             transcendentals=0,
         ),
-    )(scalars, gated, *weights, *([] if before is None else [before]))
+    )(scalars, gated_own, gated_away, *weights, *([] if before is None else [before]))
 
 
 def backward_kernel(count, scalars, fwd_hi, fwd_lo, inv_hi, inv_lo, queries, filtered, data, filt, *refs):
@@ -288,9 +327,11 @@
     grad_filtered = mul(grad_gated, queries[...])
     grads = dot(fwd_hi[:, length:], grad_filtered) + dot(fwd_lo[:, length:], grad_filtered)
     back = dot_three(inv_hi[...], inv_lo[...], times_conj(grads, filt[...])) * (1.0 / length)
-    across_ref[...] = jnp.where(scalars[1] == 1, back[:length], 0.0).astype(BF16)
+    across_ref[0] = jnp.where(scalars[1] == 1, back[:length], 0.0).astype(BF16)
     near_ref[...] = back[length:]
-    taps_ref[...] = dot_three(inv_hi[length:], inv_lo[length:], times_conj(grads, data[...])) * (1.0 / length)
+    taps = dot_three(inv_hi[length:], inv_lo[length:], times_conj(grads, data[...])) * (1.0 / length)
+    for k in range(4):
+        taps_ref[k, 0] = taps[:, k * length : (k + 1) * length]
 
 
 def backward_filter(scalars, groups, queries, filtered, data, filt, before=None):
@@ -302,11 +343,16 @@
     block = pl.BlockSpec((length, width), lambda j, s: (0, s[2 + j]))
     spectrum = pl.BlockSpec((2 * length, width), lambda j, s: (0, s[2 + j]))
     piece = pl.BlockSpec((length, 2 * length), lambda j, s: (0, 0))
-    before = [] if before is None else list(before)
+    before = [] if before is None else [before[0], before[1], before[3]]
     inputs = 9 + len(pieces)
     return pl.pallas_call(
         functools.partial(backward_kernel, count),
-        out_shape=tuple(jax.ShapeDtypeStruct((length, chans), kind) for kind in (BF16, F32, BF16, F32)),
+        out_shape=(
+            jax.ShapeDtypeStruct((length, chans), BF16),
+            jax.ShapeDtypeStruct((length, chans), F32),
+            jax.ShapeDtypeStruct((count, length, width), BF16),
+            jax.ShapeDtypeStruct((4, chans // width, length, length), F32),
+        ),
         grid_spec=pltpu.PrefetchScalarGridSpec(
             num_scalar_prefetch=1,
             grid=(count,),
@@ -314,15 +360,55 @@
             + [block, block, spectrum, spectrum]
             + [piece] * len(pieces)
             + [pl.BlockSpec(memory_space=pl.ANY)] * len(before),
-            out_specs=(block,) * 4,
+            out_specs=(
+                block,
+                block,
+                pl.BlockSpec((1, length, width), lambda j, s: (j, 0, 0)),
+                pl.BlockSpec((4, 1, length, length), lambda j, s: (0, s[2 + j], 0, 0)),
+            ),
             scratch_shapes=[pltpu.VMEM((length, width), BF16)],
         ),
-        input_output_aliases={inputs + i: i for i in range(len(before))},
-        compiler_params=pltpu.CompilerParams(vmem_limit_bytes=32 << 20),
+        input_output_aliases={inputs + i: out for i, out in zip(range(len(before)), (0, 1, 3))},
+        compiler_params=pltpu.CompilerParams(vmem_limit_bytes=16 << 20),
         cost_estimate=pl.CostEstimate(
             flops=28 * length * length * width * count, bytes_accessed=34 * length * width * count, transcendentals=0
         ),
     )(scalars, *tables(length), queries, filtered, data, filt, *pieces, *before)
+
+
+def join_kernel(count, scalars, near, keys, values, *refs):
+    parts, (grad_keys, grad_values) = refs[:count], refs[count:]
+    j = pl.program_id(0)
+    total = near[...]
+    for i, part in enumerate(parts):
+        total = total + jnp.where(scalars[j] == i, part[0].astype(F32), 0.0)
+    total = total.astype(BF16)
+    grad_keys[...] = mul(total, values[...])
+    grad_values[...] = mul(total, keys[...])
+
+
+def join(scalars, near, keys, values, parts):
+    length, chans = near.shape
+    width = parts[0].shape[2]
+    count = chans // width
+    block = pl.BlockSpec((length, width), lambda j, s: (0, j))
+    out = jax.ShapeDtypeStruct((length, chans), BF16)
+
+    def place(i):
+        return lambda j, s: (s[(1 + i) * count + j], 0, 0)
+
+    return pl.pallas_call(
+        functools.partial(join_kernel, len(parts)),
+        out_shape=(out, out),
+        grid_spec=pltpu.PrefetchScalarGridSpec(
+            num_scalar_prefetch=1,
+            grid=(count,),
+            in_specs=[block] * 3 + [pl.BlockSpec((1, length, width), place(i)) for i in range(len(parts))],
+            out_specs=(block, block),
+        ),
+        compiler_params=pltpu.CompilerParams(vmem_limit_bytes=6 << 20),
+        cost_estimate=pl.CostEstimate(flops=4 * length * chans, bytes_accessed=14 * length * chans, transcendentals=0),
+    )(scalars, near, keys, values, *parts)
 
 
 def on_ring(queries, keys, values, w_out, taps, seg_ids, cotangent):
@@ -340,65 +426,85 @@
     later = [(i, i + 1) for i in range(nseq - 1)]
     earlier = [(i + 1, i) for i in range(nseq - 1)]
     send = functools.partial(lax.ppermute, axis_name="seq")
+    tie = lax.optimization_barrier
     linked = links(seg_ids, place)
 
-    first, second = w_out[: rows // 2], w_out[rows // 2 :]
-    cot_pair = jnp.concatenate([cotangent, send(cotangent, perm=swap_pair)], 0)
-    product = mul(keys, values)
+    half = rows // 2
+    first, second = w_out[:half], w_out[half:]
+    cot_away = send(cotangent, perm=swap_pair)
+    swapped = send(w_out, perm=swap_core)
+    product, cot_away = tie((mul(keys, values), cot_away))
     before = send(product, perm=later)
     data, filt, filtered, gated = forward_filter(linked, before, product, taps, queries)
-    width = 2 * rows
-    gated_away = send(pick(gated, width, 1 - pair), perm=swap_pair)
-    gated_pair = jnp.concatenate([pick(gated, width, pair), gated_away], 0)
+    gated_own = lax.dynamic_index_in_dim(gated, pair, 0, False)
+    gated_away = send(lax.dynamic_index_in_dim(gated, 1 - pair, 0, False), perm=swap_pair)
 
     ready = [max(s, size - s) if s else 0 for s in range(size)]
-    groups_at = {t: [s for s in range(size) if ready[s] == t] for t in range(size)}
     early = max(size - 3, 0)
     stages = {early: [s for s in range(size) if ready[s] <= early]}
     for t in range(early + 1, size):
-        stages[t] = groups_at[t]
+        stages[t] = [s for s in range(size) if ready[s] == t]
+    stages = {t: sets for t, sets in stages.items() if sets}
     block = [ring_place(lax.rem(at - s + size, size), size).astype(jnp.int32) for s in range(size)]
     core = core.astype(jnp.int32)
     core_only = core.reshape(1)
-    firsts, seconds, own, away = [], [], [], []
+    cut = max(size - 3, 1)
+    firsts, seconds, own, away, parts = [], [], [], [], []
     sums = back = None
+    kept = {}
+
+    def projected(steps, sums, last):
+        groups = [firsts[s] + seconds[s] for s in steps]
+        places = [b for s in steps for b in (block[s], block[(size - s) % size])]
+        return project(jnp.stack([core] + places), gated_own, gated_away, groups, sums, last)
+
     for step in range(size):
         if step:
             if step >= 2:
-                first, second, own[step - 2], away[step - 2] = lax.optimization_barrier(
-                    (first, second, own[step - 2], away[step - 2])
-                )
-            if step == 2:
-                first, second, gated = lax.optimization_barrier((first, second, gated))
-            if step - 2 in stages and step - 2 < size - 1:
-                first, second, sums, back = lax.optimization_barrier((first, second, sums, back))
+                first, second, own[step - 2], away[step - 2] = tie((first, second, own[step - 2], away[step - 2]))
+            if step == 3:
+                first, second, gated_away = tie((first, second, gated_away))
+            if step == cut + 1 and sums is not None:
+                first, second, sums = tie((first, second, sums))
+            if step - 2 in stages:
+                first, second, kept[step - 2] = tie((first, second, kept[step - 2]))
             first, second = send(first, perm=onward), send(second, perm=backward)
-        firsts.append((first, send(first, perm=swap_core)))
-        seconds.append((second, send(second, perm=swap_core)))
-        mine, theirs = grad_product(core_only, cot_pair, firsts[step] + seconds[step])
+            firsts.append((first, send(first, perm=swap_core)))
+            seconds.append((second, send(second, perm=swap_core)))
+        else:
+            firsts.append((first, swapped[:half]))
+            seconds.append((second, swapped[half:]))
+        if step == size - 1 and back is not None:
+            firsts[step], seconds[step], back, parts[0] = tie((firsts[step], seconds[step], back, parts[0]))
+        mine, theirs = grad_product(core_only, cotangent, cot_away, firsts[step] + seconds[step])
         own.append(mine)
         away.append(send(theirs, perm=swap_pair))
-        if step in stages and stages[step]:
+        if step == cut - 1:
+            sums = projected(range(cut), None, False)
+        if step == size - 1:
+            sums = projected(range(cut, size), sums, True)
+        if step in stages:
             sets = stages[step]
-            blocks = [block[s] for s in sets]
             mirror = [(size - s) % size for s in sets]
-            groups = [
-                (firsts[s][0], seconds[m][0], firsts[s][1], seconds[m][1]) for s, m in zip(sets, mirror)
-            ]
-            sums = project(
-                jnp.stack([core] + blocks), gated_pair, groups, sums, step == size - 1
-            )
             groups = [(own[s], away[s], own[m], away[m]) for s, m in zip(sets, mirror)]
-            scalars = jnp.stack([pair.astype(jnp.int32), linked.astype(jnp.int32)] + blocks)
+            scalars = jnp.stack([pair.astype(jnp.int32), linked.astype(jnp.int32)] + [block[s] for s in sets])
             back = backward_filter(scalars, groups, queries, filtered, data, filt, back)
-    grad_queries, near, across, taps_part = back
-    ahead = send(across, perm=earlier)
-    taps_grad = scatter_sum(taps_part, nseq, place, (0, 2, 3, 4, 1)).T
+            kept[step] = back[2]
+            parts.append(send(back[2], perm=earlier))
+    grad_queries, near, _, taps_part = back
+    taps_grad = sum_over_ring(taps_part, nseq, place).T
     out_own, out_away = sums
     outputs = (out_own + send(out_away, perm=swap_pair).astype(F32)).astype(BF16)
-    grad_product_ = (near + ahead.astype(F32)).astype(BF16)
-    grad_keys = mul(grad_product_, values)
-    grad_values = mul(grad_product_, keys)
+
+    source = ring_step(jnp.minimum(place + 1, nseq - 1) >> 2, size)
+    stage_of, place_in = np.zeros(size, np.int32), np.zeros((len(stages), size), np.int32)
+    for i, sets in enumerate(stages.values()):
+        for k, s in enumerate(sets):
+            stage_of[s], place_in[i, s] = i, k
+    table = np.concatenate([stage_of[None], place_in], 0)
+    steps = jnp.stack([lax.rem(source - ring_step(jnp.int32(r), size) + size, size) for r in range(size)])
+    scalars = jnp.take(jnp.asarray(table), steps, axis=1).reshape(-1)
+    grad_keys, grad_values = join(scalars, near, keys, values, parts)
     return (outputs, grad_queries, grad_keys, grad_values, taps_grad)
 
 
@@ -431,7 +537,11 @@
     across = jnp.where(linked, back[:length], 0.0).astype(BF16)
     ahead = lax.ppermute(across, "seq", earlier)
     taps_part = inverse_dft(table_now, times_conj(grads, data), scale)
-    taps_grad = scatter_sum(taps_part, nseq, place, (0, 2, 3, 4, 1)).T
+    if nseq & (nseq - 1):
+        taps_grad = lax.psum_scatter(taps_part.T, "seq", scatter_dimension=0, tiled=True)
+    else:
+        blocks = taps_part.reshape(length, nseq, -1).transpose(1, 0, 2)
+        taps_grad = scatter_sum(blocks, nseq, place).T
     grad_product = (back[length:] + ahead.astype(F32)).astype(BF16)
     grad_keys = mul(grad_product, values)
     grad_values = mul(grad_product, keys)

time: 307 us -> 300 us (0.977)
  the two profiles are of different devices: /device:TPU:0 before, /device:TPU:1 now
where the time goes in v4:
time: 300 us; the launch traced here: 298 us
  waiting for transfers between devices  95.2 us (32%)
  Pallas kernels  70.5 us (24%)
  local copies, waits for them, and re-layouts  63.8 us (21%)
  starting transfers between devices  57.5 us (19%)
  other arithmetic  8.1 us (3%)
    unnamed x197, local copies, waits for them, and re-layouts  55.6 us
    ppermute x14, waiting for transfers between devices, on_ring(): first, second = (send(first, perm=onward), send(second, perm=backward))  39.2 us
    pallas_call x8, Pallas kernels, grad_product(): pl.pallas_call(grad_kernel, out_shape=(out, out), grid_spec=pltpu.Prefetc...  27.3 us
    ppermute x3, waiting for transfers between devices, on_ring(): parts.append(send(back[2], perm=earlier))  20.5 us
    ppermute x1, waiting for transfers between devices, on_ring(): cot_away = send(cotangent, perm=swap_pair)  17.4 us
    pallas_call x3, Pallas kernels, backward_filter(): pl.pallas_call(functools.partial(backward_kernel, count), out_shape=(jax....  15.1 us
    ppermute x8, waiting for transfers between devices, on_ring(): away.append(send(theirs, perm=swap_pair))  14.6 us
    pallas_call x2, Pallas kernels, project(): pl.pallas_call(functools.partial(project_kernel, len(groups), before is N...  13.6 us
  transfers between devices with their start and end apart: 49, of which 18 were waited for; matrix products, arithmetic and copies ran while one was open for 4% of the time, Pallas kernels for 18%

profile of v4, /device:TPU:1, one launch (start us, length us, event | category | flops | bytes accessed | tf_op | source)
XLA Modules:
  0.0 298.0 jit_solution(635508726969013993)
XLA Ops:
  9.7 17.4 %collective-permute-done.cot_away = bf16[128,4096]{1,0:T(8,128)(2,1)S(1)} collective-permute-done((bf16[128,4096]{1,0:T(8,128)(2,1)}, bf16[128,4096]{1,0:T(8,128)(2,1)S(1)}, u32[]{:S(2)}, u32[]{:S(2)}) %collective-permute-start) | collective-permute-done | bytes 1048608 | tf_op jit(solution)/shard_map/ppermute | solution.py:434
  27.1 3.9 %collective-permute-start.1 = (bf16[128,4096]{1,0:T(8,128)(2,1)}, bf16[128,4096]{1,0:T(8,128)(2,1)}, u32[]{:S(2)}, u32[]{:S(2)}) collective-permute-start(bf16[128,4096]{1,0:T(8,128)(2,1)} %multiply_convert_fusion.product), channel_id=1, source_target_pairs={{0,1},{1,2},{2,3},{3,4},{4,5},{5,6},{6,7},{7,8},{8,9},{9,10},{10,1... | collective-permute-start | bytes 3145736 | tf_op jit(solution)/shard_map/ppermute | solution.py:437
  32.4 4.3 %shard_map.264 = (bf16[128,256]{1,0:T(8,128)(2,1)S(1)}, bf16[128,256]{1,0:T(8,128)(2,1)}) custom-call(s32[1]{0:T(128)} %bitcast.scalars, bf16[128,4096]{1,0:T(8,128)(2,1)S(1)} %copy-done, bf16[128,4096]{1,0:T(8,128)(2,1)S(1)} %collective-permute-done.cot_away, bf16[64,4096]{1,0:T(8,128)(2,1)} %get-tuple-element.168.first.refs_0_, ...), custom_call_target="tpu_custom_call" | custom-call | flops 536870912 | bytes 4194304 | tf_op jit(solution)/shard_map/pallas_call | solution.py:212
  41.0 5.3 %collective-permute-done.5.refs_1_.refs_3_ = bf16[128,256]{1,0:T(8,128)(2,1)} collective-permute-done((bf16[128,256]{1,0:T(8,128)(2,1)}, bf16[128,256]{1,0:T(8,128)(2,1)}, u32[]{:S(2)}, u32[]{:S(2)}) %collective-permute-start.5) | collective-permute-done | bytes 65568 | tf_op jit(solution)/shard_map/ppermute | solution.py:481
  49.9 8.4 %shard_map.263 = (f32[256,4096]{1,0:T(8,128)S(1)}, f32[256,4096]{1,0:T(8,128)S(1)}, bf16[128,4096]{1,0:T(8,128)(2,1)S(1)}, bf16[2,128,2048]{2,1,0:T(8,128)(2,1)S(1)}) custom-call(s32[1]{0:T(128)} %bitcast.8.linked_ref, bf16[256,256]{1,0:T(8,128)(2,1)S(1)} %copy-done.66, bf16[256,256]{1,0:T(8,128)(2,1)S(1)} %copy-done.65, bf16[256,256]{1,0:T(8,128)(2,1)S(1)} %copy-done.64, ...), custom_call_target="tpu_custom_call" | custom-call | flops 1610612736 | bytes 14680064 | tf_op jit(solution)/shard_map/pallas_call | solution.py:164
  61.6 3.6 %shard_map.265 = (bf16[128,256]{1,0:T(8,128)(2,1)S(1)}, bf16[128,256]{1,0:T(8,128)(2,1)S(1)}) custom-call(s32[1]{0:T(128)} %bitcast.scalars, bf16[128,4096]{1,0:T(8,128)(2,1)S(1)} %copy-done, bf16[128,4096]{1,0:T(8,128)(2,1)S(1)} %collective-permute-done.cot_away, bf16[64,4096]{1,0:T(8,128)(2,1)} %collective-permute-done.2.first.refs_4_, ...), custom_call_target="tpu_custom_call" | custom-call | flops 536870912 | bytes 4194304 | tf_op jit(solution)/shard_map/pallas_call | solution.py:212
  67.5 6.1 %collective-permute-done.10.refs_1_.refs_7_ = bf16[128,256]{1,0:T(8,128)(2,1)S(1)} collective-permute-done((bf16[128,256]{1,0:T(8,128)(2,1)S(1)}, bf16[128,256]{1,0:T(8,128)(2,1)S(1)}, u32[]{:S(2)}, u32[]{:S(2)}) %collective-permute-start.10) | collective-permute-done | bytes 65568 | tf_op jit(solution)/shard_map/ppermute | solution.py:481
  80.1 8.7 %collective-permute-done.12.first.refs_12_ = bf16[64,4096]{1,0:T(8,128)(2,1)S(1)} collective-permute-done((bf16[64,4096]{1,0:T(8,128)(2,1)S(1)}, bf16[64,4096]{1,0:T(8,128)(2,1)S(1)}, u32[]{:S(2)}, u32[]{:S(2)}) %collective-permute-start.12) | collective-permute-done | bytes 524320 | tf_op jit(solution)/shard_map/ppermute | solution.py:471
  96.5 8.7 %collective-permute-done.17.first.refs_16_ = bf16[64,4096]{1,0:T(8,128)(2,1)} collective-permute-done((bf16[64,4096]{1,0:T(8,128)(2,1)S(1)}, bf16[64,4096]{1,0:T(8,128)(2,1)}, u32[]{:S(2)}, u32[]{:S(2)}) %collective-permute-start.17) | collective-permute-done | bytes 524320 | tf_op jit(solution)/shard_map/ppermute | solution.py:471
  109.9 3.6 %shard_map.268 = (bf16[128,256]{1,0:T(8,128)(2,1)S(1)}, bf16[128,256]{1,0:T(8,128)(2,1)S(1)}) custom-call(s32[1]{0:T(128)} %bitcast.scalars, bf16[128,4096]{1,0:T(8,128)(2,1)S(1)} %copy-done, bf16[128,4096]{1,0:T(8,128)(2,1)S(1)} %collective-permute-done.cot_away, bf16[64,4096]{1,0:T(8,128)(2,1)} %collective-permute-done.17.first.refs_16_, ...), custom_call_target="tpu_custom_call" | custom-call | flops 536870912 | bytes 4194304 | tf_op jit(solution)/shard_map/pallas_call | solution.py:212
  115.0 7.2 %collective-permute-done.22.first.refs_0_ = bf16[64,4096]{1,0:T(8,128)(2,1)} collective-permute-done((bf16[64,4096]{1,0:T(8,128)(2,1)}, bf16[64,4096]{1,0:T(8,128)(2,1)}, u32[]{:S(2)}, u32[]{:S(2)}) %collective-permute-start.22) | collective-permute-done | bytes 524320 | tf_op jit(solution)/shard_map/ppermute | solution.py:471
  130.7 6.9 %shard_map.269.refs_12_ = f32[256,4096]{1,0:T(8,128)S(1)} custom-call(s32[11]{0:T(128)S(1)} %stack.122.scalars, bf16[128,2048]{1,0:T(8,128)(2,1)S(1)} %copy-done.25, bf16[128,2048]{1,0:T(8,128)(2,1)S(1)} %copy-done.35, bf16[64,4096]{1,0:T(8,128)(2,1)} %get-tuple-element.168.first.refs_0_, bf16[64,4096]{1,0:T(8,128)(2,1)S(1)} %copy-done.30, ...), custom_call_target="tpu_custom_call" | custom-call | flops 2684354560 | bytes 15728640 | tf_op jit(solution)/shard_map/pallas_call | solution.py:281
  139.8 3.8 %shard_map.270 = (bf16[128,256]{1,0:T(8,128)(2,1)S(1)}, bf16[128,256]{1,0:T(8,128)(2,1)}) custom-call(s32[1]{0:T(128)} %bitcast.scalars, bf16[128,4096]{1,0:T(8,128)(2,1)S(1)} %copy-done, bf16[128,4096]{1,0:T(8,128)(2,1)S(1)} %collective-permute-done.cot_away, bf16[64,4096]{1,0:T(8,128)(2,1)} %collective-permute-done.22.first.refs_0_, ...), custom_call_target="tpu_custom_call" | custom-call | flops 536870912 | bytes 4194304 | tf_op jit(solution)/shard_map/pallas_call | solution.py:212
  146.7 5.6 %collective-permute-done.29.first.refs_4_ = bf16[64,4096]{1,0:T(8,128)(2,1)} collective-permute-done((bf16[64,4096]{1,0:T(8,128)(2,1)}, bf16[64,4096]{1,0:T(8,128)(2,1)}, u32[]{:S(2)}, u32[]{:S(2)}) %collective-permute-start.29) | collective-permute-done | bytes 524320 | tf_op jit(solution)/shard_map/ppermute | solution.py:471
  164.1 7.6 %shard_map.271 = (bf16[128,4096]{1,0:T(8,128)(2,1)}, f32[128,4096]{1,0:T(8,128)S(1)}, bf16[4,128,512]{2,1,0:T(8,128)(2,1)}, f32[4,8,128,128]{3,2,1,0:T(8,128)S(1)}) custom-call(s32[6]{0:T(128)S(1)} %stack.124.scalars, bf16[256,256]{1,0:T(8,128)(2,1)S(1)} %copy-done.67, bf16[256,256]{1,0:T(8,128)(2,1)S(1)} %copy-done.65, bf16[256,256]{1,0:T(8,128)(2,1)S(1)} %copy-done.64, ...), custom_call_target="tpu_custom_call" | custom-call | flops 939524096 | bytes 8912896 | tf_op jit(solution)/shard_map/pallas_call | solution.py:348
  179.9 7.2 %collective-permute-done.34.refs_8_.first = bf16[64,4096]{1,0:T(8,128)(2,1)} collective-permute-done((bf16[64,4096]{1,0:T(8,128)(2,1)}, bf16[64,4096]{1,0:T(8,128)(2,1)}, u32[]{:S(2)}, u32[]{:S(2)}) %collective-permute-start.34) | collective-permute-done | bytes 524320 | tf_op jit(solution)/shard_map/ppermute | solution.py:471
  189.3 3.6 %shard_map.272 = (bf16[128,256]{1,0:T(8,128)(2,1)S(1)}, bf16[128,256]{1,0:T(8,128)(2,1)S(1)}) custom-call(s32[1]{0:T(128)} %bitcast.scalars, bf16[128,4096]{1,0:T(8,128)(2,1)S(1)} %copy-done, bf16[128,4096]{1,0:T(8,128)(2,1)S(1)} %collective-permute-done.cot_away, bf16[64,4096]{1,0:T(8,128)(2,1)} %collective-permute-done.29.first.refs_4_, ...), custom_call_target="tpu_custom_call" | custom-call | flops 536870912 | bytes 4194304 | tf_op jit(solution)/shard_map/pallas_call | solution.py:212
  192.9 5.9 %collective-permute-start.38 = (bf16[128,256]{1,0:T(8,128)(2,1)S(1)}, bf16[128,256]{1,0:T(8,128)(2,1)S(1)}, u32[]{:S(2)}, u32[]{:S(2)}) collective-permute-start(bf16[128,256]{1,0:T(8,128)(2,1)S(1)} %get-tuple-element.124), channel_id=1, source_target_pairs={{0,2},{1,3},{2,0},{3,1},{4,6},{5,7},{6,4},{7,5},{8,10},{9,11},{10,... | collective-permute-start | bytes 196616 | tf_op jit(solution)/shard_map/ppermute | solution.py:481
  209.7 3.6 %shard_map.273 = (bf16[128,4096]{1,0:T(8,128)(2,1)}, f32[128,4096]{1,0:T(8,128)S(1)}, bf16[2,128,512]{2,1,0:T(8,128)(2,1)S(1)}, f32[4,8,128,128]{3,2,1,0:T(8,128)S(1)}) custom-call(s32[4]{0:T(128)S(1)} %pad_add_fusion.scalars, bf16[256,256]{1,0:T(8,128)(2,1)S(1)} %copy-done.68, ...), custom_call_target="tpu_custom_call", output_to_operand_aliasing={{0}: (17, {}), {1}: (18, {}), {3}: (19, {})} | custom-call | flops 469762048 | bytes 4456448 | tf_op jit(solution)/shard_map/pallas_call | solution.py:348
  214.1 4.6 %shard_map.275 = (bf16[128,256]{1,0:T(8,128)(2,1)S(1)}, bf16[128,256]{1,0:T(8,128)(2,1)S(1)}) custom-call(s32[1]{0:T(128)} %bitcast.scalars, bf16[128,4096]{1,0:T(8,128)(2,1)S(1)} %copy-done, bf16[128,4096]{1,0:T(8,128)(2,1)S(1)} %collective-permute-done.cot_away, bf16[64,4096]{1,0:T(8,128)(2,1)} %collective-permute-done.34.refs_8_.first, ...), custom_call_target="tpu_custom_call" | custom-call | flops 536870912 | bytes 4194304 | tf_op jit(solution)/shard_map/pallas_call | solution.py:212
  225.1 3.9 %shard_map.276 = (bf16[128,4096]{1,0:T(8,128)(2,1)}, f32[128,4096]{1,0:T(8,128)S(1)}, bf16[2,128,512]{2,1,0:T(8,128)(2,1)}, f32[4,8,128,128]{3,2,1,0:T(8,128)S(1)}) custom-call(s32[4]{0:T(128)S(1)} %pad_add_fusion.2.scalars, bf16[256,256]{1,0:T(8,128)(2,1)S(1)} %copy-done.68, ...), custom_call_target="tpu_custom_call", output_to_operand_aliasing={{0}: (17, {}), {1}: (18, {}), {3}: (19, {})} | custom-call | flops 469762048 | bytes 4456448 | tf_op jit(solution)/shard_map/pallas_call | solution.py:348
  246.0 6.7 %shard_map.274 = (f32[128,4096]{1,0:T(8,128)S(1)}, bf16[128,4096]{1,0:T(8,128)(2,1)}) custom-call(s32[7]{0:T(128)S(1)} %stack.119.scalars, bf16[128,2048]{1,0:T(8,128)(2,1)S(1)} %copy-done.26, bf16[128,2048]{1,0:T(8,128)(2,1)S(1)} %copy-done.36, bf16[64,4096]{1,0:T(8,128)(2,1)} %collective-permute-done.22.first.refs_0_, bf16[64,4096]{1,0:T(8,128)(2,1)S(1)} %copy-done.38, ...), custom_call_target="tpu_custom_call" | custom-call | flops 1610612736 | bytes 11534336 | tf_op jit(solution)/shard_map/pallas_call | solution.py:281
  264.4 17.6 %collective-permute-done.42.refs_1_ = bf16[2,128,512]{2,1,0:T(8,128)(2,1)S(1)} collective-permute-done((bf16[2,128,512]{2,1,0:T(8,128)(2,1)S(1)}, bf16[2,128,512]{2,1,0:T(8,128)(2,1)S(1)}, u32[]{:S(2)}, u32[]{:S(2)}) %collective-permute-start.42) | collective-permute-done | bytes 262176 | tf_op jit(solution)/shard_map/ppermute | solution.py:493
  287.3 6.2 %shard_map.277 = (bf16[128,4096]{1,0:T(8,128)(2,1)}, bf16[128,4096]{1,0:T(8,128)(2,1)}) custom-call(s32[32]{0:T(128)S(1)} %select_n.130.scalars, f32[128,4096]{1,0:T(8,128)S(1)} %copy-done.17, bf16[128,4096]{1,0:T(8,128)(2,1)S(1)} %copy-done.33, bf16[128,4096]{1,0:T(8,128)(2,1)S(1)} %copy-done.32, bf16[4,128,512]{2,1,0:T(8,128)(2,1)} %collective-permute-done.39.refs_0_, ...), custom_call_target="tpu_custom_call" | custom-call | flops 2097152 | bytes 7340032 | tf_op jit(solution)/shard_map/pallas_call | solution.py:400
  (316 shorter events, 134.8 us)
Async XLA Ops:
  0.6 30.4 %collective-permute-start.4 = (bf16[128,4096]{1,0:T(8,128)(2,1)}, bf16[128,4096]{1,0:T(8,128)(2,1)}, u32[]{:S(2)}, u32[]{:S(2)}) collective-permute-start(bf16[128,4096]{1,0:T(8,128)(2,1)} %param.27), channel_id=1, source_target_pairs={{0,1},{1,0},{2,3},{3,2},{4,5},{5,4},{6,7},{7,6},{8,9},{9,8},{10,11... | collective-permute-start | bytes 3145736 | tf_op jit(solution)/shard_map/ppermute | solution.py:435
  0.8 26.3 %collective-permute-start = (bf16[128,4096]{1,0:T(8,128)(2,1)}, bf16[128,4096]{1,0:T(8,128)(2,1)S(1)}, u32[]{:S(2)}, u32[]{:S(2)}) collective-permute-start(bf16[128,4096]{1,0:T(8,128)(2,1)} %cot_own.15), channel_id=1, source_target_pairs={{0,2},{1,3},{2,0},{3,1},{4,6},{5,7},{6,4},{7,5},{8,10},{9,11},{10,... | collective-permute-start | bytes 3145736 | tf_op jit(solution)/shard_map/ppermute | solution.py:434
  5.7 34.7 %collective-permute-start.3 = (bf16[64,4096]{1,0:T(8,128)(2,1)}, bf16[64,4096]{1,0:T(8,128)(2,1)}, u32[]{:S(2)}, u32[]{:S(2)}) collective-permute-start(bf16[64,4096]{1,0:T(8,128)(2,1)} %get-tuple-element.167.second.refs_2_), channel_id=1, source_target_pairs={{8,0},{9,1},{10,2},{11,3},{16,8},{17,9},{18,10},{19,11},{24,16},{2... | collective-permute-start | bytes 1572872 | tf_op jit(solution)/shard_map/ppermute | solution.py:471
  6.9 33.5 %collective-permute-start.2 = (bf16[64,4096]{1,0:T(8,128)(2,1)}, bf16[64,4096]{1,0:T(8,128)(2,1)}, u32[]{:S(2)}, u32[]{:S(2)}) collective-permute-start(bf16[64,4096]{1,0:T(8,128)(2,1)} %get-tuple-element.168.first.refs_0_), channel_id=1, source_target_pairs={{0,8},{1,9},{2,10},{3,11},{8,16},{9,17},{10,18},{11,19},{16,24},{1... | collective-permute-start | bytes 1572872 | tf_op jit(solution)/shard_map/ppermute | solution.py:471
  27.1 20.7 %collective-permute-start.1 = (bf16[128,4096]{1,0:T(8,128)(2,1)}, bf16[128,4096]{1,0:T(8,128)(2,1)}, u32[]{:S(2)}, u32[]{:S(2)}) collective-permute-start(bf16[128,4096]{1,0:T(8,128)(2,1)} %multiply_convert_fusion.product), channel_id=1, source_target_pairs={{0,1},{1,2},{2,3},{3,4},{4,5},{5,6},{6,7},{7,8},{8,9},{9,10},{10,1... | collective-permute-start | bytes 3145736 | tf_op jit(solution)/shard_map/ppermute | solution.py:437
  40.4 21.1 %collective-permute-start.9 = (bf16[64,4096]{1,0:T(8,128)(2,1)}, bf16[64,4096]{1,0:T(8,128)(2,1)S(1)}, u32[]{:S(2)}, u32[]{:S(2)}) collective-permute-start(bf16[64,4096]{1,0:T(8,128)(2,1)} %collective-permute-done.3.second.refs_6_), channel_id=1, source_target_pairs={{0,1},{1,0},{2,3},{3,2},{4,5},{5,4},{6,7},{7,6},{8,9},{9,8},{10,11... | collective-permute-start | bytes 1572872 | tf_op jit(solution)/shard_map/ppermute | solution.py:473
  40.5 21.0 %collective-permute-start.8 = (bf16[64,4096]{1,0:T(8,128)(2,1)}, bf16[64,4096]{1,0:T(8,128)(2,1)S(1)}, u32[]{:S(2)}, u32[]{:S(2)}) collective-permute-start(bf16[64,4096]{1,0:T(8,128)(2,1)} %collective-permute-done.2.first.refs_4_), channel_id=1, source_target_pairs={{0,1},{1,0},{2,3},{3,2},{4,5},{5,4},{6,7},{7,6},{8,9},{9,8},{10,11... | collective-permute-start | bytes 1572872 | tf_op jit(solution)/shard_map/ppermute | solution.py:472
  46.3 20.7 %collective-permute-start.6 = (bf16[64,4096]{1,0:T(8,128)(2,1)}, bf16[64,4096]{1,0:T(8,128)(2,1)S(1)}, u32[]{:S(2)}, u32[]{:S(2)}) collective-permute-start(bf16[64,4096]{1,0:T(8,128)(2,1)} %collective-permute-done.2.first.refs_4_), channel_id=1, source_target_pairs={{0,8},{1,9},{2,10},{3,11},{8,16},{9,17},{10,18},{11,19},{16,24},{1... | collective-permute-start | bytes 1572872 | tf_op jit(solution)/shard_map/ppermute | solution.py:471
  47.6 19.4 %collective-permute-start.7 = (bf16[64,4096]{1,0:T(8,128)(2,1)}, bf16[64,4096]{1,0:T(8,128)(2,1)S(1)}, u32[]{:S(2)}, u32[]{:S(2)}) collective-permute-start(bf16[64,4096]{1,0:T(8,128)(2,1)} %collective-permute-done.3.second.refs_6_), channel_id=1, source_target_pairs={{8,0},{9,1},{10,2},{11,3},{16,8},{17,9},{18,10},{19,11},{24,16},{2... | collective-permute-start | bytes 1572872 | tf_op jit(solution)/shard_map/ppermute | solution.py:471
  74.3 14.6 %collective-permute-start.12 = (bf16[64,4096]{1,0:T(8,128)(2,1)S(1)}, bf16[64,4096]{1,0:T(8,128)(2,1)S(1)}, u32[]{:S(2)}, u32[]{:S(2)}) collective-permute-start(bf16[64,4096]{1,0:T(8,128)(2,1)S(1)} %collective-permute-done.6.first.refs_8_), channel_id=1, source_target_pairs={{0,8},{1,9},{2,10},{3,11},{8,16},{9,17},{10,18},{11,19},{16,24},{1... | collective-permute-start | bytes 1572872 | tf_op jit(solution)/shard_map/ppermute | solution.py:471
  108.3 13.9 %collective-permute-start.22 = (bf16[64,4096]{1,0:T(8,128)(2,1)}, bf16[64,4096]{1,0:T(8,128)(2,1)}, u32[]{:S(2)}, u32[]{:S(2)}) collective-permute-start(bf16[64,4096]{1,0:T(8,128)(2,1)} %collective-permute-done.17.first.refs_16_), channel_id=1, source_target_pairs={{0,8},{1,9},{2,10},{3,11},{8,16},{9,17},{10,18},{11,19},{16,24},{1... | collective-permute-start | bytes 1572872 | tf_op jit(solution)/shard_map/ppermute | solution.py:471
  114.2 23.4 %collective-permute-start.28 = (bf16[128,256]{1,0:T(8,128)(2,1)S(1)}, bf16[128,256]{1,0:T(8,128)(2,1)S(1)}, u32[]{:S(2)}, u32[]{:S(2)}) collective-permute-start(bf16[128,256]{1,0:T(8,128)(2,1)S(1)} %get-tuple-element.102), channel_id=1, source_target_pairs={{0,2},{1,3},{2,0},{3,1},{4,6},{5,7},{6,4},{7,5},{8,10},{9,11},{10,... | collective-permute-start | bytes 196616 | tf_op jit(solution)/shard_map/ppermute | solution.py:481
  122.1 17.6 %collective-permute-start.23 = (bf16[64,4096]{1,0:T(8,128)(2,1)}, bf16[64,4096]{1,0:T(8,128)(2,1)S(1)}, u32[]{:S(2)}, u32[]{:S(2)}) collective-permute-start(bf16[64,4096]{1,0:T(8,128)(2,1)} %collective-permute-done.22.first.refs_0_), channel_id=1, source_target_pairs={{0,1},{1,0},{2,3},{3,2},{4,5},{5,4},{6,7},{7,6},{8,9},{9,8},{10,11... | collective-permute-start | bytes 1572872 | tf_op jit(solution)/shard_map/ppermute | solution.py:472
  123.3 16.5 %collective-permute-start.25 = (bf16[64,4096]{1,0:T(8,128)(2,1)}, bf16[64,4096]{1,0:T(8,128)(2,1)S(1)}, u32[]{:S(2)}, u32[]{:S(2)}) collective-permute-start(bf16[64,4096]{1,0:T(8,128)(2,1)} %collective-permute-done.24.second.refs_2_), channel_id=1, source_target_pairs={{0,1},{1,0},{2,3},{3,2},{4,5},{5,4},{6,7},{7,6},{8,9},{9,8},{10,11... | collective-permute-start | bytes 1572872 | tf_op jit(solution)/shard_map/ppermute | solution.py:473
  138.3 14.0 %collective-permute-start.29 = (bf16[64,4096]{1,0:T(8,128)(2,1)}, bf16[64,4096]{1,0:T(8,128)(2,1)}, u32[]{:S(2)}, u32[]{:S(2)}) collective-permute-start(bf16[64,4096]{1,0:T(8,128)(2,1)} %collective-permute-done.22.first.refs_0_), channel_id=1, source_target_pairs={{0,8},{1,9},{2,10},{3,11},{8,16},{9,17},{10,18},{11,19},{16,24},{1... | collective-permute-start | bytes 1572872 | tf_op jit(solution)/shard_map/ppermute | solution.py:471
  174.6 14.3 %collective-permute-start.36 = (bf16[64,4096]{1,0:T(8,128)(2,1)}, bf16[64,4096]{1,0:T(8,128)(2,1)}, u32[]{:S(2)}, u32[]{:S(2)}) collective-permute-start(bf16[64,4096]{1,0:T(8,128)(2,1)} %collective-permute-done.31.second.refs_6_), channel_id=1, source_target_pairs={{8,0},{9,1},{10,2},{11,3},{16,8},{17,9},{18,10},{19,11},{24,16},{2... | collective-permute-start | bytes 1572872 | tf_op jit(solution)/shard_map/ppermute | solution.py:471
  177.3 36.7 %collective-permute-start.39 = (bf16[4,128,512]{2,1,0:T(8,128)(2,1)}, bf16[4,128,512]{2,1,0:T(8,128)(2,1)}, u32[]{:S(2)}, u32[]{:S(2)}) collective-permute-start(bf16[4,128,512]{2,1,0:T(8,128)(2,1)} %get-tuple-element.118), channel_id=1, source_target_pairs={{1,0},{2,1},{3,2},{4,3},{5,4},{6,5},{7,6},{8,7},{9,8},{10,9},{11,1... | collective-permute-start | bytes 1572872 | tf_op jit(solution)/shard_map/ppermute | solution.py:493
  187.1 26.9 %collective-permute-start.35 = (bf16[64,4096]{1,0:T(8,128)(2,1)}, bf16[64,4096]{1,0:T(8,128)(2,1)}, u32[]{:S(2)}, u32[]{:S(2)}) collective-permute-start(bf16[64,4096]{1,0:T(8,128)(2,1)} %collective-permute-done.34.refs_8_.first), channel_id=1, source_target_pairs={{0,1},{1,0},{2,3},{3,2},{4,5},{5,4},{6,7},{7,6},{8,9},{9,8},{10,11... | collective-permute-start | bytes 1572872 | tf_op jit(solution)/shard_map/ppermute | solution.py:472
  189.0 25.0 %collective-permute-start.37 = (bf16[64,4096]{1,0:T(8,128)(2,1)}, bf16[64,4096]{1,0:T(8,128)(2,1)}, u32[]{:S(2)}, u32[]{:S(2)}) collective-permute-start(bf16[64,4096]{1,0:T(8,128)(2,1)} %collective-permute-done.36.refs_10_.second), channel_id=1, source_target_pairs={{0,1},{1,0},{2,3},{3,2},{4,5},{5,4},{6,7},{7,6},{8,9},{9,8},{10,11... | collective-permute-start | bytes 1572872 | tf_op jit(solution)/shard_map/ppermute | solution.py:473
  239.3 14.8 %collective-permute-start.45 = (bf16[1,8,128,128]{3,2,1,0:T(8,128)(2,1)}, bf16[1,8,128,128]{3,2,1,0:T(8,128)(2,1)}, u32[]{:S(2)}, u32[]{:S(2)}) collective-permute-start(bf16[1,8,128,128]{3,2,1,0:T(8,128)(2,1)} %dynamic-slice_convert_fusion), channel_id=1, source_target_pairs={{0,2},{1,3},{2,0},{3,1},{4,6},{5,7},{6,4},{7,5},{8,10},{9,11},{10,... | collective-permute-start | bytes 786440 | tf_op jit(solution)/shard_map/ppermute | solution.py:74
  254.1 39.5 %collective-permute-start.40 = (bf16[128,4096]{1,0:T(8,128)(2,1)}, bf16[128,4096]{1,0:T(8,128)(2,1)}, u32[]{:S(2)}, u32[]{:S(2)}) collective-permute-start(bf16[128,4096]{1,0:T(8,128)(2,1)} %get-tuple-element.138), channel_id=1, source_target_pairs={{0,2},{1,3},{2,0},{3,1},{4,6},{5,7},{6,4},{7,5},{8,10},{9,11},{10,... | collective-permute-start | bytes 3145736 | tf_op jit(solution)/shard_map/ppermute | solution.py:497
  255.4 26.6 %collective-permute-start.42 = (bf16[2,128,512]{2,1,0:T(8,128)(2,1)S(1)}, bf16[2,128,512]{2,1,0:T(8,128)(2,1)S(1)}, u32[]{:S(2)}, u32[]{:S(2)}) collective-permute-start(bf16[2,128,512]{2,1,0:T(8,128)(2,1)S(1)} %copy-done.91), channel_id=1, source_target_pairs={{1,0},{2,1},{3,2},{4,3},{5,4},{6,5},{7,6},{8,7},{9,8},{10,9},{11,1... | collective-permute-start | bytes 786440 | tf_op jit(solution)/shard_map/ppermute | solution.py:493
  258.0 26.8 %collective-permute-start.43 = (bf16[2,128,512]{2,1,0:T(8,128)(2,1)}, bf16[2,128,512]{2,1,0:T(8,128)(2,1)S(1)}, u32[]{:S(2)}, u32[]{:S(2)}) collective-permute-start(bf16[2,128,512]{2,1,0:T(8,128)(2,1)} %get-tuple-element.149), channel_id=1, source_target_pairs={{1,0},{2,1},{3,2},{4,3},{5,4},{6,5},{7,6},{8,7},{9,8},{10,9},{11,1... | collective-permute-start | bytes 786440 | tf_op jit(solution)/shard_map/ppermute | solution.py:493
  260.7 32.8 %collective-permute-start.47 = (bf16[2,128,128]{2,1,0:T(8,128)(2,1)S(1)}, bf16[2,128,128]{2,1,0:T(8,128)(2,1)S(1)}, u32[]{:S(2)}, u32[]{:S(2)}) collective-permute-start(bf16[2,128,128]{2,1,0:T(8,128)(2,1)S(1)} %fusion.1), channel_id=1, source_target_pairs={{0,8},{1,9},{2,10},{3,11},{4,12},{5,13},{6,14},{7,15},{8,0},{9,1},... | collective-permute-start | bytes 196616 | tf_op jit(solution)/shard_map/ppermute | solution.py:74
  (123 other events, 741.0 us)

commit v5 on v4

--- a/solution.py
+++ b/solution.py
@@ -76,11 +76,6 @@
 
     part = halve(part.reshape(2, 2, size, lags, chans), 1, core, F32)
     part = halve(part.reshape(1, 2, size, lags, chans), 2, pair, BF16).reshape(size, lags, chans)
-    if size & (size - 1):
-        return lax.psum_scatter(
-            part, "seq", scatter_dimension=0,
-            axis_index_groups=[[4 * r + k for r in range(size)] for k in range(4)],
-        )
     left = size
     while left > 1:
         bit = size // left
@@ -169,7 +164,7 @@
         + [fixed] * 4
         + [block, block, pl.BlockSpec((width, length), lambda j: (j, 0)), block],
         out_specs=(spectrum, spectrum, block, pl.BlockSpec((2, length, width // 2), lambda j: (0, 0, j))),
-        compiler_params=pltpu.CompilerParams(vmem_limit_bytes=12 << 20),
+        compiler_params=pltpu.CompilerParams(vmem_limit_bytes=56 << 20),
         cost_estimate=pl.CostEstimate(
             flops=24 * length * length * chans, bytes_accessed=28 * length * chans, transcendentals=0
         ),
@@ -220,7 +215,7 @@
             out_specs=(whole, whole),
             scratch_shapes=[pltpu.VMEM((tokens, 4 * depth), F32)],
         ),
-        compiler_params=pltpu.CompilerParams(vmem_limit_bytes=8 << 20),
+        compiler_params=pltpu.CompilerParams(vmem_limit_bytes=56 << 20),
         cost_estimate=pl.CostEstimate(
             flops=8 * tokens * depth * feats, bytes_accessed=(2 * tokens + 8 * depth) * feats, transcendentals=0
         ),
@@ -293,7 +288,7 @@
                 pltpu.VMEM((2 * rows, tile), F32),
             ],
         ),
-        compiler_params=pltpu.CompilerParams(vmem_limit_bytes=16 << 20),
+        compiler_params=pltpu.CompilerParams(vmem_limit_bytes=56 << 20),
         cost_estimate=pl.CostEstimate(
             flops=4 * rows * depth * len(weights) * feats,
             bytes_accessed=2 * depth * feats * len(weights) + 4 * rows * chans + 8 * rows * feats,
@@ -369,7 +364,7 @@
             scratch_shapes=[pltpu.VMEM((length, width), BF16)],
         ),
         input_output_aliases={inputs + i: out for i, out in zip(range(len(before)), (0, 1, 3))},
-        compiler_params=pltpu.CompilerParams(vmem_limit_bytes=16 << 20),
+        compiler_params=pltpu.CompilerParams(vmem_limit_bytes=56 << 20),
         cost_estimate=pl.CostEstimate(
             flops=28 * length * length * width * count, bytes_accessed=34 * length * width * count, transcendentals=0
         ),
@@ -406,7 +401,7 @@
             in_specs=[block] * 3 + [pl.BlockSpec((1, length, width), place(i)) for i in range(len(parts))],
             out_specs=(block, block),
         ),
-        compiler_params=pltpu.CompilerParams(vmem_limit_bytes=6 << 20),
+        compiler_params=pltpu.CompilerParams(vmem_limit_bytes=56 << 20),
         cost_estimate=pl.CostEstimate(flops=4 * length * chans, bytes_accessed=14 * length * chans, transcendentals=0),
     )(scalars, near, keys, values, *parts)
 
@@ -435,12 +430,9 @@
     swapped = send(w_out, perm=swap_core)
     product, cot_away = tie((mul(keys, values), cot_away))
     before = send(product, perm=later)
-    data, filt, filtered, gated = forward_filter(linked, before, product, taps, queries)
-    gated_own = lax.dynamic_index_in_dim(gated, pair, 0, False)
-    gated_away = send(lax.dynamic_index_in_dim(gated, 1 - pair, 0, False), perm=swap_pair)
 
     ready = [max(s, size - s) if s else 0 for s in range(size)]
-    early = max(size - 3, 0)
+    early = max(size - 3, 1)
     stages = {early: [s for s in range(size) if ready[s] <= early]}
     for t in range(early + 1, size):
         stages[t] = [s for s in range(size) if ready[s] == t]
@@ -460,10 +452,9 @@
 
     for step in range(size):
         if step:
-            if step >= 2:
-                first, second, own[step - 2], away[step - 2] = tie((first, second, own[step - 2], away[step - 2]))
-            if step == 3:
-                first, second, gated_away = tie((first, second, gated_away))
+            if step >= 3:
+                for s in (0, 1) if step == 3 else (step - 2,):
+                    first, second, own[s], away[s] = tie((first, second, own[s], away[s]))
             if step == cut + 1 and sums is not None:
                 first, second, sums = tie((first, second, sums))
             if step - 2 in stages:
@@ -471,18 +462,30 @@
             first, second = send(first, perm=onward), send(second, perm=backward)
             firsts.append((first, send(first, perm=swap_core)))
             seconds.append((second, send(second, perm=swap_core)))
+            if step == 1:
+                _, _, cot_away = tie((first, second, cot_away))
+                mine, theirs = grad_product(core_only, cotangent, cot_away, firsts[0] + seconds[0])
+                own.append(mine)
+                away.append(send(theirs, perm=swap_pair))
+            if step == max(min(2, early), 1):
+                _, _, before = tie((first, second, before))
+                data, filt, filtered, gated = forward_filter(linked, before, product, taps, queries)
+                gated_own = lax.dynamic_index_in_dim(gated, pair, 0, False)
+                gated_away = send(lax.dynamic_index_in_dim(gated, 1 - pair, 0, False), perm=swap_pair)
         else:
             firsts.append((first, swapped[:half]))
             seconds.append((second, swapped[half:]))
+            continue
         if step == size - 1 and back is not None:
             firsts[step], seconds[step], back, parts[0] = tie((firsts[step], seconds[step], back, parts[0]))
         mine, theirs = grad_product(core_only, cotangent, cot_away, firsts[step] + seconds[step])
         own.append(mine)
         away.append(send(theirs, perm=swap_pair))
-        if step == cut - 1:
+        if step == max(cut - 1, 1) and step < size - 1:
             sums = projected(range(cut), None, False)
         if step == size - 1:
-            sums = projected(range(cut, size), sums, True)
+            sums = projected(range(0 if sums is None else cut, size), sums, True)
+            away[step], sums = tie((away[step], sums))
         if step in stages:
             sets = stages[step]
             mirror = [(size - s) % size for s in sets]
@@ -550,11 +553,12 @@
 
 def solution(mesh):
     block = P("seq", "tp")
-    ring = mesh.shape["tp"] == 1 and mesh.shape["seq"] % 4 == 0 and mesh.shape["seq"] > 4
+    count = mesh.shape["seq"]
+    ring = mesh.shape["tp"] == 1 and count & (count - 1) == 0 and count >= 8
 
     def run(queries, keys, values, w_out, taps, seg_ids, cotangent):
         rows, chans = queries.shape
-        place = on_ring if ring and rows * lax.axis_size("seq") == chans else on_device
+        place = on_ring if ring and rows * count == chans else on_device
         return place(queries, keys, values, w_out, taps, seg_ids, cotangent)
 
     return jax.shard_map(

time: 300 us -> 255 us (0.85)
  local copies, waits for them, and re-layouts: 63.8 us -> 23.9 us
  waiting for transfers between devices: 95.2 us -> 70.4 us
  Pallas kernels: 70.5 us -> 90.2 us
    unnamed x197 -> x89, local copies, waits for them, and re-layouts: 55.6 us -> 13.7 us
    ppermute x14, waiting for transfers between devices: 39.2 us -> 26.6 us  [on_ring(): first, second = (send(first, perm=onward), send(second, perm=backward))]
    ppermute x1, waiting for transfers between devices: 17.4 us -> 6.33 us  [on_ring(): cot_away = send(cotangent, perm=swap_pair)]
    ppermute x8, waiting for transfers between devices: 14.6 us -> 6.47 us  [on_ring(): away.append(send(theirs, perm=swap_pair))]
    pallas_call x8, Pallas kernels: 27.3 us -> 34.2 us  [grad_product(): pl.pallas_call(grad_kernel, out_shape=(out, out), grid_spec=pltpu.Prefetc...]
    ppermute x5, waiting for transfers between devices: 3.6 us -> 10.1 us  [halve(): away = lax.ppermute(away, 'seq', [(i, i ^ bit) for i in range(nseq)])]
    pallas_call x3, Pallas kernels: 15.1 us -> 20.6 us  [backward_filter(): pl.pallas_call(functools.partial(backward_kernel, count), out_shape=(jax....]
    ppermute x5, starting transfers between devices: 7.84 us -> 2.95 us  [halve(): away = lax.ppermute(away, 'seq', [(i, i ^ bit) for i in range(nseq)])]
  transfers between devices with their start and end apart: 49 -> 49, of which waited for: 18 -> 15; matrix products, arithmetic and copies ran while one was open for 4% -> 5% of each run, Pallas kernels for 18% -> 28%
where the time goes in v5:
time: 255 us; the launch traced here: 253 us
  Pallas kernels  90.2 us (35%)
  waiting for transfers between devices  70.4 us (28%)
  starting transfers between devices  59.9 us (23%)
  local copies, waits for them, and re-layouts  23.9 us (9%)
  other arithmetic  6.44 us (3%)
    pallas_call x8, Pallas kernels, grad_product(): pl.pallas_call(grad_kernel, out_shape=(out, out), grid_spec=pltpu.Prefetc...  34.2 us
    ppermute x14, waiting for transfers between devices, on_ring(): first, second = (send(first, perm=onward), send(second, perm=backward))  26.6 us
    ppermute x3, waiting for transfers between devices, on_ring(): parts.append(send(back[2], perm=earlier))  20.8 us
    pallas_call x3, Pallas kernels, backward_filter(): pl.pallas_call(functools.partial(backward_kernel, count), out_shape=(jax....  20.6 us
    pallas_call x2, Pallas kernels, project(): pl.pallas_call(functools.partial(project_kernel, len(groups), before is N...  18.2 us
    ppermute x14, starting transfers between devices, on_ring(): first, second = (send(first, perm=onward), send(second, perm=backward))  14.8 us
    unnamed x89, local copies, waits for them, and re-layouts  13.7 us
    ppermute x5, waiting for transfers between devices, halve(): away = lax.ppermute(away, 'seq', [(i, i ^ bit) for i in range(nseq)])  10.1 us
  transfers between devices with their start and end apart: 49, of which 15 were waited for; matrix products, arithmetic and copies ran while one was open for 5% of the time, Pallas kernels for 28%

profile of v5, /device:TPU:1, one launch (start us, length us, event | category | flops | bytes accessed | tf_op | source)
XLA Modules:
  0.0 253.3 jit_solution(14424039653982410843)
XLA Ops:
  8.7 9.4 %collective-permute-done.1.second.refs_6_ = bf16[64,4096]{1,0:T(8,128)(2,1)} collective-permute-done((bf16[64,4096]{1,0:T(8,128)(2,1)S(1)}, bf16[64,4096]{1,0:T(8,128)(2,1)}, u32[]{:S(2)}, u32[]{:S(2)}) %collective-permute-start.1) | collective-permute-done | bytes 524320 | tf_op jit(solution)/shard_map/ppermute | solution.py:462
  20.8 6.3 %collective-permute-done.2.cot_away = bf16[128,4096]{1,0:T(8,128)(2,1)S(1)} collective-permute-done((bf16[128,4096]{1,0:T(8,128)(2,1)}, bf16[128,4096]{1,0:T(8,128)(2,1)S(1)}, u32[]{:S(2)}, u32[]{:S(2)}) %collective-permute-start.2) | collective-permute-done | bytes 1048608 | tf_op jit(solution)/shard_map/ppermute | solution.py:429
  28.5 4.1 %collective-permute-start.25 = (bf16[128,4096]{1,0:T(8,128)(2,1)}, bf16[128,4096]{1,0:T(8,128)(2,1)}, u32[]{:S(2)}, u32[]{:S(2)}) collective-permute-start(bf16[128,4096]{1,0:T(8,128)(2,1)} %multiply_convert_fusion.product), channel_id=1, source_target_pairs={{0,1},{1,2},{2,3},{3,4},{4,5},{5,6},{6,7},{7,8},{8,9},{9,10},{10,1... | collective-permute-start | bytes 3145736 | tf_op jit(solution)/shard_map/ppermute | solution.py:432
  34.9 4.3 %shard_map.263 = (bf16[128,256]{1,0:T(8,128)(2,1)}, bf16[128,256]{1,0:T(8,128)(2,1)}) custom-call(s32[1]{0:T(128)} %bitcast.scalars, bf16[128,4096]{1,0:T(8,128)(2,1)} %cot_own.15, bf16[128,4096]{1,0:T(8,128)(2,1)} %copy-done, bf16[64,4096]{1,0:T(8,128)(2,1)} %copy-done.3, bf16[64,4096]{1,0:T(8,128)(2,1)} %get-tuple-element.170.first_other.refs_1_, ...), custom_call_target="tpu_custom_call" | custom-call | flops 536870912 | bytes 4194304 | tf_op jit(solution)/shard_map/pallas_call | solution.py:207
  40.8 4.3 %shard_map.264 = (bf16[128,256]{1,0:T(8,128)(2,1)}, bf16[128,256]{1,0:T(8,128)(2,1)}) custom-call(s32[1]{0:T(128)} %bitcast.scalars, bf16[128,4096]{1,0:T(8,128)(2,1)} %cot_own.15, bf16[128,4096]{1,0:T(8,128)(2,1)} %copy-done, bf16[64,4096]{1,0:T(8,128)(2,1)} %collective-permute-done.first.refs_4_, bf16[64,4096]{1,0:T(8,128)(2,1)} %copy-done.7, ...), custom_call_target="tpu_custom_call" | custom-call | flops 536870912 | bytes 4194304 | tf_op jit(solution)/shard_map/pallas_call | solution.py:207
  52.4 4.3 %shard_map.265 = (bf16[128,256]{1,0:T(8,128)(2,1)}, bf16[128,256]{1,0:T(8,128)(2,1)}) custom-call(s32[1]{0:T(128)} %bitcast.scalars, bf16[128,4096]{1,0:T(8,128)(2,1)} %cot_own.15, bf16[128,4096]{1,0:T(8,128)(2,1)} %copy-done, bf16[64,4096]{1,0:T(8,128)(2,1)} %copy-done.8, bf16[64,4096]{1,0:T(8,128)(2,1)} %copy-done.13, bf16[64,4096]{1,0:T(8,128)(2,1)} %copy-done.6, ...), custom_call_target="tpu_custom_call" | custom-call | flops 536870912 | bytes 4194304 | tf_op jit(solution)/shard_map/pallas_call | solution.py:207
  57.4 4.9 %collective-permute-done.10.first.refs_12_ = bf16[64,4096]{1,0:T(8,128)(2,1)S(1)} collective-permute-done((bf16[64,4096]{1,0:T(8,128)(2,1)S(1)}, bf16[64,4096]{1,0:T(8,128)(2,1)S(1)}, u32[]{:S(2)}, u32[]{:S(2)}) %collective-permute-start.10) | collective-permute-done | bytes 524320 | tf_op jit(solution)/shard_map/ppermute | solution.py:462
  70.9 9.6 %shard_map.268 = (f32[256,4096]{1,0:T(8,128)}, f32[256,4096]{1,0:T(8,128)}, bf16[128,4096]{1,0:T(8,128)(2,1)}, bf16[2,128,2048]{2,1,0:T(8,128)(2,1)}) custom-call(s32[1]{0:T(128)} %bitcast.10.linked_ref, bf16[256,256]{1,0:T(8,128)(2,1)} %constant.198.clone.fwd_hi, bf16[256,256]{1,0:T(8,128)(2,1)} %constant.199.clone.fwd_lo, ...), custom_call_target="tpu_custom_call" | custom-call | flops 1610612736 | bytes 14680064 | tf_op jit(solution)/shard_map/pallas_call | solution.py:159
  82.2 4.3 %shard_map.266 = (bf16[128,256]{1,0:T(8,128)(2,1)}, bf16[128,256]{1,0:T(8,128)(2,1)}) custom-call(s32[1]{0:T(128)} %bitcast.scalars, bf16[128,4096]{1,0:T(8,128)(2,1)} %cot_own.15, bf16[128,4096]{1,0:T(8,128)(2,1)} %copy-done, bf16[64,4096]{1,0:T(8,128)(2,1)} %copy-done.14, bf16[64,4096]{1,0:T(8,128)(2,1)} %copy-done.16, bf16[64,4096]{1,0:T(8,128)(2,1)} %copy-done.15, ...), custom_call_target="tpu_custom_call" | custom-call | flops 536870912 | bytes 4194304 | tf_op jit(solution)/shard_map/pallas_call | solution.py:207
  94.8 4.3 %shard_map.267 = (bf16[128,256]{1,0:T(8,128)(2,1)}, bf16[128,256]{1,0:T(8,128)(2,1)}) custom-call(s32[1]{0:T(128)} %bitcast.scalars, bf16[128,4096]{1,0:T(8,128)(2,1)} %cot_own.15, bf16[128,4096]{1,0:T(8,128)(2,1)} %copy-done, bf16[64,4096]{1,0:T(8,128)(2,1)} %copy-done.18, bf16[64,4096]{1,0:T(8,128)(2,1)} %copy-done.19, ...), custom_call_target="tpu_custom_call" | custom-call | flops 536870912 | bytes 4194304 | tf_op jit(solution)/shard_map/pallas_call | solution.py:207
  107.3 9.7 %shard_map.269.refs_12_ = f32[256,4096]{1,0:T(8,128)} custom-call(s32[11]{0:T(128)} %stack.118.scalars, bf16[128,2048]{1,0:T(8,128)(2,1)} %get-tuple-element.168.gated_own, bf16[128,2048]{1,0:T(8,128)(2,1)} %copy-done.11, bf16[64,4096]{1,0:T(8,128)(2,1)} %copy-done.3, bf16[64,4096]{1,0:T(8,128)(2,1)} %get-tuple-element.170.first_other.refs_1_, ...), custom_call_target="tpu_custom_call" | custom-call | flops 2684354560 | bytes 15728640 | tf_op jit(solution)/shard_map/pallas_call | solution.py:276
  120.1 4.2 %shard_map.270 = (bf16[128,256]{1,0:T(8,128)(2,1)}, bf16[128,256]{1,0:T(8,128)(2,1)}) custom-call(s32[1]{0:T(128)} %bitcast.scalars, bf16[128,4096]{1,0:T(8,128)(2,1)} %cot_own.15, bf16[128,4096]{1,0:T(8,128)(2,1)} %copy-done, bf16[64,4096]{1,0:T(8,128)(2,1)} %copy-done.9, bf16[64,4096]{1,0:T(8,128)(2,1)} %copy-done.21, bf16[64,4096]{1,0:T(8,128)(2,1)} %copy-done.10, ...), custom_call_target="tpu_custom_call" | custom-call | flops 536870912 | bytes 4194304 | tf_op jit(solution)/shard_map/pallas_call | solution.py:207
  125.6 4.3 %collective-permute-done.27.first.refs_4_ = bf16[64,4096]{1,0:T(8,128)(2,1)S(1)} collective-permute-done((bf16[64,4096]{1,0:T(8,128)(2,1)S(1)}, bf16[64,4096]{1,0:T(8,128)(2,1)S(1)}, u32[]{:S(2)}, u32[]{:S(2)}) %collective-permute-start.27) | collective-permute-done | bytes 524320 | tf_op jit(solution)/shard_map/ppermute | solution.py:462
  131.7 8.9 %shard_map.271 = (bf16[128,4096]{1,0:T(8,128)(2,1)}, f32[128,4096]{1,0:T(8,128)}, bf16[4,128,512]{2,1,0:T(8,128)(2,1)}, f32[4,8,128,128]{3,2,1,0:T(8,128)}) custom-call(s32[6]{0:T(128)} %stack.120.scalars, bf16[256,256]{1,0:T(8,128)(2,1)} %constant.198.clone.fwd_hi, bf16[256,256]{1,0:T(8,128)(2,1)} %constant.199.clone.fwd_lo, ...), custom_call_target="tpu_custom_call" | custom-call | flops 939524096 | bytes 8912896 | tf_op jit(solution)/shard_map/pallas_call | solution.py:343
  147.1 5.1 %collective-permute-done.32.first.refs_8_ = bf16[64,4096]{1,0:T(8,128)(2,1)S(1)} collective-permute-done((bf16[64,4096]{1,0:T(8,128)(2,1)S(1)}, bf16[64,4096]{1,0:T(8,128)(2,1)S(1)}, u32[]{:S(2)}, u32[]{:S(2)}) %collective-permute-start.32) | collective-permute-done | bytes 524320 | tf_op jit(solution)/shard_map/ppermute | solution.py:462
  159.4 4.3 %shard_map.272 = (bf16[128,256]{1,0:T(8,128)(2,1)}, bf16[128,256]{1,0:T(8,128)(2,1)}) custom-call(s32[1]{0:T(128)} %bitcast.scalars, bf16[128,4096]{1,0:T(8,128)(2,1)} %cot_own.15, bf16[128,4096]{1,0:T(8,128)(2,1)} %copy-done, bf16[64,4096]{1,0:T(8,128)(2,1)} %copy-done.23, bf16[64,4096]{1,0:T(8,128)(2,1)} %copy-done.27, bf16[64,4096]{1,0:T(8,128)(2,1)} %copy-done.24, ...), custom_call_target="tpu_custom_call" | custom-call | flops 536870912 | bytes 4194304 | tf_op jit(solution)/shard_map/pallas_call | solution.py:207
  163.7 4.3 %collective-permute-start.38 = (bf16[128,256]{1,0:T(8,128)(2,1)}, bf16[128,256]{1,0:T(8,128)(2,1)S(1)}, u32[]{:S(2)}, u32[]{:S(2)}) collective-permute-start(bf16[128,256]{1,0:T(8,128)(2,1)} %get-tuple-element.125), channel_id=1, source_target_pairs={{0,2},{1,3},{2,0},{3,1},{4,6},{5,7},{6,4},{7,5},{8,10},{9,11},{10,... | collective-permute-start | bytes 196616 | tf_op jit(solution)/shard_map/ppermute | solution.py:483
  171.1 5.8 %shard_map.273 = (bf16[128,4096]{1,0:T(8,128)(2,1)}, f32[128,4096]{1,0:T(8,128)}, bf16[2,128,512]{2,1,0:T(8,128)(2,1)}, f32[4,8,128,128]{3,2,1,0:T(8,128)}) custom-call(s32[4]{0:T(128)} %pad_add_fusion.scalars, bf16[256,256]{1,0:T(8,128)(2,1)} %constant.198.clone.fwd_hi, ...), custom_call_target="tpu_custom_call", output_to_operand_aliasing={{0}: (17, {}), {1}: (18, {}), {3}: (19, {})} | custom-call | flops 469762048 | bytes 4456448 | tf_op jit(solution)/shard_map/pallas_call | solution.py:343
  176.9 4.3 %shard_map.274 = (bf16[128,256]{1,0:T(8,128)(2,1)}, bf16[128,256]{1,0:T(8,128)(2,1)}) custom-call(s32[1]{0:T(128)} %bitcast.scalars, bf16[128,4096]{1,0:T(8,128)(2,1)} %cot_own.15, bf16[128,4096]{1,0:T(8,128)(2,1)} %copy-done, bf16[64,4096]{1,0:T(8,128)(2,1)} %copy-done.25, bf16[64,4096]{1,0:T(8,128)(2,1)} %collective-permute-done.33.first_other.refs_9_, ...), custom_call_target="tpu_custom_call" | custom-call | flops 536870912 | bytes 4194304 | tf_op jit(solution)/shard_map/pallas_call | solution.py:207
  182.1 8.6 %shard_map.275 = (f32[128,4096]{1,0:T(8,128)}, bf16[128,4096]{1,0:T(8,128)(2,1)}) custom-call(s32[7]{0:T(128)} %stack.122.scalars, bf16[128,2048]{1,0:T(8,128)(2,1)} %get-tuple-element.168.gated_own, bf16[128,2048]{1,0:T(8,128)(2,1)} %copy-done.11, bf16[64,4096]{1,0:T(8,128)(2,1)} %copy-done.9, bf16[64,4096]{1,0:T(8,128)(2,1)} %copy-done.21, ...), custom_call_target="tpu_custom_call" | custom-call | flops 1610612736 | bytes 11534336 | tf_op jit(solution)/shard_map/pallas_call | solution.py:276
  191.3 5.8 %shard_map.276 = (bf16[128,4096]{1,0:T(8,128)(2,1)}, f32[128,4096]{1,0:T(8,128)}, bf16[2,128,512]{2,1,0:T(8,128)(2,1)}, f32[4,8,128,128]{3,2,1,0:T(8,128)}) custom-call(s32[4]{0:T(128)} %pad_add_fusion.2.scalars, bf16[256,256]{1,0:T(8,128)(2,1)} %constant.198.clone.fwd_hi, ...), custom_call_target="tpu_custom_call", output_to_operand_aliasing={{0}: (17, {}), {1}: (18, {}), {3}: (19, {})} | custom-call | flops 469762048 | bytes 4456448 | tf_op jit(solution)/shard_map/pallas_call | solution.py:343
  206.5 5.4 %collective-permute-done.45 = bf16[1,8,128,128]{3,2,1,0:T(8,128)(2,1)S(1)} collective-permute-done((bf16[1,8,128,128]{3,2,1,0:T(8,128)(2,1)S(1)}, bf16[1,8,128,128]{3,2,1,0:T(8,128)(2,1)S(1)}, u32[]{:S(2)}, u32[]{:S(2)}) %collective-permute-start.45) | collective-permute-done | bytes 262176 | tf_op jit(solution)/shard_map/ppermute | solution.py:74
  219.7 18.0 %collective-permute-done.42.refs_1_ = bf16[2,128,512]{2,1,0:T(8,128)(2,1)S(1)} collective-permute-done((bf16[2,128,512]{2,1,0:T(8,128)(2,1)S(1)}, bf16[2,128,512]{2,1,0:T(8,128)(2,1)S(1)}, u32[]{:S(2)}, u32[]{:S(2)}) %collective-permute-start.42) | collective-permute-done | bytes 262176 | tf_op jit(solution)/shard_map/ppermute | solution.py:496
  241.2 7.6 %shard_map.277 = (bf16[128,4096]{1,0:T(8,128)(2,1)}, bf16[128,4096]{1,0:T(8,128)(2,1)}) custom-call(s32[32]{0:T(128)} %select_n.130.scalars, f32[128,4096]{1,0:T(8,128)} %get-tuple-element.151.near, bf16[128,4096]{1,0:T(8,128)(2,1)} %keys.1, bf16[128,4096]{1,0:T(8,128)(2,1)} %values.1, bf16[4,128,512]{2,1,0:T(8,128)(2,1)} %collective-permute-done.39.refs_0_, ...), custom_call_target="tpu_custom_call" | custom-call | flops 2097152 | bytes 7340032 | tf_op jit(solution)/shard_map/pallas_call | solution.py:395
  (208 shorter events, 98.7 us)
Async XLA Ops:
  0.6 27.8 %collective-permute-start.5 = (bf16[128,4096]{1,0:T(8,128)(2,1)}, bf16[128,4096]{1,0:T(8,128)(2,1)}, u32[]{:S(2)}, u32[]{:S(2)}) collective-permute-start(bf16[128,4096]{1,0:T(8,128)(2,1)} %param.27), channel_id=1, source_target_pairs={{0,1},{1,0},{2,3},{3,2},{4,5},{5,4},{6,7},{7,6},{8,9},{9,8},{10,11... | collective-permute-start | bytes 3145736 | tf_op jit(solution)/shard_map/ppermute | solution.py:430
  0.8 26.3 %collective-permute-start.2 = (bf16[128,4096]{1,0:T(8,128)(2,1)}, bf16[128,4096]{1,0:T(8,128)(2,1)S(1)}, u32[]{:S(2)}, u32[]{:S(2)}) collective-permute-start(bf16[128,4096]{1,0:T(8,128)(2,1)} %cot_own.15), channel_id=1, source_target_pairs={{0,2},{1,3},{2,0},{3,1},{4,6},{5,7},{6,4},{7,5},{8,10},{9,11},{10,... | collective-permute-start | bytes 3145736 | tf_op jit(solution)/shard_map/ppermute | solution.py:429
  6.0 14.4 %collective-permute-start = (bf16[64,4096]{1,0:T(8,128)(2,1)S(1)}, bf16[64,4096]{1,0:T(8,128)(2,1)}, u32[]{:S(2)}, u32[]{:S(2)}) collective-permute-start(bf16[64,4096]{1,0:T(8,128)(2,1)S(1)} %get-tuple-element.172.first.refs_0_), channel_id=1, source_target_pairs={{0,8},{1,9},{2,10},{3,11},{8,16},{9,17},{10,18},{11,19},{16,24},{1... | collective-permute-start | bytes 1572872 | tf_op jit(solution)/shard_map/ppermute | solution.py:462
  18.1 21.1 %collective-permute-start.8 = (bf16[64,4096]{1,0:T(8,128)(2,1)}, bf16[64,4096]{1,0:T(8,128)(2,1)S(1)}, u32[]{:S(2)}, u32[]{:S(2)}) collective-permute-start(bf16[64,4096]{1,0:T(8,128)(2,1)} %collective-permute-done.1.second.refs_6_), channel_id=1, source_target_pairs={{0,1},{1,0},{2,3},{3,2},{4,5},{5,4},{6,7},{7,6},{8,9},{9,8},{10,11... | collective-permute-start | bytes 1572872 | tf_op jit(solution)/shard_map/ppermute | solution.py:464
  19.2 26.5 %collective-permute-start.4 = (bf16[64,4096]{1,0:T(8,128)(2,1)}, bf16[64,4096]{1,0:T(8,128)(2,1)S(1)}, u32[]{:S(2)}, u32[]{:S(2)}) collective-permute-start(bf16[64,4096]{1,0:T(8,128)(2,1)} %collective-permute-done.1.second.refs_6_), channel_id=1, source_target_pairs={{8,0},{9,1},{10,2},{11,3},{16,8},{17,9},{18,10},{19,11},{24,16},{2... | collective-permute-start | bytes 1572872 | tf_op jit(solution)/shard_map/ppermute | solution.py:462
  20.5 18.8 %collective-permute-start.7 = (bf16[64,4096]{1,0:T(8,128)(2,1)}, bf16[64,4096]{1,0:T(8,128)(2,1)S(1)}, u32[]{:S(2)}, u32[]{:S(2)}) collective-permute-start(bf16[64,4096]{1,0:T(8,128)(2,1)} %collective-permute-done.first.refs_4_), channel_id=1, source_target_pairs={{0,1},{1,0},{2,3},{3,2},{4,5},{5,4},{6,7},{7,6},{8,9},{9,8},{10,11... | collective-permute-start | bytes 1572872 | tf_op jit(solution)/shard_map/ppermute | solution.py:463
  27.1 18.7 %collective-permute-start.3 = (bf16[64,4096]{1,0:T(8,128)(2,1)}, bf16[64,4096]{1,0:T(8,128)(2,1)S(1)}, u32[]{:S(2)}, u32[]{:S(2)}) collective-permute-start(bf16[64,4096]{1,0:T(8,128)(2,1)} %collective-permute-done.first.refs_4_), channel_id=1, source_target_pairs={{0,8},{1,9},{2,10},{3,11},{8,16},{9,17},{10,18},{11,19},{16,24},{1... | collective-permute-start | bytes 1572872 | tf_op jit(solution)/shard_map/ppermute | solution.py:462
  28.5 42.4 %collective-permute-start.25 = (bf16[128,4096]{1,0:T(8,128)(2,1)}, bf16[128,4096]{1,0:T(8,128)(2,1)}, u32[]{:S(2)}, u32[]{:S(2)}) collective-permute-start(bf16[128,4096]{1,0:T(8,128)(2,1)} %multiply_convert_fusion.product), channel_id=1, source_target_pairs={{0,1},{1,2},{2,3},{3,4},{4,5},{5,6},{6,7},{7,8},{8,9},{9,10},{10,1... | collective-permute-start | bytes 3145736 | tf_op jit(solution)/shard_map/ppermute | solution.py:432
  62.3 18.3 %collective-permute-start.17 = (bf16[64,4096]{1,0:T(8,128)(2,1)S(1)}, bf16[64,4096]{1,0:T(8,128)(2,1)S(1)}, u32[]{:S(2)}, u32[]{:S(2)}) collective-permute-start(bf16[64,4096]{1,0:T(8,128)(2,1)S(1)} %collective-permute-done.10.first.refs_12_), channel_id=1, source_target_pairs={{0,1},{1,0},{2,3},{3,2},{4,5},{5,4},{6,7},{7,6},{8,9},{9,8},{10,11... | collective-permute-start | bytes 1572872 | tf_op jit(solution)/shard_map/ppermute | solution.py:463
  63.6 16.9 %collective-permute-start.18 = (bf16[64,4096]{1,0:T(8,128)(2,1)S(1)}, bf16[64,4096]{1,0:T(8,128)(2,1)S(1)}, u32[]{:S(2)}, u32[]{:S(2)}) collective-permute-start(bf16[64,4096]{1,0:T(8,128)(2,1)S(1)} %collective-permute-done.11.second.refs_14_), channel_id=1, source_target_pairs={{0,1},{1,0},{2,3},{3,2},{4,5},{5,4},{6,7},{7,6},{8,9},{9,8},{10,11... | collective-permute-start | bytes 1572872 | tf_op jit(solution)/shard_map/ppermute | solution.py:464
  64.9 21.6 %collective-permute-start.15 = (bf16[64,4096]{1,0:T(8,128)(2,1)S(1)}, bf16[64,4096]{1,0:T(8,128)(2,1)S(1)}, u32[]{:S(2)}, u32[]{:S(2)}) collective-permute-start(bf16[64,4096]{1,0:T(8,128)(2,1)S(1)} %collective-permute-done.10.first.refs_12_), channel_id=1, source_target_pairs={{0,8},{1,9},{2,10},{3,11},{8,16},{9,17},{10,18},{11,19},{16,24},{1... | collective-permute-start | bytes 1572872 | tf_op jit(solution)/shard_map/ppermute | solution.py:462
  69.0 18.0 %collective-permute-start.16 = (bf16[64,4096]{1,0:T(8,128)(2,1)S(1)}, bf16[64,4096]{1,0:T(8,128)(2,1)}, u32[]{:S(2)}, u32[]{:S(2)}) collective-permute-start(bf16[64,4096]{1,0:T(8,128)(2,1)S(1)} %collective-permute-done.11.second.refs_14_), channel_id=1, source_target_pairs={{8,0},{9,1},{10,2},{11,3},{16,8},{17,9},{18,10},{19,11},{24,16},{2... | collective-permute-start | bytes 1572872 | tf_op jit(solution)/shard_map/ppermute | solution.py:462
  91.9 14.6 %collective-permute-start.26 = (bf16[128,2048]{1,0:T(8,128)(2,1)}, bf16[128,2048]{1,0:T(8,128)(2,1)S(1)}, u32[]{:S(2)}, u32[]{:S(2)}) collective-permute-start(bf16[128,2048]{1,0:T(8,128)(2,1)} %get-tuple-element.167), channel_id=1, source_target_pairs={{0,2},{1,3},{2,0},{3,1},{4,6},{5,7},{6,4},{7,5},{8,10},{9,11},{10,... | collective-permute-start | bytes 1572872 | tf_op jit(solution)/shard_map/ppermute | solution.py:474
  99.1 17.9 %collective-permute-start.24 = (bf16[128,256]{1,0:T(8,128)(2,1)}, bf16[128,256]{1,0:T(8,128)(2,1)S(1)}, u32[]{:S(2)}, u32[]{:S(2)}) collective-permute-start(bf16[128,256]{1,0:T(8,128)(2,1)} %get-tuple-element.100), channel_id=1, source_target_pairs={{0,2},{1,3},{2,0},{3,1},{4,6},{5,7},{6,4},{7,5},{8,10},{9,11},{10,... | collective-permute-start | bytes 196616 | tf_op jit(solution)/shard_map/ppermute | solution.py:483
  101.8 16.7 %collective-permute-start.29 = (bf16[64,4096]{1,0:T(8,128)(2,1)S(1)}, bf16[64,4096]{1,0:T(8,128)(2,1)S(1)}, u32[]{:S(2)}, u32[]{:S(2)}) collective-permute-start(bf16[64,4096]{1,0:T(8,128)(2,1)S(1)} %collective-permute-done.20.first.refs_0_), channel_id=1, source_target_pairs={{0,1},{1,0},{2,3},{3,2},{4,5},{5,4},{6,7},{7,6},{8,9},{9,8},{10,11... | collective-permute-start | bytes 1572872 | tf_op jit(solution)/shard_map/ppermute | solution.py:463
  104.2 14.3 %collective-permute-start.30 = (bf16[64,4096]{1,0:T(8,128)(2,1)S(1)}, bf16[64,4096]{1,0:T(8,128)(2,1)S(1)}, u32[]{:S(2)}, u32[]{:S(2)}) collective-permute-start(bf16[64,4096]{1,0:T(8,128)(2,1)S(1)} %collective-permute-done.21.second.refs_2_), channel_id=1, source_target_pairs={{0,1},{1,0},{2,3},{3,2},{4,5},{5,4},{6,7},{7,6},{8,9},{9,8},{10,11... | collective-permute-start | bytes 1572872 | tf_op jit(solution)/shard_map/ppermute | solution.py:464
  142.1 15.6 %collective-permute-start.36 = (bf16[64,4096]{1,0:T(8,128)(2,1)S(1)}, bf16[64,4096]{1,0:T(8,128)(2,1)S(1)}, u32[]{:S(2)}, u32[]{:S(2)}) collective-permute-start(bf16[64,4096]{1,0:T(8,128)(2,1)S(1)} %collective-permute-done.27.first.refs_4_), channel_id=1, source_target_pairs={{0,1},{1,0},{2,3},{3,2},{4,5},{5,4},{6,7},{7,6},{8,9},{9,8},{10,11... | collective-permute-start | bytes 1572872 | tf_op jit(solution)/shard_map/ppermute | solution.py:463
  144.6 32.3 %collective-permute-start.39 = (bf16[4,128,512]{2,1,0:T(8,128)(2,1)}, bf16[4,128,512]{2,1,0:T(8,128)(2,1)}, u32[]{:S(2)}, u32[]{:S(2)}) collective-permute-start(bf16[4,128,512]{2,1,0:T(8,128)(2,1)} %get-tuple-element.119), channel_id=1, source_target_pairs={{1,0},{2,1},{3,2},{4,3},{5,4},{6,5},{7,6},{8,7},{9,8},{10,9},{11,1... | collective-permute-start | bytes 1572872 | tf_op jit(solution)/shard_map/ppermute | solution.py:496
  152.3 24.6 %collective-permute-start.33 = (bf16[64,4096]{1,0:T(8,128)(2,1)S(1)}, bf16[64,4096]{1,0:T(8,128)(2,1)}, u32[]{:S(2)}, u32[]{:S(2)}) collective-permute-start(bf16[64,4096]{1,0:T(8,128)(2,1)S(1)} %collective-permute-done.32.first.refs_8_), channel_id=1, source_target_pairs={{0,1},{1,0},{2,3},{3,2},{4,5},{5,4},{6,7},{7,6},{8,9},{9,8},{10,11... | collective-permute-start | bytes 1572872 | tf_op jit(solution)/shard_map/ppermute | solution.py:463
  155.0 21.9 %collective-permute-start.35 = (bf16[64,4096]{1,0:T(8,128)(2,1)S(1)}, bf16[64,4096]{1,0:T(8,128)(2,1)}, u32[]{:S(2)}, u32[]{:S(2)}) collective-permute-start(bf16[64,4096]{1,0:T(8,128)(2,1)S(1)} %collective-permute-done.34.second.refs_10_), channel_id=1, source_target_pairs={{0,1},{1,0},{2,3},{3,2},{4,5},{5,4},{6,7},{7,6},{8,9},{9,8},{10,11... | collective-permute-start | bytes 1572872 | tf_op jit(solution)/shard_map/ppermute | solution.py:464
  205.1 43.8 %collective-permute-start.41 = (bf16[128,4096]{1,0:T(8,128)(2,1)}, bf16[128,4096]{1,0:T(8,128)(2,1)S(1)}, u32[]{:S(2)}, u32[]{:S(2)}) collective-permute-start(bf16[128,4096]{1,0:T(8,128)(2,1)} %get-tuple-element.142), channel_id=1, source_target_pairs={{0,2},{1,3},{2,0},{3,1},{4,6},{5,7},{6,4},{7,5},{8,10},{9,11},{10,... | collective-permute-start | bytes 3145736 | tf_op jit(solution)/shard_map/ppermute | solution.py:500
  212.1 25.6 %collective-permute-start.42 = (bf16[2,128,512]{2,1,0:T(8,128)(2,1)S(1)}, bf16[2,128,512]{2,1,0:T(8,128)(2,1)S(1)}, u32[]{:S(2)}, u32[]{:S(2)}) collective-permute-start(bf16[2,128,512]{2,1,0:T(8,128)(2,1)S(1)} %copy-done.43), channel_id=1, source_target_pairs={{1,0},{2,1},{3,2},{4,3},{5,4},{6,5},{7,6},{8,7},{9,8},{10,9},{11,1... | collective-permute-start | bytes 786440 | tf_op jit(solution)/shard_map/ppermute | solution.py:496
  216.0 24.5 %collective-permute-start.43 = (bf16[2,128,512]{2,1,0:T(8,128)(2,1)}, bf16[2,128,512]{2,1,0:T(8,128)(2,1)S(1)}, u32[]{:S(2)}, u32[]{:S(2)}) collective-permute-start(bf16[2,128,512]{2,1,0:T(8,128)(2,1)} %get-tuple-element.153), channel_id=1, source_target_pairs={{1,0},{2,1},{3,2},{4,3},{5,4},{6,5},{7,6},{8,7},{9,8},{10,9},{11,1... | collective-permute-start | bytes 786440 | tf_op jit(solution)/shard_map/ppermute | solution.py:496
  218.0 30.8 %collective-permute-start.47 = (bf16[2,128,128]{2,1,0:T(8,128)(2,1)S(1)}, bf16[2,128,128]{2,1,0:T(8,128)(2,1)S(1)}, u32[]{:S(2)}, u32[]{:S(2)}) collective-permute-start(bf16[2,128,128]{2,1,0:T(8,128)(2,1)S(1)} %fusion.1), channel_id=1, source_target_pairs={{0,8},{1,9},{2,10},{3,11},{4,12},{5,13},{6,14},{7,15},{8,0},{9,1},... | collective-permute-start | bytes 196616 | tf_op jit(solution)/shard_map/ppermute | solution.py:74
  (69 other events, 607.0 us)

commit v6 on v5

--- a/solution.py
+++ b/solution.py
@@ -10,6 +10,7 @@
 
 F32 = jnp.float32
 BF16 = jnp.bfloat16
+GRANT = 16 << 20
 
 
 def spectrum_table(length):
@@ -107,6 +108,10 @@
 
 def ring_step(row, size):
     return jnp.where(row & 1 == 0, row >> 1, size - 1 - (row >> 1))
+
+
+def pinned(space, *arrays):
+    return [pltpu.with_memory_space_constraint(a, space) for a in arrays]
 
 
 def split(data):
@@ -154,33 +159,39 @@
     fixed = pl.BlockSpec((2 * length, 2 * length), lambda j: (0, 0))
     block = pl.BlockSpec((length, width), lambda j: (0, j))
     spectrum = pl.BlockSpec((2 * length, width), lambda j: (0, j))
-    wide = jax.ShapeDtypeStruct((2 * length, chans), F32)
-    narrow = jax.ShapeDtypeStruct((length, chans), BF16)
+    wide = pltpu.HBM((2 * length, chans), F32)
+    narrow = pltpu.HBM((length, chans), BF16)
     return pl.pallas_call(
         forward_kernel,
-        out_shape=(wide, wide, narrow, jax.ShapeDtypeStruct((2, length, chans // 2), BF16)),
+        out_shape=(wide, wide, narrow, pltpu.HBM((2, length, chans // 2), BF16)),
         grid=(chans // width,),
         in_specs=[pl.BlockSpec(memory_space=pltpu.SMEM)]
         + [fixed] * 4
         + [block, block, pl.BlockSpec((width, length), lambda j: (j, 0)), block],
         out_specs=(spectrum, spectrum, block, pl.BlockSpec((2, length, width // 2), lambda j: (0, 0, j))),
-        compiler_params=pltpu.CompilerParams(vmem_limit_bytes=56 << 20),
+        compiler_params=pltpu.CompilerParams(vmem_limit_bytes=GRANT),
         cost_estimate=pl.CostEstimate(
             flops=24 * length * length * chans, bytes_accessed=28 * length * chans, transcendentals=0
         ),
-    )(linked.astype(jnp.int32).reshape(1), *tables(length), before, product, taps, queries)
-
-
-def grad_kernel(scalars, cot_own, cot_away, first, first_other, second, second_other, own_ref, away_ref, total):
-    @pl.when(pl.program_id(0) == 0)
-    def _():
-        total[...] = jnp.zeros_like(total)
+    )(linked.astype(jnp.int32).reshape(1), *tables(length), *pinned(pltpu.HBM, before, product, taps, queries))
+
+
+def grad_kernel(scalars, cot_own, cot_away, first, first_other, second, second_other, own_ref, away_ref):
+    rows, feats = cot_own.shape
+    tile = min(512, feats)
+    depth = first.shape[0]
+    dims = (((1,), (1,)), ((), ()))
 
     def add(refs):
-        rows = jnp.concatenate([ref[...] for ref in refs], 0)
-        dims = (((1,), (1,)), ((), ()))
-        cot = jnp.concatenate([cot_own[...], cot_away[...]], 0)
-        total[...] += lax.dot_general(cot, rows, dims, preferred_element_type=F32)
+        def step(j, total):
+            at = pl.ds(pl.multiple_of(j * tile, tile), tile)
+            left = jnp.concatenate([cot_own[:, at], cot_away[:, at]], 0)
+            right = jnp.concatenate([ref[:, at] for ref in refs], 0)
+            return total + lax.dot_general(left, right, dims, preferred_element_type=F32)
+
+        total = lax.fori_loop(0, feats // tile, step, jnp.zeros((2 * rows, 4 * depth), F32))
+        own_ref[...] = total[:rows].astype(BF16)
+        away_ref[...] = total[rows:].astype(BF16)
 
     @pl.when(scalars[0] == 0)
     def _():
@@ -190,34 +201,20 @@
     def _():
         add((first_other, first, second_other, second))
 
-    @pl.when(pl.program_id(0) == pl.num_programs(0) - 1)
-    def _():
-        rows = own_ref.shape[0]
-        own_ref[...] = total[:rows].astype(BF16)
-        away_ref[...] = total[rows:].astype(BF16)
-
 
 def grad_product(core, cot_own, cot_away, weights):
     rows, feats = cot_own.shape
-    tokens = 2 * rows
     depth = weights[0].shape[0]
-    tile = min(1024, feats)
     out = jax.ShapeDtypeStruct((rows, 4 * depth), BF16)
-    whole = pl.BlockSpec(out.shape, lambda j, core: (0, 0))
+    vmem = pl.BlockSpec(memory_space=pltpu.VMEM)
     return pl.pallas_call(
         grad_kernel,
         out_shape=(out, out),
-        grid_spec=pltpu.PrefetchScalarGridSpec(
-            num_scalar_prefetch=1,
-            grid=(feats // tile,),
-            in_specs=[pl.BlockSpec((rows, tile), lambda j, core: (0, j))] * 2
-            + [pl.BlockSpec((depth, tile), lambda j, core: (0, j))] * 4,
-            out_specs=(whole, whole),
-            scratch_shapes=[pltpu.VMEM((tokens, 4 * depth), F32)],
-        ),
-        compiler_params=pltpu.CompilerParams(vmem_limit_bytes=56 << 20),
+        in_specs=[pl.BlockSpec(memory_space=pltpu.SMEM)] + [vmem] * 6,
+        out_specs=(vmem, vmem),
+        compiler_params=pltpu.CompilerParams(vmem_limit_bytes=GRANT),
         cost_estimate=pl.CostEstimate(
-            flops=8 * tokens * depth * feats, bytes_accessed=(2 * tokens + 8 * depth) * feats, transcendentals=0
+            flops=16 * rows * depth * feats, bytes_accessed=(4 * rows + 8 * depth) * feats, transcendentals=0
         ),
     )(core, cot_own, cot_away, *weights)
 
@@ -272,10 +269,10 @@
     weights = [w for group in groups for w in group]
     whole = pl.BlockSpec((2 * rows, tile), lambda j, s: (0, j))
     block = pl.BlockSpec((rows, tile), lambda j, s: (0, j))
-    halves = tuple(jax.ShapeDtypeStruct((rows, feats), kind) for kind in (F32, BF16))
+    halves = tuple(pltpu.HBM((rows, feats), kind) for kind in (F32, BF16))
     return pl.pallas_call(
         functools.partial(project_kernel, len(groups), before is None, last),
-        out_shape=halves if last else jax.ShapeDtypeStruct((2 * rows, feats), F32),
+        out_shape=halves if last else pltpu.HBM((2 * rows, feats), F32),
         grid_spec=pltpu.PrefetchScalarGridSpec(
             num_scalar_prefetch=1,
             grid=(feats // tile,),
@@ -288,13 +285,18 @@
                 pltpu.VMEM((2 * rows, tile), F32),
             ],
         ),
-        compiler_params=pltpu.CompilerParams(vmem_limit_bytes=56 << 20),
+        compiler_params=pltpu.CompilerParams(vmem_limit_bytes=GRANT),
         cost_estimate=pl.CostEstimate(
             flops=4 * rows * depth * len(weights) * feats,
             bytes_accessed=2 * depth * feats * len(weights) + 4 * rows * chans + 8 * rows * feats,
             transcendentals=0,
         ),
-    )(scalars, gated_own, gated_away, *weights, *([] if before is None else [before]))
+    )(
+        scalars,
+        *pinned(pltpu.HBM, gated_own, gated_away),
+        *pinned(pltpu.VMEM, *weights),
+        *([] if before is None else pinned(pltpu.HBM, before)),
+    )
 
 
 def backward_kernel(count, scalars, fwd_hi, fwd_lo, inv_hi, inv_lo, queries, filtered, data, filt, *refs):
@@ -343,10 +345,10 @@
     return pl.pallas_call(
         functools.partial(backward_kernel, count),
         out_shape=(
-            jax.ShapeDtypeStruct((length, chans), BF16),
-            jax.ShapeDtypeStruct((length, chans), F32),
-            jax.ShapeDtypeStruct((count, length, width), BF16),
-            jax.ShapeDtypeStruct((4, chans // width, length, length), F32),
+            pltpu.HBM((length, chans), BF16),
+            pltpu.HBM((length, chans), F32),
+            pltpu.HBM((count, length, width), BF16),
+            pltpu.HBM((4, chans // width, length, length), F32),
         ),
         grid_spec=pltpu.PrefetchScalarGridSpec(
             num_scalar_prefetch=1,
@@ -364,11 +366,17 @@
             scratch_shapes=[pltpu.VMEM((length, width), BF16)],
         ),
         input_output_aliases={inputs + i: out for i, out in zip(range(len(before)), (0, 1, 3))},
-        compiler_params=pltpu.CompilerParams(vmem_limit_bytes=56 << 20),
+        compiler_params=pltpu.CompilerParams(vmem_limit_bytes=GRANT),
         cost_estimate=pl.CostEstimate(
             flops=28 * length * length * width * count, bytes_accessed=34 * length * width * count, transcendentals=0
         ),
-    )(scalars, *tables(length), queries, filtered, data, filt, *pieces, *before)
+    )(
+        scalars,
+        *tables(length),
+        *pinned(pltpu.HBM, queries, filtered, data, filt),
+        *pinned(pltpu.VMEM, *pieces),
+        *pinned(pltpu.HBM, *before),
+    )
 
 
 def join_kernel(count, scalars, near, keys, values, *refs):
@@ -401,9 +409,9 @@
             in_specs=[block] * 3 + [pl.BlockSpec((1, length, width), place(i)) for i in range(len(parts))],
             out_specs=(block, block),
         ),
-        compiler_params=pltpu.CompilerParams(vmem_limit_bytes=56 << 20),
+        compiler_params=pltpu.CompilerParams(vmem_limit_bytes=GRANT),
         cost_estimate=pl.CostEstimate(flops=4 * length * chans, bytes_accessed=14 * length * chans, transcendentals=0),
-    )(scalars, near, keys, values, *parts)
+    )(scalars, *pinned(pltpu.HBM, near, keys, values), *pinned(pltpu.VMEM, *parts))
 
 
 def on_ring(queries, keys, values, w_out, taps, seg_ids, cotangent):

time: 255 us -> 251 us (0.984)
  Pallas kernels: 90.2 us -> 79.4 us
  waiting for transfers between devices: 70.4 us -> 80 us
  local copies, waits for them, and re-layouts: 23.9 us -> 19.9 us
    pallas_call x12, Pallas kernels: 64.4 us -> 55.5 us  [the longest x8 28 us: grad_product(): pl.pallas_call(grad_kernel, out_shape=(out, out), in_specs=[pl.BlockSpec(...]
    ppermute x14, waiting for transfers between devices: 26.6 us -> 33.8 us  [on_ring(): first, second = (send(first, perm=onward), send(second, perm=backward))]
    ppermute x14, starting transfers between devices: 14.8 us -> 18 us  [on_ring(): first, second = (send(first, perm=onward), send(second, perm=backward))]
    unnamed x89 -> x109, local copies, waits for them, and re-layouts: 13.7 us -> 12.9 us
  transfers between devices with their start and end apart: 49 -> 49, of which waited for: 15 -> 17; matrix products, arithmetic and copies ran while one was open for 5% -> 4% of each run, Pallas kernels for 28% -> 25%
where the time goes in v6:
time: 251 us; the launch traced here: 250 us
  waiting for transfers between devices  80 us (32%)
  Pallas kernels  79.4 us (32%)
  starting transfers between devices  62.1 us (25%)
  local copies, waits for them, and re-layouts  19.9 us (8%)
  other arithmetic  5.81 us (2%)
  between operations  2.78 us (1%)
    ppermute x14, waiting for transfers between devices, on_ring(): first, second = (send(first, perm=onward), send(second, perm=backward))  33.8 us
    pallas_call x8, Pallas kernels, grad_product(): pl.pallas_call(grad_kernel, out_shape=(out, out), in_specs=[pl.BlockSpec(...  28 us
    ppermute x3, waiting for transfers between devices, on_ring(): parts.append(send(back[2], perm=earlier))  21.2 us
    pallas_call x3, Pallas kernels, backward_filter(): pl.pallas_call(functools.partial(backward_kernel, count), out_shape=(pltp...  18 us
    ppermute x14, starting transfers between devices, on_ring(): first, second = (send(first, perm=onward), send(second, perm=backward))  18 us
    pallas_call x2, Pallas kernels, project(): pl.pallas_call(functools.partial(project_kernel, len(groups), before is N...  16.6 us
    unnamed x109, local copies, waits for them, and re-layouts  12.9 us
    ppermute x5, waiting for transfers between devices, halve(): away = lax.ppermute(away, 'seq', [(i, i ^ bit) for i in range(nseq)])  10.1 us
  transfers between devices with their start and end apart: 49, of which 17 were waited for; matrix products, arithmetic and copies ran while one was open for 4% of the time, Pallas kernels for 25%

profile of v6, /device:TPU:1, one launch (start us, length us, event | category | flops | bytes accessed | tf_op | source)
XLA Modules:
  0.0 250.0 jit_solution(757690431318671475)
XLA Ops:
  9.1 9.0 %collective-permute-done.1.second.refs_6_ = bf16[64,4096]{1,0:T(8,128)(2,1)} collective-permute-done((bf16[64,4096]{1,0:T(8,128)(2,1)S(1)}, bf16[64,4096]{1,0:T(8,128)(2,1)}, u32[]{:S(2)}, u32[]{:S(2)}) %collective-permute-start.1) | collective-permute-done | bytes 524320 | tf_op jit(solution)/shard_map/ppermute | solution.py:470
  20.7 6.3 %collective-permute-done.2.cot_away = bf16[128,4096]{1,0:T(8,128)(2,1)S(1)} collective-permute-done((bf16[128,4096]{1,0:T(8,128)(2,1)}, bf16[128,4096]{1,0:T(8,128)(2,1)S(1)}, u32[]{:S(2)}, u32[]{:S(2)}) %collective-permute-start.2) | collective-permute-done | bytes 1048608 | tf_op jit(solution)/shard_map/ppermute | solution.py:437
  28.5 4.1 %collective-permute-start.25 = (bf16[128,4096]{1,0:T(8,128)(2,1)}, bf16[128,4096]{1,0:T(8,128)(2,1)}, u32[]{:S(2)}, u32[]{:S(2)}) collective-permute-start(bf16[128,4096]{1,0:T(8,128)(2,1)} %multiply_convert_fusion.product), channel_id=1, source_target_pairs={{0,1},{1,2},{2,3},{3,4},{4,5},{5,6},{6,7},{7,8},{8,9},{9,10},{10,1... | collective-permute-start | bytes 3145736 | tf_op jit(solution)/shard_map/ppermute | solution.py:440
  42.5 4.4 %collective-permute-done.6.refs_1_.refs_3_ = bf16[128,256]{1,0:T(8,128)(2,1)S(1)} collective-permute-done((bf16[128,256]{1,0:T(8,128)(2,1)S(1)}, bf16[128,256]{1,0:T(8,128)(2,1)S(1)}, u32[]{:S(2)}, u32[]{:S(2)}) %collective-permute-start.6) | collective-permute-done | bytes 65568 | tf_op jit(solution)/shard_map/ppermute | solution.py:477
  54.0 6.6 %collective-permute-done.10.first.refs_12_ = bf16[64,4096]{1,0:T(8,128)(2,1)} collective-permute-done((bf16[64,4096]{1,0:T(8,128)(2,1)S(1)}, bf16[64,4096]{1,0:T(8,128)(2,1)}, u32[]{:S(2)}, u32[]{:S(2)}) %collective-permute-start.10) | collective-permute-done | bytes 524320 | tf_op jit(solution)/shard_map/ppermute | solution.py:470
  62.5 7.2 %collective-permute-start.15 = (bf16[64,4096]{1,0:T(8,128)(2,1)}, bf16[64,4096]{1,0:T(8,128)(2,1)}, u32[]{:S(2)}, u32[]{:S(2)}) collective-permute-start(bf16[64,4096]{1,0:T(8,128)(2,1)} %collective-permute-done.10.first.refs_12_), channel_id=1, source_target_pairs={{0,8},{1,9},{2,10},{3,11},{8,16},{9,17},{10,18},{11,19},{16,24},{1... | collective-permute-start | bytes 1572872 | tf_op jit(solution)/shard_map/ppermute | solution.py:470
  72.6 9.5 %shard_map.268 = (f32[256,4096]{1,0:T(8,128)}, f32[256,4096]{1,0:T(8,128)}, bf16[128,4096]{1,0:T(8,128)(2,1)}, bf16[2,128,2048]{2,1,0:T(8,128)(2,1)}) custom-call(s32[1]{0:T(128)} %bitcast.10.linked_ref, bf16[256,256]{1,0:T(8,128)(2,1)S(1)} %copy-done.24, bf16[256,256]{1,0:T(8,128)(2,1)S(1)} %copy-done.23, bf16[256,256]{1,0:T(8,128)(2,1)S(1)} %copy-done.22, ...), custom_call_target="tpu_custom_call" | custom-call | flops 1610612736 | bytes 14680064 | tf_op jit(solution)/shard_map/pallas_call | solution.py:164
  82.1 3.8 %shard_map.266 = (bf16[128,256]{1,0:T(8,128)(2,1)S(1)}, bf16[128,256]{1,0:T(8,128)(2,1)S(1)}) custom-call(s32[1]{0:T(128)} %bitcast.scalars, bf16[128,4096]{1,0:T(8,128)(2,1)S(1)} %copy-done, bf16[128,4096]{1,0:T(8,128)(2,1)S(1)} %collective-permute-done.2.cot_away, bf16[64,4096]{1,0:T(8,128)(2,1)} %collective-permute-done.10.first.refs_12_, ...), custom_call_target="tpu_custom_call" | custom-call | flops 536870912 | bytes 4194304 | tf_op jit(solution)/shard_map/pallas_call | solution.py:210
  93.2 3.9 %shard_map.267 = (bf16[128,256]{1,0:T(8,128)(2,1)S(1)}, bf16[128,256]{1,0:T(8,128)(2,1)S(1)}) custom-call(s32[1]{0:T(128)} %bitcast.scalars, bf16[128,4096]{1,0:T(8,128)(2,1)S(1)} %copy-done, bf16[128,4096]{1,0:T(8,128)(2,1)S(1)} %collective-permute-done.2.cot_away, bf16[64,4096]{1,0:T(8,128)(2,1)} %collective-permute-done.15.first.refs_16_, ...), custom_call_target="tpu_custom_call" | custom-call | flops 536870912 | bytes 4194304 | tf_op jit(solution)/shard_map/pallas_call | solution.py:210
  98.1 4.5 %collective-permute-done.20.first.refs_0_ = bf16[64,4096]{1,0:T(8,128)(2,1)} collective-permute-done((bf16[64,4096]{1,0:T(8,128)(2,1)}, bf16[64,4096]{1,0:T(8,128)(2,1)}, u32[]{:S(2)}, u32[]{:S(2)}) %collective-permute-start.20) | collective-permute-done | bytes 524320 | tf_op jit(solution)/shard_map/ppermute | solution.py:470
  107.1 8.7 %shard_map.269.refs_12_ = f32[256,4096]{1,0:T(8,128)} custom-call(s32[11]{0:T(128)S(1)} %stack.118.scalars, bf16[128,2048]{1,0:T(8,128)(2,1)} %get-tuple-element.168.gated_own, bf16[128,2048]{1,0:T(8,128)(2,1)} %collective-permute-done.26.gated_away, bf16[64,4096]{1,0:T(8,128)(2,1)S(1)} %get-tuple-element.172.first.refs_0_, bf16[64,4096]{1,0:T(8,128)(2,1)S(1)} %copy-done.4, ...), custom_call_target="tpu_custom_call" | custom-call | flops 2684354560 | bytes 15728640 | tf_op jit(solution)/shard_map/pallas_call | solution.py:273
  118.0 4.4 %shard_map.270 = (bf16[128,256]{1,0:T(8,128)(2,1)S(1)}, bf16[128,256]{1,0:T(8,128)(2,1)}) custom-call(s32[1]{0:T(128)} %bitcast.scalars, bf16[128,4096]{1,0:T(8,128)(2,1)S(1)} %copy-done, bf16[128,4096]{1,0:T(8,128)(2,1)S(1)} %collective-permute-done.2.cot_away, bf16[64,4096]{1,0:T(8,128)(2,1)} %collective-permute-done.20.first.refs_0_, ...), custom_call_target="tpu_custom_call" | custom-call | flops 536870912 | bytes 4194304 | tf_op jit(solution)/shard_map/pallas_call | solution.py:210
  123.7 5.8 %collective-permute-done.27.first.refs_4_ = bf16[64,4096]{1,0:T(8,128)(2,1)S(1)} collective-permute-done((bf16[64,4096]{1,0:T(8,128)(2,1)}, bf16[64,4096]{1,0:T(8,128)(2,1)S(1)}, u32[]{:S(2)}, u32[]{:S(2)}) %collective-permute-start.27) | collective-permute-done | bytes 524320 | tf_op jit(solution)/shard_map/ppermute | solution.py:470
  137.5 7.9 %shard_map.271 = (bf16[128,4096]{1,0:T(8,128)(2,1)}, f32[128,4096]{1,0:T(8,128)}, bf16[4,128,512]{2,1,0:T(8,128)(2,1)}, f32[4,8,128,128]{3,2,1,0:T(8,128)}) custom-call(s32[6]{0:T(128)S(1)} %stack.120.scalars, bf16[256,256]{1,0:T(8,128)(2,1)S(1)} %copy-done.25, bf16[256,256]{1,0:T(8,128)(2,1)S(1)} %copy-done.23, bf16[256,256]{1,0:T(8,128)(2,1)S(1)} %copy-done.22, ...), custom_call_target="tpu_custom_call" | custom-call | flops 939524096 | bytes 8912896 | tf_op jit(solution)/shard_map/pallas_call | solution.py:345
  151.7 5.5 %collective-permute-done.32.first.refs_8_ = bf16[64,4096]{1,0:T(8,128)(2,1)} collective-permute-done((bf16[64,4096]{1,0:T(8,128)(2,1)S(1)}, bf16[64,4096]{1,0:T(8,128)(2,1)}, u32[]{:S(2)}, u32[]{:S(2)}) %collective-permute-start.32) | collective-permute-done | bytes 524320 | tf_op jit(solution)/shard_map/ppermute | solution.py:470
  165.3 4.3 %collective-permute-start.38 = (bf16[128,256]{1,0:T(8,128)(2,1)S(1)}, bf16[128,256]{1,0:T(8,128)(2,1)S(1)}, u32[]{:S(2)}, u32[]{:S(2)}) collective-permute-start(bf16[128,256]{1,0:T(8,128)(2,1)S(1)} %get-tuple-element.125), channel_id=1, source_target_pairs={{0,2},{1,3},{2,0},{3,1},{4,6},{5,7},{6,4},{7,5},{8,10},{9,11},{10,... | collective-permute-start | bytes 196616 | tf_op jit(solution)/shard_map/ppermute | solution.py:491
  171.5 5.1 %shard_map.273 = (bf16[128,4096]{1,0:T(8,128)(2,1)}, f32[128,4096]{1,0:T(8,128)}, bf16[2,128,512]{2,1,0:T(8,128)(2,1)}, f32[4,8,128,128]{3,2,1,0:T(8,128)}) custom-call(s32[4]{0:T(128)S(1)} %pad_add_fusion.scalars, bf16[256,256]{1,0:T(8,128)(2,1)S(1)} %copy-done.26, ...), custom_call_target="tpu_custom_call", output_to_operand_aliasing={{0}: (17, {}), {1}: (18, {}), {3}: (19, {})} | custom-call | flops 469762048 | bytes 4456448 | tf_op jit(solution)/shard_map/pallas_call | solution.py:345
  176.6 3.8 %shard_map.274 = (bf16[128,256]{1,0:T(8,128)(2,1)S(1)}, bf16[128,256]{1,0:T(8,128)(2,1)S(1)}) custom-call(s32[1]{0:T(128)} %bitcast.scalars, bf16[128,4096]{1,0:T(8,128)(2,1)S(1)} %copy-done, bf16[128,4096]{1,0:T(8,128)(2,1)S(1)} %collective-permute-done.2.cot_away, bf16[64,4096]{1,0:T(8,128)(2,1)} %collective-permute-done.32.first.refs_8_, ...), custom_call_target="tpu_custom_call" | custom-call | flops 536870912 | bytes 4194304 | tf_op jit(solution)/shard_map/pallas_call | solution.py:210
  181.7 8.0 %shard_map.275 = (f32[128,4096]{1,0:T(8,128)}, bf16[128,4096]{1,0:T(8,128)(2,1)}) custom-call(s32[7]{0:T(128)S(1)} %stack.122.scalars, bf16[128,2048]{1,0:T(8,128)(2,1)} %get-tuple-element.168.gated_own, bf16[128,2048]{1,0:T(8,128)(2,1)} %collective-permute-done.26.gated_away, bf16[64,4096]{1,0:T(8,128)(2,1)} %collective-permute-done.20.first.refs_0_, ...), custom_call_target="tpu_custom_call" | custom-call | flops 1610612736 | bytes 11534336 | tf_op jit(solution)/shard_map/pallas_call | solution.py:273
  189.7 5.0 %shard_map.276 = (bf16[128,4096]{1,0:T(8,128)(2,1)}, f32[128,4096]{1,0:T(8,128)}, bf16[2,128,512]{2,1,0:T(8,128)(2,1)}, f32[4,8,128,128]{3,2,1,0:T(8,128)}) custom-call(s32[4]{0:T(128)S(1)} %pad_add_fusion.2.scalars, bf16[256,256]{1,0:T(8,128)(2,1)S(1)} %copy-done.26, ...), custom_call_target="tpu_custom_call", output_to_operand_aliasing={{0}: (17, {}), {1}: (18, {}), {3}: (19, {})} | custom-call | flops 469762048 | bytes 4456448 | tf_op jit(solution)/shard_map/pallas_call | solution.py:345
  204.3 5.4 %collective-permute-done.45 = bf16[1,8,128,128]{3,2,1,0:T(8,128)(2,1)S(1)} collective-permute-done((bf16[1,8,128,128]{3,2,1,0:T(8,128)(2,1)S(1)}, bf16[1,8,128,128]{3,2,1,0:T(8,128)(2,1)S(1)}, u32[]{:S(2)}, u32[]{:S(2)}) %collective-permute-start.45) | collective-permute-done | bytes 262176 | tf_op jit(solution)/shard_map/ppermute | solution.py:75
  209.9 3.9 %collective-permute-start.42 = (bf16[2,128,512]{2,1,0:T(8,128)(2,1)}, bf16[2,128,512]{2,1,0:T(8,128)(2,1)S(1)}, u32[]{:S(2)}, u32[]{:S(2)}) collective-permute-start(bf16[2,128,512]{2,1,0:T(8,128)(2,1)} %get-tuple-element.131), channel_id=1, source_target_pairs={{1,0},{2,1},{3,2},{4,3},{5,4},{6,5},{7,6},{8,7},{9,8},{10,9},{11,1... | collective-permute-start | bytes 786440 | tf_op jit(solution)/shard_map/ppermute | solution.py:504
  217.1 18.4 %collective-permute-done.42.refs_1_ = bf16[2,128,512]{2,1,0:T(8,128)(2,1)S(1)} collective-permute-done((bf16[2,128,512]{2,1,0:T(8,128)(2,1)}, bf16[2,128,512]{2,1,0:T(8,128)(2,1)S(1)}, u32[]{:S(2)}, u32[]{:S(2)}) %collective-permute-start.42) | collective-permute-done | bytes 262176 | tf_op jit(solution)/shard_map/ppermute | solution.py:504
  238.3 7.2 %shard_map.277 = (bf16[128,4096]{1,0:T(8,128)(2,1)}, bf16[128,4096]{1,0:T(8,128)(2,1)}) custom-call(s32[32]{0:T(128)S(1)} %select_n.130.scalars, f32[128,4096]{1,0:T(8,128)} %get-tuple-element.151.near, bf16[128,4096]{1,0:T(8,128)(2,1)} %keys.1, bf16[128,4096]{1,0:T(8,128)(2,1)} %values.1, bf16[4,128,512]{2,1,0:T(8,128)(2,1)} %collective-permute-done.39.refs_0_, ...), custom_call_target="tpu_custom_call" | custom-call | flops 2097152 | bytes 7340032 | tf_op jit(solution)/shard_map/pallas_call | solution.py:403
  (228 shorter events, 94.4 us)
Async XLA Ops:
  0.6 27.8 %collective-permute-start.5 = (bf16[128,4096]{1,0:T(8,128)(2,1)}, bf16[128,4096]{1,0:T(8,128)(2,1)}, u32[]{:S(2)}, u32[]{:S(2)}) collective-permute-start(bf16[128,4096]{1,0:T(8,128)(2,1)} %param.27), channel_id=1, source_target_pairs={{0,1},{1,0},{2,3},{3,2},{4,5},{5,4},{6,7},{7,6},{8,9},{9,8},{10,11... | collective-permute-start | bytes 3145736 | tf_op jit(solution)/shard_map/ppermute | solution.py:438
  0.8 26.3 %collective-permute-start.2 = (bf16[128,4096]{1,0:T(8,128)(2,1)}, bf16[128,4096]{1,0:T(8,128)(2,1)S(1)}, u32[]{:S(2)}, u32[]{:S(2)}) collective-permute-start(bf16[128,4096]{1,0:T(8,128)(2,1)} %cot_own.15), channel_id=1, source_target_pairs={{0,2},{1,3},{2,0},{3,1},{4,6},{5,7},{6,4},{7,5},{8,10},{9,11},{10,... | collective-permute-start | bytes 3145736 | tf_op jit(solution)/shard_map/ppermute | solution.py:437
  4.7 13.3 %collective-permute-start.1 = (bf16[64,4096]{1,0:T(8,128)(2,1)S(1)}, bf16[64,4096]{1,0:T(8,128)(2,1)}, u32[]{:S(2)}, u32[]{:S(2)}) collective-permute-start(bf16[64,4096]{1,0:T(8,128)(2,1)S(1)} %get-tuple-element.171.second.refs_2_), channel_id=1, source_target_pairs={{8,0},{9,1},{10,2},{11,3},{16,8},{17,9},{18,10},{19,11},{24,16},{2... | collective-permute-start | bytes 1572872 | tf_op jit(solution)/shard_map/ppermute | solution.py:470
  6.0 14.4 %collective-permute-start = (bf16[64,4096]{1,0:T(8,128)(2,1)S(1)}, bf16[64,4096]{1,0:T(8,128)(2,1)}, u32[]{:S(2)}, u32[]{:S(2)}) collective-permute-start(bf16[64,4096]{1,0:T(8,128)(2,1)S(1)} %get-tuple-element.172.first.refs_0_), channel_id=1, source_target_pairs={{0,8},{1,9},{2,10},{3,11},{8,16},{9,17},{10,18},{11,19},{16,24},{1... | collective-permute-start | bytes 1572872 | tf_op jit(solution)/shard_map/ppermute | solution.py:470
  18.0 18.8 %collective-permute-start.8 = (bf16[64,4096]{1,0:T(8,128)(2,1)}, bf16[64,4096]{1,0:T(8,128)(2,1)S(1)}, u32[]{:S(2)}, u32[]{:S(2)}) collective-permute-start(bf16[64,4096]{1,0:T(8,128)(2,1)} %collective-permute-done.1.second.refs_6_), channel_id=1, source_target_pairs={{0,1},{1,0},{2,3},{3,2},{4,5},{5,4},{6,7},{7,6},{8,9},{9,8},{10,11... | collective-permute-start | bytes 1572872 | tf_op jit(solution)/shard_map/ppermute | solution.py:472
  19.2 22.8 %collective-permute-start.4 = (bf16[64,4096]{1,0:T(8,128)(2,1)}, bf16[64,4096]{1,0:T(8,128)(2,1)S(1)}, u32[]{:S(2)}, u32[]{:S(2)}) collective-permute-start(bf16[64,4096]{1,0:T(8,128)(2,1)} %collective-permute-done.1.second.refs_6_), channel_id=1, source_target_pairs={{8,0},{9,1},{10,2},{11,3},{16,8},{17,9},{18,10},{19,11},{24,16},{2... | collective-permute-start | bytes 1572872 | tf_op jit(solution)/shard_map/ppermute | solution.py:470
  20.4 16.4 %collective-permute-start.7 = (bf16[64,4096]{1,0:T(8,128)(2,1)}, bf16[64,4096]{1,0:T(8,128)(2,1)S(1)}, u32[]{:S(2)}, u32[]{:S(2)}) collective-permute-start(bf16[64,4096]{1,0:T(8,128)(2,1)} %collective-permute-done.first.refs_4_), channel_id=1, source_target_pairs={{0,1},{1,0},{2,3},{3,2},{4,5},{5,4},{6,7},{7,6},{8,9},{9,8},{10,11... | collective-permute-start | bytes 1572872 | tf_op jit(solution)/shard_map/ppermute | solution.py:471
  27.1 15.0 %collective-permute-start.3 = (bf16[64,4096]{1,0:T(8,128)(2,1)}, bf16[64,4096]{1,0:T(8,128)(2,1)S(1)}, u32[]{:S(2)}, u32[]{:S(2)}) collective-permute-start(bf16[64,4096]{1,0:T(8,128)(2,1)} %collective-permute-done.first.refs_4_), channel_id=1, source_target_pairs={{0,8},{1,9},{2,10},{3,11},{8,16},{9,17},{10,18},{11,19},{16,24},{1... | collective-permute-start | bytes 1572872 | tf_op jit(solution)/shard_map/ppermute | solution.py:470
  28.5 43.2 %collective-permute-start.25 = (bf16[128,4096]{1,0:T(8,128)(2,1)}, bf16[128,4096]{1,0:T(8,128)(2,1)}, u32[]{:S(2)}, u32[]{:S(2)}) collective-permute-start(bf16[128,4096]{1,0:T(8,128)(2,1)} %multiply_convert_fusion.product), channel_id=1, source_target_pairs={{0,1},{1,2},{2,3},{3,4},{4,5},{5,6},{6,7},{7,8},{8,9},{9,10},{10,1... | collective-permute-start | bytes 3145736 | tf_op jit(solution)/shard_map/ppermute | solution.py:440
  60.6 21.5 %collective-permute-start.17 = (bf16[64,4096]{1,0:T(8,128)(2,1)}, bf16[64,4096]{1,0:T(8,128)(2,1)}, u32[]{:S(2)}, u32[]{:S(2)}) collective-permute-start(bf16[64,4096]{1,0:T(8,128)(2,1)} %collective-permute-done.10.first.refs_12_), channel_id=1, source_target_pairs={{0,1},{1,0},{2,3},{3,2},{4,5},{5,4},{6,7},{7,6},{8,9},{9,8},{10,11... | collective-permute-start | bytes 1572872 | tf_op jit(solution)/shard_map/ppermute | solution.py:471
  61.9 20.2 %collective-permute-start.18 = (bf16[64,4096]{1,0:T(8,128)(2,1)}, bf16[64,4096]{1,0:T(8,128)(2,1)}, u32[]{:S(2)}, u32[]{:S(2)}) collective-permute-start(bf16[64,4096]{1,0:T(8,128)(2,1)} %collective-permute-done.11.second.refs_14_), channel_id=1, source_target_pairs={{0,1},{1,0},{2,3},{3,2},{4,5},{5,4},{6,7},{7,6},{8,9},{9,8},{10,11... | collective-permute-start | bytes 1572872 | tf_op jit(solution)/shard_map/ppermute | solution.py:472
  62.5 24.1 %collective-permute-start.15 = (bf16[64,4096]{1,0:T(8,128)(2,1)}, bf16[64,4096]{1,0:T(8,128)(2,1)}, u32[]{:S(2)}, u32[]{:S(2)}) collective-permute-start(bf16[64,4096]{1,0:T(8,128)(2,1)} %collective-permute-done.10.first.refs_12_), channel_id=1, source_target_pairs={{0,8},{1,9},{2,10},{3,11},{8,16},{9,17},{10,18},{11,19},{16,24},{1... | collective-permute-start | bytes 1572872 | tf_op jit(solution)/shard_map/ppermute | solution.py:470
  69.7 17.2 %collective-permute-start.16 = (bf16[64,4096]{1,0:T(8,128)(2,1)}, bf16[64,4096]{1,0:T(8,128)(2,1)}, u32[]{:S(2)}, u32[]{:S(2)}) collective-permute-start(bf16[64,4096]{1,0:T(8,128)(2,1)} %collective-permute-done.11.second.refs_14_), channel_id=1, source_target_pairs={{8,0},{9,1},{10,2},{11,3},{16,8},{17,9},{18,10},{19,11},{24,16},{2... | collective-permute-start | bytes 1572872 | tf_op jit(solution)/shard_map/ppermute | solution.py:470
  92.4 14.7 %collective-permute-start.26 = (bf16[128,2048]{1,0:T(8,128)(2,1)}, bf16[128,2048]{1,0:T(8,128)(2,1)}, u32[]{:S(2)}, u32[]{:S(2)}) collective-permute-start(bf16[128,2048]{1,0:T(8,128)(2,1)} %get-tuple-element.167), channel_id=1, source_target_pairs={{0,2},{1,3},{2,0},{3,1},{4,6},{5,7},{6,4},{7,5},{8,10},{9,11},{10,... | collective-permute-start | bytes 1572872 | tf_op jit(solution)/shard_map/ppermute | solution.py:482
  97.1 18.7 %collective-permute-start.24 = (bf16[128,256]{1,0:T(8,128)(2,1)S(1)}, bf16[128,256]{1,0:T(8,128)(2,1)S(1)}, u32[]{:S(2)}, u32[]{:S(2)}) collective-permute-start(bf16[128,256]{1,0:T(8,128)(2,1)S(1)} %get-tuple-element.100), channel_id=1, source_target_pairs={{0,2},{1,3},{2,0},{3,1},{4,6},{5,7},{6,4},{7,5},{8,10},{9,11},{10,... | collective-permute-start | bytes 196616 | tf_op jit(solution)/shard_map/ppermute | solution.py:491
  102.6 15.3 %collective-permute-start.29 = (bf16[64,4096]{1,0:T(8,128)(2,1)}, bf16[64,4096]{1,0:T(8,128)(2,1)S(1)}, u32[]{:S(2)}, u32[]{:S(2)}) collective-permute-start(bf16[64,4096]{1,0:T(8,128)(2,1)} %collective-permute-done.20.first.refs_0_), channel_id=1, source_target_pairs={{0,1},{1,0},{2,3},{3,2},{4,5},{5,4},{6,7},{7,6},{8,9},{9,8},{10,11... | collective-permute-start | bytes 1572872 | tf_op jit(solution)/shard_map/ppermute | solution.py:471
  147.0 14.6 %collective-permute-start.36 = (bf16[64,4096]{1,0:T(8,128)(2,1)S(1)}, bf16[64,4096]{1,0:T(8,128)(2,1)}, u32[]{:S(2)}, u32[]{:S(2)}) collective-permute-start(bf16[64,4096]{1,0:T(8,128)(2,1)S(1)} %collective-permute-done.27.first.refs_4_), channel_id=1, source_target_pairs={{0,1},{1,0},{2,3},{3,2},{4,5},{5,4},{6,7},{7,6},{8,9},{9,8},{10,11... | collective-permute-start | bytes 1572872 | tf_op jit(solution)/shard_map/ppermute | solution.py:471
  149.2 27.3 %collective-permute-start.39 = (bf16[4,128,512]{2,1,0:T(8,128)(2,1)}, bf16[4,128,512]{2,1,0:T(8,128)(2,1)}, u32[]{:S(2)}, u32[]{:S(2)}) collective-permute-start(bf16[4,128,512]{2,1,0:T(8,128)(2,1)} %get-tuple-element.119), channel_id=1, source_target_pairs={{1,0},{2,1},{3,2},{4,3},{5,4},{6,5},{7,6},{8,7},{9,8},{10,9},{11,1... | collective-permute-start | bytes 1572872 | tf_op jit(solution)/shard_map/ppermute | solution.py:504
  157.1 19.5 %collective-permute-start.33 = (bf16[64,4096]{1,0:T(8,128)(2,1)}, bf16[64,4096]{1,0:T(8,128)(2,1)}, u32[]{:S(2)}, u32[]{:S(2)}) collective-permute-start(bf16[64,4096]{1,0:T(8,128)(2,1)} %collective-permute-done.32.first.refs_8_), channel_id=1, source_target_pairs={{0,1},{1,0},{2,3},{3,2},{4,5},{5,4},{6,7},{7,6},{8,9},{9,8},{10,11... | collective-permute-start | bytes 1572872 | tf_op jit(solution)/shard_map/ppermute | solution.py:471
  159.8 16.8 %collective-permute-start.35 = (bf16[64,4096]{1,0:T(8,128)(2,1)}, bf16[64,4096]{1,0:T(8,128)(2,1)}, u32[]{:S(2)}, u32[]{:S(2)}) collective-permute-start(bf16[64,4096]{1,0:T(8,128)(2,1)} %collective-permute-done.34.second.refs_10_), channel_id=1, source_target_pairs={{0,1},{1,0},{2,3},{3,2},{4,5},{5,4},{6,7},{7,6},{8,9},{9,8},{10,11... | collective-permute-start | bytes 1572872 | tf_op jit(solution)/shard_map/ppermute | solution.py:472
  202.8 42.7 %collective-permute-start.41 = (bf16[128,4096]{1,0:T(8,128)(2,1)}, bf16[128,4096]{1,0:T(8,128)(2,1)S(1)}, u32[]{:S(2)}, u32[]{:S(2)}) collective-permute-start(bf16[128,4096]{1,0:T(8,128)(2,1)} %get-tuple-element.142), channel_id=1, source_target_pairs={{0,2},{1,3},{2,0},{3,1},{4,6},{5,7},{6,4},{7,5},{8,10},{9,11},{10,... | collective-permute-start | bytes 3145736 | tf_op jit(solution)/shard_map/ppermute | solution.py:508
  209.9 25.6 %collective-permute-start.42 = (bf16[2,128,512]{2,1,0:T(8,128)(2,1)}, bf16[2,128,512]{2,1,0:T(8,128)(2,1)S(1)}, u32[]{:S(2)}, u32[]{:S(2)}) collective-permute-start(bf16[2,128,512]{2,1,0:T(8,128)(2,1)} %get-tuple-element.131), channel_id=1, source_target_pairs={{1,0},{2,1},{3,2},{4,3},{5,4},{6,5},{7,6},{8,7},{9,8},{10,9},{11,1... | collective-permute-start | bytes 786440 | tf_op jit(solution)/shard_map/ppermute | solution.py:504
  213.8 24.5 %collective-permute-start.43 = (bf16[2,128,512]{2,1,0:T(8,128)(2,1)}, bf16[2,128,512]{2,1,0:T(8,128)(2,1)S(1)}, u32[]{:S(2)}, u32[]{:S(2)}) collective-permute-start(bf16[2,128,512]{2,1,0:T(8,128)(2,1)} %get-tuple-element.153), channel_id=1, source_target_pairs={{1,0},{2,1},{3,2},{4,3},{5,4},{6,5},{7,6},{8,7},{9,8},{10,9},{11,1... | collective-permute-start | bytes 786440 | tf_op jit(solution)/shard_map/ppermute | solution.py:504
  215.8 29.7 %collective-permute-start.47 = (bf16[2,128,128]{2,1,0:T(8,128)(2,1)S(1)}, bf16[2,128,128]{2,1,0:T(8,128)(2,1)S(1)}, u32[]{:S(2)}, u32[]{:S(2)}) collective-permute-start(bf16[2,128,128]{2,1,0:T(8,128)(2,1)S(1)} %fusion.1), channel_id=1, source_target_pairs={{0,8},{1,9},{2,10},{3,11},{4,12},{5,13},{6,14},{7,15},{8,0},{9,1},... | collective-permute-start | bytes 196616 | tf_op jit(solution)/shard_map/ppermute | solution.py:75
  (79 other events, 639.1 us)

commit v7 on v1

v7 whole, which is shorter than its diff:
```python
import functools

import jax
import jax.numpy as jnp
import numpy as np
from jax import lax
from jax.experimental import pallas as pl
from jax.experimental.pallas import tpu as pltpu
from jax.sharding import PartitionSpec as P

F32 = jnp.float32
BF16 = jnp.bfloat16
GRANT = 16 << 20


def spectrum_table(length):
    angles = np.pi * (2 * np.arange(length)[:, None] + 1) * np.arange(-length, length)[None, :] / (2 * length)
    table = np.concatenate([np.cos(angles), -np.sin(angles)], 0).astype(np.float32)
    high = table.astype(BF16)
    low = (table - high.astype(np.float32)).astype(BF16)
    return table, high, low


def forward_dft(high, low, data, dims):
    first = lax.dot_general(high, data, (dims, ((), ())), preferred_element_type=F32)
    second = lax.dot_general(low, data, (dims, ((), ())), preferred_element_type=F32)
    return first + second


def times(a, b):
    half = a.shape[0] // 2
    ar, ai, br, bi = a[:half], a[half:], b[:half], b[half:]
    return jnp.concatenate([ar * br - ai * bi, ar * bi + ai * br], 0)


def times_conj(a, b):
    half = a.shape[0] // 2
    ar, ai, br, bi = a[:half], a[half:], b[:half], b[half:]
    return jnp.concatenate([ar * br + ai * bi, ai * br - ar * bi], 0)


def inverse_dft(table, spectrum, scale):
    done = lax.dot_general(
        table, spectrum, (((0,), (0,)), ((), ())), precision=lax.Precision.HIGH, preferred_element_type=F32
    )
    return done * scale


def mul(a, b):
    return (a.astype(F32) * b.astype(F32)).astype(BF16)


def pick(data, width, side):
    blocks = [data[:, i : i + width] for i in range(0, data.shape[1], width)]
    return jnp.concatenate([jnp.where(side == 0, a, b) for a, b in zip(blocks[::2], blocks[1::2])], 1)


def scatter_sum(part, nseq, place, order):
    share = part.shape[1] // nseq
    bits = nseq.bit_length() - 1
    if nseq != 1 << bits:
        return lax.psum_scatter(part, "seq", scatter_dimension=1, tiled=True)
    left = list(range(bits))
    for step in [b for b in order if b < bits] + [b for b in range(bits) if b not in order]:
        width = share << sum(b < step for b in left)
        left.remove(step)
        mine = (place >> step) & 1
        away = pick(part, width, 1 - mine)
        if step:
            away = away.astype(BF16)
        away = lax.ppermute(away, "seq", [(i, i ^ (1 << step)) for i in range(nseq)])
        part = pick(part, width, mine) + away.astype(F32)
    return part


def sum_over_ring(part, nseq, place):
    core, pair, row = place & 1, (place >> 1) & 1, place >> 2
    lags, chans = part.shape
    size, chans = nseq // 4, chans // nseq

    def halve(part, bit, mine, kind):
        away = lax.dynamic_index_in_dim(part, 1 - mine, 1, False).astype(kind)
        away = lax.ppermute(away, "seq", [(i, i ^ bit) for i in range(nseq)])
        return lax.dynamic_index_in_dim(part, mine, 1, False) + away.astype(F32)

    kept, away = deal(core.astype(jnp.int32), part, chans, 2)
    part = kept + lax.ppermute(away, "seq", [(i, i ^ 1) for i in range(nseq)])
    part = halve(part.reshape(1, 2, size, lags, chans), 2, pair, BF16).reshape(size, lags, chans)
    left = size
    while left > 1:
        bit = size // left
        part = halve(part.reshape(left // 2, 2, lags, chans), 4 * bit, (row // bit) & 1, BF16)
        left //= 2
    return part.reshape(lags, chans)


def links(seg_ids, place):
    own = lax.dynamic_index_in_dim(seg_ids, place, 0, False)
    prior = lax.dynamic_index_in_dim(seg_ids, jnp.maximum(place - 1, 0), 0, False)
    return (place > 0) & (own == prior)


def gathered_products(gated, cotangent, w_out):
    weights = lax.all_gather(w_out, "seq", axis=0, tiled=True)
    grad_gated = lax.dot_general(cotangent, weights, (((1,), (1,)), ((), ())), preferred_element_type=F32)
    grad_gated = lax.psum_scatter(grad_gated, "tp", scatter_dimension=1, tiled=True).astype(BF16)
    outputs = jnp.dot(
        lax.all_gather(gated, "tp", axis=1, tiled=True), weights, preferred_element_type=F32
    ).astype(BF16)
    return grad_gated, outputs


def ring_place(step, size):
    half = (size + 1) // 2
    return jnp.where(step < half, 2 * step, 2 * (size - 1 - step) + 1)


def ring_step(row, size):
    return jnp.where(row & 1 == 0, row >> 1, size - 1 - (row >> 1))


def place_kernel(count, scalars, *refs):
    pieces, out_ref = refs[: 4 * count], refs[-1]
    width = out_ref.shape[0]
    half = width // 2
    for i in range(4 * count):
        if i % 4 < 2:
            first, second = pieces[i], pieces[i + 2]
            for k in (0, 1):
                at = pl.ds(pl.multiple_of(scalars[4 * (i // 4) + 2 * (i % 4) + k] * width, width), width)
                out_ref[:, at] = jnp.concatenate(
                    [first[:, k * half : (k + 1) * half], second[:, (2 + k) * half : (3 + k) * half]], 1
                )


def place_pieces(scalars, groups, chans):
    pieces = [p for group in groups for p in group]
    rows = pieces[0].shape[0]
    vmem = pl.BlockSpec(memory_space=pltpu.VMEM)
    return pl.pallas_call(
        functools.partial(place_kernel, len(groups)),
        out_shape=jax.ShapeDtypeStruct((rows, chans), BF16),
        in_specs=[pl.BlockSpec(memory_space=pltpu.SMEM)] + [vmem] * len(pieces),
        out_specs=vmem,
        compiler_params=pltpu.CompilerParams(vmem_limit_bytes=16 << 20),
        cost_estimate=pl.CostEstimate(flops=0, bytes_accessed=4 * rows * chans, transcendentals=0),
    )(scalars, *pieces)


def deal_kernel(sides, scalars, data, kept, away):
    width = kept.shape[-1]
    for i in range(data.shape[1] // (2 * width)):
        for ref, side in ((kept, scalars[0]), (away, 1 - scalars[0])):
            block = data[:, pl.ds(pl.multiple_of((2 * i + side) * width, width), width)]
            if sides:
                ref[i % sides, i // sides] = block
            else:
                ref[i] = block


def deal(side, data, width, sides=0):
    rows, chans = data.shape
    count = chans // (2 * width)
    lead = (sides, count // sides) if sides else (count,)
    out = jax.ShapeDtypeStruct(lead + (rows, width), data.dtype)
    vmem = pl.BlockSpec(memory_space=pltpu.VMEM)
    return pl.pallas_call(
        functools.partial(deal_kernel, sides),
        out_shape=(out, out),
        in_specs=[pl.BlockSpec(memory_space=pltpu.SMEM), vmem],
        out_specs=(vmem, vmem),
        compiler_params=pltpu.CompilerParams(vmem_limit_bytes=GRANT),
        cost_estimate=pl.CostEstimate(flops=0, bytes_accessed=8 * rows * chans, transcendentals=0),
    )(side.reshape(1), data)


def dot(a, b):
    return jnp.dot(a, b, preferred_element_type=F32)


def project_kernel(count, first, last, scalars, gated_own, gated_away, *refs):
    weights, refs = refs[:count], refs[count:]
    width = weights[0].shape[0]
    depth = width // 4
    left, total = refs[-2:]

    def arrange(order):
        for i in range(count):
            for part, ref in enumerate((gated_own, gated_away)):
                blocks = [ref[scalars[1 + 2 * i + way]] for way in (0, 1)]
                rows = ref.shape[1]
                left[i, part * rows : (part + 1) * rows] = jnp.concatenate(
                    [blocks[way][:, (2 * k + way) * depth : (2 * k + way + 1) * depth] for way in (0, 1) for k in order],
                    1,
                )

    @pl.when((pl.program_id(0) == 0) & (scalars[0] == 0))
    def _():
        arrange((0, 1))

    @pl.when((pl.program_id(0) == 0) & (scalars[0] != 0))
    def _():
        arrange((1, 0))

    total[...] = dot(left[0], weights[0][...]) + (0.0 if first else refs[0][...])
    for i in range(1, count):
        total[...] += dot(left[i], weights[i][...])
    if last:
        own_ref, away_ref = refs[-4:-2]
        rows = own_ref.shape[0]
        own_ref[...] = total[:rows]
        away_ref[...] = total[rows:].astype(BF16)
    else:
        refs[-3][...] = total[...]


def project(scalars, gated_own, gated_away, weights, before=None, last=False):
    rows = gated_own.shape[1]
    depth, feats = weights[0].shape
    tile = min(1024, feats)
    whole = pl.BlockSpec((2 * rows, tile), lambda j, s: (0, j))
    block = pl.BlockSpec((rows, tile), lambda j, s: (0, j))
    halves = tuple(jax.ShapeDtypeStruct((rows, feats), kind) for kind in (F32, BF16))
    return pl.pallas_call(
        functools.partial(project_kernel, len(weights), before is None, last),
        out_shape=halves if last else jax.ShapeDtypeStruct((2 * rows, feats), F32),
        grid_spec=pltpu.PrefetchScalarGridSpec(
            num_scalar_prefetch=1,
            grid=(feats // tile,),
            in_specs=[pl.BlockSpec(gated_own.shape, lambda j, s: (0, 0, 0))] * 2
            + [pl.BlockSpec((depth, tile), lambda j, s: (0, j))] * len(weights)
            + [whole] * (before is not None),
            out_specs=(block, block) if last else whole,
            scratch_shapes=[
                pltpu.VMEM((len(weights), 2 * rows, depth), BF16),
                pltpu.VMEM((2 * rows, tile), F32),
            ],
        ),
        compiler_params=pltpu.CompilerParams(vmem_limit_bytes=GRANT),
        cost_estimate=pl.CostEstimate(
            flops=4 * rows * depth * len(weights) * feats,
            bytes_accessed=2 * depth * feats * len(weights) + 4 * gated_own.size + 8 * rows * feats,
            transcendentals=0,
        ),
    )(scalars, gated_own, gated_away, *weights, *([] if before is None else [before]))


def on_ring(queries, keys, values, w_out, taps, seg_ids, cotangent):
    rows, chans = queries.shape
    length = rows
    nseq = lax.axis_size("seq")
    place = lax.axis_index("seq")
    size = nseq // 4
    core, pair, row = [i.astype(jnp.int32) for i in (place & 1, (place >> 1) & 1, place >> 2)]
    at = ring_step(row, size)
    swap_core = [(i, i ^ 1) for i in range(nseq)]
    swap_pair = [(i, i ^ 2) for i in range(nseq)]
    walk = list(range(0, size, 2)) + list(range(1, size, 2))[::-1]
    onward = [(4 * walk[i] + k, 4 * walk[(i + 1) % size] + k) for i in range(size) for k in range(4)]
    backward = [(b, a) for a, b in onward]
    later = [(i, i + 1) for i in range(nseq - 1)]
    earlier = [(i + 1, i) for i in range(nseq - 1)]
    send = functools.partial(lax.ppermute, axis_name="seq")
    tie = lax.optimization_barrier
    linked = links(seg_ids, place)
    table, high, low = spectrum_table(length)
    table_now, high_now, low_now = table[:, length:], high[:, length:], low[:, length:]
    scale = 1.0 / length

    half = rows // 2
    first, second = w_out[:half], w_out[half:]
    cot_away = send(cotangent, perm=swap_pair)
    swapped = send(w_out, perm=swap_core)
    product, cot_away = tie((mul(keys, values), cot_away))
    before = send(product, perm=later)
    filt = forward_dft(high_now, low_now, tie(taps.T), ((1,), (0,)))

    block = [ring_place(lax.rem(at - s + size, size), size) for s in range(size)]
    middle = min(2, size - 1)
    cuts = [range(0, max(size // 2, 1)), range(max(size // 2, 1), size - 1), range(size - 1, size)]
    weights, own, away = [None] * size, [None] * size, [None] * size
    fresh = []
    sums = None
    dims = (((1,), (1,)), ((), ()))

    def product_of(step, parts):
        weights[step] = jnp.concatenate(parts, 0)
        grad = lax.dot_general(cot_pair, weights[step], dims, preferred_element_type=F32).astype(BF16)
        own[step], away[step] = grad[:rows], send(grad[rows:], perm=swap_pair)
        fresh.append(step)

    def projected(steps, sums, last):
        places = [b for s in steps for b in (block[s], block[(size - s) % size])]
        scalars = jnp.stack([core] + places)
        return project(scalars, gated_own, gated_away, [weights[s] for s in steps], sums, last)

    waiting = [(first, swapped[:half], second, swapped[half:])]
    for step in range(1, size):
        due = fresh[:-1] if step < size - 1 else fresh[:]
        for s in due:
            first, second, own[s], away[s] = tie((first, second, own[s], away[s]))
        fresh = fresh[len(due) :]
        if step == size - 1 and sums is not None:
            first, second, sums = tie((first, second, sums))
        first, second = send(first, perm=onward), send(second, perm=backward)
        waiting.append((first, send(first, perm=swap_core), second, send(second, perm=swap_core)))
        if step < middle:
            continue
        if step == middle:
            _, _, cot_away, before = tie((first, second, cot_away, before))
            cot_pair = jnp.concatenate([cotangent, cot_away], 0)
        if step == size - 1 and sums is not None and len(cuts[1]):
            sums = projected(cuts[1], sums, False)
            waiting[-1], sums = tie((waiting[-1], sums))
        for s, parts in enumerate(waiting, step + 1 - len(waiting)):
            product_of(s, parts if s < step else tie(parts))
        waiting = []
        if step == middle:
            before = jnp.where(linked, before, jnp.zeros_like(before))
            data = forward_dft(high, low, jnp.concatenate([before, product], 0), ((1,), (0,)))
            filtered = inverse_dft(table_now, times(filt, data), scale).astype(BF16)
            gated = mul(queries, filtered)
            width = chans // (2 * size)
            gated_own, gated_away = deal(pair, gated, width)
            gated_away = send(gated_away, perm=swap_pair)
        if step == max(cuts[0][-1] + 1, middle) and step < size - 1:
            sums = projected(cuts[0], None, False)
        if step == size - 1:
            sums = projected(cuts[2] if sums is not None else range(size), sums, True)
            away[step], sums = tie((away[step], sums))

    out_own, out_away = sums
    out_away = send(out_away, perm=swap_pair)
    groups, places = [], []
    for s in range(size):
        m = (size - s) % size
        groups.append((own[s], away[s], own[m], away[m]))
        for side in (pair, 1 - pair):
            places += [4 * block[s] + 2 * side + core, 4 * block[s] + 2 * side + 1 - core]
    grad_gated = place_pieces(jnp.stack(places), groups, chans)
    grad_queries = mul(grad_gated, filtered)
    grad_filtered = mul(grad_gated, queries)
    grads = forward_dft(high_now, low_now, grad_filtered, ((1,), (0,)))
    back = inverse_dft(table, times_conj(grads, filt), scale)
    across = jnp.where(linked, back[:length], 0.0).astype(BF16)
    ahead = send(across, perm=earlier)
    taps_part = inverse_dft(table_now, times_conj(grads, data), scale)
    taps_grad = sum_over_ring(taps_part, nseq, place).T
    outputs = (out_own + out_away.astype(F32)).astype(BF16)
    grad_product = (back[length:] + ahead.astype(F32)).astype(BF16)
    grad_keys = mul(grad_product, values)
    grad_values = mul(grad_product, keys)
    return (outputs, grad_queries, grad_keys, grad_values, taps_grad)


def on_device(queries, keys, values, w_out, taps, seg_ids, cotangent):
    rows, chans = queries.shape
    length = taps.shape[1]
    assert rows == length
    nseq = lax.axis_size("seq")
    place = lax.axis_index("seq")
    table, high, low = spectrum_table(length)
    table_now, high_now, low_now = table[:, length:], high[:, length:], low[:, length:]
    scale = 1.0 / length
    later = [(i, i + 1) for i in range(nseq - 1)]
    earlier = [(i + 1, i) for i in range(nseq - 1)]
    linked = links(seg_ids, place)

    product = mul(keys, values)
    before = lax.ppermute(product, "seq", later)
    before = jnp.where(linked, before, jnp.zeros_like(before))
    data = forward_dft(high, low, jnp.concatenate([before, product], 0), ((1,), (0,)))
    filt = forward_dft(high_now, low_now, taps, ((1,), (1,)))
    filtered = inverse_dft(table_now, times(filt, data), scale).astype(BF16)
    gated = mul(queries, filtered)

    grad_gated, outputs = gathered_products(gated, cotangent, w_out)
    grad_queries = mul(grad_gated, filtered)
    grad_filtered = mul(grad_gated, queries)
    grads = forward_dft(high_now, low_now, grad_filtered, ((1,), (0,)))
    back = inverse_dft(table, times_conj(grads, filt), scale)
    across = jnp.where(linked, back[:length], 0.0).astype(BF16)
    ahead = lax.ppermute(across, "seq", earlier)
    taps_part = inverse_dft(table_now, times_conj(grads, data), scale)
    taps_grad = scatter_sum(taps_part, nseq, place, ()).T
    grad_product = (back[length:] + ahead.astype(F32)).astype(BF16)
    grad_keys = mul(grad_product, values)
    grad_values = mul(grad_product, keys)
    return (outputs, grad_queries, grad_keys, grad_values, taps_grad)


def solution(mesh):
    block = P("seq", "tp")
    count = mesh.shape["seq"]
    ring = mesh.shape["tp"] == 1 and count & (count - 1) == 0 and count >= 8

    def run(queries, keys, values, w_out, taps, seg_ids, cotangent):
        rows, chans = queries.shape
        place = on_ring if ring and rows * count == chans else on_device
        return place(queries, keys, values, w_out, taps, seg_ids, cotangent)

    return jax.shard_map(
        run,
        mesh=mesh,
        in_specs=(block, block, block, block, P("tp", None), P(), block),
        out_specs=(block, block, block, block, P(("tp", "seq"), None)),
        check_vma=False,
    )
```

time: 339 us -> 250 us (0.74)
  waiting for transfers between devices: 205 us -> 108 us
  matrix products: 52.1 us -> 31.2 us
  local copies, waits for them, and re-layouts: 20.7 us -> 40.6 us
  Pallas kernels: 0 us -> 13.7 us
  between operations: 15.7 us -> 3.06 us
  starting transfers between devices: 36.4 us -> 43.1 us
    all_gather x1 -> x0, waiting for transfers between devices: 193 us -> none  [on_device(): weights = lax.all_gather(w_out, 'seq', axis=0, tiled=True)]
    ppermute x7 -> x47, waiting for transfers between devices: 11.8 us -> 108 us  [the longest x14 52.7 us: on_ring(): first, second = (send(first, perm=onward), send(second, perm=backward))]
    dot_general x4 -> x8, matrix products: 32.3 us -> 8.52 us  [product_of(): lax.dot_general(cot_pair, weights[step], dims, preferred_element_type=F32)]
    pallas_call x0 -> x6, Pallas kernels: none -> 13.7 us  [the longest x3 11.5 us: project(): pl.pallas_call(functools.partial(project_kernel, len(weights), before is...]
    unnamed x48 -> x143, local copies, waits for them, and re-layouts: 19.1 us -> 32.1 us
    ppermute x7 -> x47, starting transfers between devices: 36.4 us -> 43.1 us  [the longest x8 15.1 us: product_of(): own[step], away[step] = (grad[:rows], send(grad[rows:], perm=swap_pair))]
    slice x0 -> x10, local copies, waits for them, and re-layouts: none -> 4.87 us  [the longest x1 2.26 us: on_ring(): first, second = (w_out[:half], w_out[half:])]
    dot_general x4 -> x6, matrix products: 12 us -> 14.9 us  [inverse_dft(): lax.dot_general(table, spectrum, (((0,), (0,)), ((), ())), precision=lax....]
  transfers between devices with their start and end apart: 8 -> 47, of which waited for: 5 -> 22; matrix products, arithmetic and copies ran while one was open for 12% -> 18% of each run, Pallas kernels for 0% -> 5%
where the time goes in v7:
time: 250 us; the launch traced here: 248 us
  waiting for transfers between devices  108 us (43%)
  starting transfers between devices  43.1 us (17%)
  local copies, waits for them, and re-layouts  40.6 us (16%)
  matrix products  31.2 us (12%)
  Pallas kernels  13.7 us (5%)
  other arithmetic  7.61 us (3%)
  between operations  3.06 us (1%)
    ppermute x14, waiting for transfers between devices, on_ring(): first, second = (send(first, perm=onward), send(second, perm=backward))  52.7 us
    unnamed x143, local copies, waits for them, and re-layouts  32.1 us
    ppermute x4, waiting for transfers between devices, halve(): away = lax.ppermute(away, 'seq', [(i, i ^ bit) for i in range(nseq)])  20.7 us
    ppermute x8, starting transfers between devices, product_of(): own[step], away[step] = (grad[:rows], send(grad[rows:], perm=swap_pair))  15.1 us
    ppermute x14, starting transfers between devices, on_ring(): first, second = (send(first, perm=onward), send(second, perm=backward))  14.9 us
    dot_general x6, matrix products, inverse_dft(): lax.dot_general(table, spectrum, (((0,), (0,)), ((), ())), precision=lax....  14.9 us
    ppermute x1, waiting for transfers between devices, on_ring(): out_away = send(out_away, perm=swap_pair)  13.4 us
    pallas_call x3, Pallas kernels, project(): pl.pallas_call(functools.partial(project_kernel, len(weights), before is...  11.5 us
  transfers between devices with their start and end apart: 47, of which 22 were waited for; matrix products, arithmetic and copies ran while one was open for 18% of the time, Pallas kernels for 5%

profile of v7, /device:TPU:0, one launch (start us, length us, event | category | flops | bytes accessed | tf_op | source)
XLA Modules:
  0.0 247.5 jit_solution(3237934746035486059)
XLA Ops:
  3.4 2.7 %collective-permute-start = (bf16[64,4096]{1,0:T(8,128)(2,1)}, bf16[64,4096]{1,0:T(8,128)(2,1)}, u32[]{:S(2)}, u32[]{:S(2)}) collective-permute-start(bf16[64,4096]{1,0:T(8,128)(2,1)} %get-tuple-element.166), channel_id=1, source_target_pairs={{0,8},{1,9},{2,10},{3,11},{8,16},{9,17},{10,18},{11,19},{16,24},{1... | collective-permute-start | bytes 1572872 | tf_op jit(solution)/shard_map/ppermute | solution.py:305
  8.8 2.6 %copy.33 = bf16[128,4096]{0,1:T(8,128)(2,1)} copy(bf16[128,4096]{1,0:T(8,128)(2,1)} %param.15) | data formatting | bytes 2097152 | tf_op args[2]
  13.8 2.7 %convolution_add_fusion.4 = f32[256,4096]{1,0:T(8,128)} fusion(f32[256,4096]{1,0:T(8,128)S(1)} %fusion.84, bf16[256,128]{1,0:T(8,128)(2,1)S(1)} %copy-done.43, bf16[128,4096]{0,1:T(8,128)(2,1)S(1)} %bitcast.105), kind=kOutput, calls=%fused_computation.9 | convolution fusion | flops 269484032 | bytes 9502720 | tf_op jit(solution)/shard_map/dot_general | solution.py:26
  23.0 8.6 %collective-permute-done.4 = bf16[128,4096]{1,0:T(8,128)(2,1)} collective-permute-done((bf16[128,4096]{1,0:T(8,128)(2,1)}, bf16[128,4096]{1,0:T(8,128)(2,1)}, u32[]{:S(2)}, u32[]{:S(2)}) %collective-permute-start.4) | collective-permute-done | bytes 1048608 | tf_op jit(solution)/shard_map/ppermute | solution.py:272
  31.6 2.5 collective-permute-start.5
  40.7 2.9 %convolution_convert_fusion.7 = bf16[256,256]{1,0:T(8,128)(2,1)S(1)} fusion(bf16[256,4096]{1,0:T(8,128)(2,1)S(1)} %constant_dynamic-update-slice_fusion, bf16[64,4096]{1,0:T(8,128)(2,1)S(1)} %get-tuple-element.164, bf16[64,4096]{1,0:T(8,128)(2,1)} %get-tuple-element.165, bf16[64,4096]{1,0:T(8,128)(2,1)S(1)} %get-tuple-element.163, ...), kind=kOutput, calls=%fused_computation.88 | convolution fusion | flops 545325056 | bytes 4325376 | tf_op jit(solution)/shard_map/dot_general | solution.py:288
  43.7 10.0 %collective-permute-start.7 = (bf16[128,256]{1,0:T(8,128)(2,1)S(1)}, bf16[128,256]{1,0:T(8,128)(2,1)S(1)}, u32[]{:S(2)}, u32[]{:S(2)}) collective-permute-start(bf16[128,256]{1,0:T(8,128)(2,1)S(1)} %get-tuple-element.181), channel_id=1, source_target_pairs={{0,2},{1,3},{2,0},{3,1},{4,6},{5,7},{6,4},{7,5},{8,10},{9,11},{10,... | collective-permute-start | bytes 196616 | tf_op jit(solution)/shard_map/ppermute | solution.py:289
  56.0 2.8 %collective-permute-done.10.refs_5_.refs_31_ = bf16[128,256]{1,0:T(8,128)(2,1)S(1)} collective-permute-done((bf16[128,256]{1,0:T(8,128)(2,1)S(1)}, bf16[128,256]{1,0:T(8,128)(2,1)S(1)}, u32[]{:S(2)}, u32[]{:S(2)}) %collective-permute-start.10) | collective-permute-done | bytes 65568 | tf_op jit(solution)/shard_map/ppermute | solution.py:289
  62.3 8.7 %collective-permute-done.11 = bf16[64,4096]{1,0:T(8,128)(2,1)S(1)} collective-permute-done((bf16[64,4096]{1,0:T(8,128)(2,1)S(1)}, bf16[64,4096]{1,0:T(8,128)(2,1)S(1)}, u32[]{:S(2)}, u32[]{:S(2)}) %collective-permute-start.11) | collective-permute-done | bytes 524320 | tf_op jit(solution)/shard_map/ppermute | solution.py:305
  73.6 3.3 %collective-permute-done.15.refs_9_.refs_27_ = bf16[128,256]{1,0:T(8,128)(2,1)S(1)} collective-permute-done((bf16[128,256]{1,0:T(8,128)(2,1)S(1)}, bf16[128,256]{1,0:T(8,128)(2,1)S(1)}, u32[]{:S(2)}, u32[]{:S(2)}) %collective-permute-start.15) | collective-permute-done | bytes 65568 | tf_op jit(solution)/shard_map/ppermute | solution.py:289
  80.5 10.0 %collective-permute-done.16 = bf16[64,4096]{1,0:T(8,128)(2,1)S(1)} collective-permute-done((bf16[64,4096]{1,0:T(8,128)(2,1)S(1)}, bf16[64,4096]{1,0:T(8,128)(2,1)S(1)}, u32[]{:S(2)}, u32[]{:S(2)}) %collective-permute-start.16) | collective-permute-done | bytes 524320 | tf_op jit(solution)/shard_map/ppermute | solution.py:305
  95.9 11.5 %collective-permute-done.21 = bf16[64,4096]{1,0:T(8,128)(2,1)S(1)} collective-permute-done((bf16[64,4096]{1,0:T(8,128)(2,1)S(1)}, bf16[64,4096]{1,0:T(8,128)(2,1)S(1)}, u32[]{:S(2)}, u32[]{:S(2)}) %collective-permute-start.21) | collective-permute-done | bytes 524320 | tf_op jit(solution)/shard_map/ppermute | solution.py:305
  113.2 3.0 %collective-permute-done.25.refs_17_.refs_19_ = bf16[128,256]{1,0:T(8,128)(2,1)S(1)} collective-permute-done((bf16[128,256]{1,0:T(8,128)(2,1)S(1)}, bf16[128,256]{1,0:T(8,128)(2,1)S(1)}, u32[]{:S(2)}, u32[]{:S(2)}) %collective-permute-start.25) | collective-permute-done | bytes 65568 | tf_op jit(solution)/shard_map/ppermute | solution.py:289
  119.5 2.8 %fusion.12 = (bf16[128,4096]{1,0:T(8,128)(2,1)S(1)}, f32[128,4096]{1,0:T(8,128)}) fusion(bf16[128,4096]{1,0:T(8,128)(2,1)S(1)} %copy-done.36, f32[4096,128]{0,1:T(8,128)S(1)} %fusion.36, f32[128,128]{1,0:T(8,128)S(1)} %copy-done.49, f32[256,4096]{1,0:T(8,128)S(1)} %fusion.4, f32[256,4096]{1,0:T(8,128)S(1)} %copy-done.30), kind=kOutput, calls=%fused_computation.25 | convolution fusion | flops 407896064 | bytes 14745600 | tf_op jit(solution)/shard_map/dot_general | solution.py:43
  123.1 5.9 %collective-permute-done.26 = bf16[64,4096]{1,0:T(8,128)(2,1)S(1)} collective-permute-done((bf16[64,4096]{1,0:T(8,128)(2,1)S(1)}, bf16[64,4096]{1,0:T(8,128)(2,1)S(1)}, u32[]{:S(2)}, u32[]{:S(2)}) %collective-permute-start.26) | collective-permute-done | bytes 524320 | tf_op jit(solution)/shard_map/ppermute | solution.py:305
  135.5 4.5 %shard_map.165.refs_3_ = f32[256,4096]{1,0:T(8,128)S(1)} custom-call(s32[9]{0:T(128)S(1)} %stack.153.scalars, bf16[8,128,256]{2,1,0:T(8,128)(2,1)S(1)} %get-tuple-element.116.gated_own, bf16[8,128,256]{2,1,0:T(8,128)(2,1)S(1)} %collective-permute-done.34.gated_away, bf16[256,4096]{1,0:T(8,128)(2,1)S(1)} %pad_maximum_fusion.refs_0_, ...), custom_call_target="tpu_custom_call" | custom-call | flops 2147483648 | bytes 13631488 | tf_op jit(solution)/shard_map/pallas_call | solution.py:224
  145.4 11.3 %collective-permute-done.35 = bf16[64,4096]{1,0:T(8,128)(2,1)} collective-permute-done((bf16[64,4096]{1,0:T(8,128)(2,1)S(1)}, bf16[64,4096]{1,0:T(8,128)(2,1)}, u32[]{:S(2)}, u32[]{:S(2)}) %collective-permute-start.35) | collective-permute-done | bytes 524320 | tf_op jit(solution)/shard_map/ppermute | solution.py:305
  162.8 4.1 %shard_map.166.refs_1_ = f32[256,4096]{1,0:T(8,128)S(1)} custom-call(s32[7]{0:T(128)S(1)} %stack.155.scalars, bf16[8,128,256]{2,1,0:T(8,128)(2,1)S(1)} %get-tuple-element.116.gated_own, bf16[8,128,256]{2,1,0:T(8,128)(2,1)S(1)} %collective-permute-done.34.gated_away, bf16[256,4096]{1,0:T(8,128)(2,1)S(1)} %get-tuple-element.187.refs_0_, ...), custom_call_target="tpu_custom_call" | custom-call | flops 1610612736 | bytes 11534336 | tf_op jit(solution)/shard_map/pallas_call | solution.py:224
  178.5 2.8 %shard_map.167 = (f32[128,4096]{1,0:T(8,128)S(1)}, bf16[128,4096]{1,0:T(8,128)(2,1)S(1)}) custom-call(s32[3]{0:T(128)S(1)} %pad_add_fusion.scalars, bf16[8,128,256]{2,1,0:T(8,128)(2,1)S(1)} %get-tuple-element.116.gated_own, bf16[8,128,256]{2,1,0:T(8,128)(2,1)S(1)} %collective-permute-done.34.gated_away, ...), custom_call_target="tpu_custom_call" | custom-call | flops 536870912 | bytes 7340032 | tf_op jit(solution)/shard_map/pallas_call | solution.py:224
  191.1 5.9 %fusion.29 = f32[4096,256]{1,0:T(8,128)S(1)} fusion(f32[128,256]{1,0:T(8,128)S(1)} %copy-done.54, f32[256,4096]{1,0:T(8,128)} %copy-done.34, f32[256,4096]{1,0:T(8,128)} %convolution_add_fusion.4), kind=kOutput, calls=%fused_computation.45 | convolution fusion | flops 806879232 | bytes 12713984 | tf_op jit(solution)/shard_map/dot_general | solution.py:43
  203.2 16.3 %collective-permute-done.43 = bf16[1,8,128,128]{3,2,1,0:T(8,128)(2,1)S(1)} collective-permute-done((bf16[1,8,128,128]{3,2,1,0:T(8,128)(2,1)S(1)}, bf16[1,8,128,128]{3,2,1,0:T(8,128)(2,1)S(1)}, u32[]{:S(2)}, u32[]{:S(2)}) %collective-permute-start.43) | collective-permute-done | bytes 262176 | tf_op jit(solution)/shard_map/ppermute | solution.py:83
  221.0 2.5 %collective-permute-start.40 = (bf16[128,4096]{1,0:T(8,128)(2,1)S(1)}, bf16[128,4096]{1,0:T(8,128)(2,1)S(1)}, u32[]{:S(2)}, u32[]{:S(2)}) collective-permute-start(bf16[128,4096]{1,0:T(8,128)(2,1)S(1)} %copy-done.29), channel_id=1, source_target_pairs={{0,2},{1,3},{2,0},{3,1},{4,6},{5,7},{6,4},{7,5},{8,10},{9,11},{10,... | collective-permute-start | bytes 3145736 | tf_op jit(solution)/shard_map/ppermute | solution.py:333
  225.9 3.2 %collective-permute-done.45 = bf16[2,128,128]{2,1,0:T(8,128)(2,1)S(1)} collective-permute-done((bf16[2,128,128]{2,1,0:T(8,128)(2,1)S(1)}, bf16[2,128,128]{2,1,0:T(8,128)(2,1)S(1)}, u32[]{:S(2)}, u32[]{:S(2)}) %collective-permute-start.45) | collective-permute-done | bytes 65568 | tf_op jit(solution)/shard_map/ppermute | solution.py:83
  229.6 13.4 %collective-permute-done.40 = bf16[128,4096]{1,0:T(8,128)(2,1)S(1)} collective-permute-done((bf16[128,4096]{1,0:T(8,128)(2,1)S(1)}, bf16[128,4096]{1,0:T(8,128)(2,1)S(1)}, u32[]{:S(2)}, u32[]{:S(2)}) %collective-permute-start.40) | collective-permute-done | bytes 1048608 | tf_op jit(solution)/shard_map/ppermute | solution.py:333
  (278 shorter events, 100.2 us)
Async XLA Ops:
  0.7 31.0 %collective-permute-start.6 = (bf16[128,4096]{1,0:T(8,128)(2,1)}, bf16[128,4096]{1,0:T(8,128)(2,1)}, u32[]{:S(2)}, u32[]{:S(2)}) collective-permute-start(bf16[128,4096]{1,0:T(8,128)(2,1)} %param.16), channel_id=1, source_target_pairs={{0,1},{1,0},{2,3},{3,2},{4,5},{5,4},{6,7},{7,6},{8,9},{9,8},{10,11... | collective-permute-start | bytes 3145736 | tf_op jit(solution)/shard_map/ppermute | solution.py:273
  3.4 16.4 %collective-permute-start = (bf16[64,4096]{1,0:T(8,128)(2,1)}, bf16[64,4096]{1,0:T(8,128)(2,1)}, u32[]{:S(2)}, u32[]{:S(2)}) collective-permute-start(bf16[64,4096]{1,0:T(8,128)(2,1)} %get-tuple-element.166), channel_id=1, source_target_pairs={{0,8},{1,9},{2,10},{3,11},{8,16},{9,17},{10,18},{11,19},{16,24},{1... | collective-permute-start | bytes 1572872 | tf_op jit(solution)/shard_map/ppermute | solution.py:305
  6.2 15.3 %collective-permute-start.2 = (bf16[64,4096]{1,0:T(8,128)(2,1)}, bf16[64,4096]{1,0:T(8,128)(2,1)}, u32[]{:S(2)}, u32[]{:S(2)}) collective-permute-start(bf16[64,4096]{1,0:T(8,128)(2,1)} %get-tuple-element.165), channel_id=1, source_target_pairs={{8,0},{9,1},{10,2},{11,3},{16,8},{17,9},{18,10},{19,11},{24,16},{2... | collective-permute-start | bytes 1572872 | tf_op jit(solution)/shard_map/ppermute | solution.py:305
  6.2 25.4 %collective-permute-start.4 = (bf16[128,4096]{1,0:T(8,128)(2,1)}, bf16[128,4096]{1,0:T(8,128)(2,1)}, u32[]{:S(2)}, u32[]{:S(2)}) collective-permute-start(bf16[128,4096]{1,0:T(8,128)(2,1)} %param.19), channel_id=1, source_target_pairs={{0,2},{1,3},{2,0},{3,1},{4,6},{5,7},{6,4},{7,5},{8,10},{9,11},{10,... | collective-permute-start | bytes 3145736 | tf_op jit(solution)/shard_map/ppermute | solution.py:272
  19.9 15.5 %collective-permute-start.1 = (bf16[64,4096]{1,0:T(8,128)(2,1)}, bf16[64,4096]{1,0:T(8,128)(2,1)S(1)}, u32[]{:S(2)}, u32[]{:S(2)}) collective-permute-start(bf16[64,4096]{1,0:T(8,128)(2,1)} %collective-permute-done), channel_id=1, source_target_pairs={{0,8},{1,9},{2,10},{3,11},{8,16},{9,17},{10,18},{11,19},{16,24},{1... | collective-permute-start | bytes 1572872 | tf_op jit(solution)/shard_map/ppermute | solution.py:305
  21.5 16.6 %collective-permute-start.8 = (bf16[64,4096]{1,0:T(8,128)(2,1)}, bf16[64,4096]{1,0:T(8,128)(2,1)S(1)}, u32[]{:S(2)}, u32[]{:S(2)}) collective-permute-start(bf16[64,4096]{1,0:T(8,128)(2,1)} %collective-permute-done), channel_id=1, source_target_pairs={{0,1},{1,0},{2,3},{3,2},{4,5},{5,4},{6,7},{7,6},{8,9},{9,8},{10,11... | collective-permute-start | bytes 1572872 | tf_op jit(solution)/shard_map/ppermute | solution.py:306
  21.5 15.2 %collective-permute-start.3 = (bf16[64,4096]{1,0:T(8,128)(2,1)}, bf16[64,4096]{1,0:T(8,128)(2,1)S(1)}, u32[]{:S(2)}, u32[]{:S(2)}) collective-permute-start(bf16[64,4096]{1,0:T(8,128)(2,1)} %collective-permute-done.2), channel_id=1, source_target_pairs={{8,0},{9,1},{10,2},{11,3},{16,8},{17,9},{18,10},{19,11},{24,16},{2... | collective-permute-start | bytes 1572872 | tf_op jit(solution)/shard_map/ppermute | solution.py:305
  43.7 12.3 %collective-permute-start.7 = (bf16[128,256]{1,0:T(8,128)(2,1)S(1)}, bf16[128,256]{1,0:T(8,128)(2,1)S(1)}, u32[]{:S(2)}, u32[]{:S(2)}) collective-permute-start(bf16[128,256]{1,0:T(8,128)(2,1)S(1)} %get-tuple-element.181), channel_id=1, source_target_pairs={{0,2},{1,3},{2,0},{3,1},{4,6},{5,7},{6,4},{7,5},{8,10},{9,11},{10,... | collective-permute-start | bytes 196616 | tf_op jit(solution)/shard_map/ppermute | solution.py:289
  76.9 13.6 %collective-permute-start.16 = (bf16[64,4096]{1,0:T(8,128)(2,1)S(1)}, bf16[64,4096]{1,0:T(8,128)(2,1)S(1)}, u32[]{:S(2)}, u32[]{:S(2)}) collective-permute-start(bf16[64,4096]{1,0:T(8,128)(2,1)S(1)} %collective-permute-done.11), channel_id=1, source_target_pairs={{0,8},{1,9},{2,10},{3,11},{8,16},{9,17},{10,18},{11,19},{16,24},{1... | collective-permute-start | bytes 1572872 | tf_op jit(solution)/shard_map/ppermute | solution.py:305
  78.4 13.3 %collective-permute-start.17 = (bf16[64,4096]{1,0:T(8,128)(2,1)S(1)}, bf16[64,4096]{1,0:T(8,128)(2,1)S(1)}, u32[]{:S(2)}, u32[]{:S(2)}) collective-permute-start(bf16[64,4096]{1,0:T(8,128)(2,1)S(1)} %collective-permute-done.12), channel_id=1, source_target_pairs={{8,0},{9,1},{10,2},{11,3},{16,8},{17,9},{18,10},{19,11},{24,16},{2... | collective-permute-start | bytes 1572872 | tf_op jit(solution)/shard_map/ppermute | solution.py:305
  79.9 12.6 %collective-permute-start.20 = (bf16[128,256]{1,0:T(8,128)(2,1)S(1)}, bf16[128,256]{1,0:T(8,128)(2,1)S(1)}, u32[]{:S(2)}, u32[]{:S(2)}) collective-permute-start(bf16[128,256]{1,0:T(8,128)(2,1)S(1)} %get-tuple-element.175), channel_id=1, source_target_pairs={{0,2},{1,3},{2,0},{3,1},{4,6},{5,7},{6,4},{7,5},{8,10},{9,11},{10,... | collective-permute-start | bytes 196616 | tf_op jit(solution)/shard_map/ppermute | solution.py:289
  93.1 14.3 %collective-permute-start.21 = (bf16[64,4096]{1,0:T(8,128)(2,1)S(1)}, bf16[64,4096]{1,0:T(8,128)(2,1)S(1)}, u32[]{:S(2)}, u32[]{:S(2)}) collective-permute-start(bf16[64,4096]{1,0:T(8,128)(2,1)S(1)} %collective-permute-done.16), channel_id=1, source_target_pairs={{0,8},{1,9},{2,10},{3,11},{8,16},{9,17},{10,18},{11,19},{16,24},{1... | collective-permute-start | bytes 1572872 | tf_op jit(solution)/shard_map/ppermute | solution.py:305
  94.6 14.1 %collective-permute-start.22 = (bf16[64,4096]{1,0:T(8,128)(2,1)S(1)}, bf16[64,4096]{1,0:T(8,128)(2,1)S(1)}, u32[]{:S(2)}, u32[]{:S(2)}) collective-permute-start(bf16[64,4096]{1,0:T(8,128)(2,1)S(1)} %collective-permute-done.17), channel_id=1, source_target_pairs={{8,0},{9,1},{10,2},{11,3},{16,8},{17,9},{18,10},{19,11},{24,16},{2... | collective-permute-start | bytes 1572872 | tf_op jit(solution)/shard_map/ppermute | solution.py:305
  116.2 12.8 %collective-permute-start.26 = (bf16[64,4096]{1,0:T(8,128)(2,1)S(1)}, bf16[64,4096]{1,0:T(8,128)(2,1)S(1)}, u32[]{:S(2)}, u32[]{:S(2)}) collective-permute-start(bf16[64,4096]{1,0:T(8,128)(2,1)S(1)} %collective-permute-done.21), channel_id=1, source_target_pairs={{0,8},{1,9},{2,10},{3,11},{8,16},{9,17},{10,18},{11,19},{16,24},{1... | collective-permute-start | bytes 1572872 | tf_op jit(solution)/shard_map/ppermute | solution.py:305
  117.2 12.5 %collective-permute-start.27 = (bf16[64,4096]{1,0:T(8,128)(2,1)S(1)}, bf16[64,4096]{1,0:T(8,128)(2,1)S(1)}, u32[]{:S(2)}, u32[]{:S(2)}) collective-permute-start(bf16[64,4096]{1,0:T(8,128)(2,1)S(1)} %collective-permute-done.22), channel_id=1, source_target_pairs={{8,0},{9,1},{10,2},{11,3},{16,8},{17,9},{18,10},{19,11},{24,16},{2... | collective-permute-start | bytes 1572872 | tf_op jit(solution)/shard_map/ppermute | solution.py:305
  122.5 13.0 %collective-permute-start.34 = (bf16[8,128,256]{2,1,0:T(8,128)(2,1)S(1)}, bf16[8,128,256]{2,1,0:T(8,128)(2,1)S(1)}, u32[]{:S(2)}, u32[]{:S(2)}) collective-permute-start(bf16[8,128,256]{2,1,0:T(8,128)(2,1)S(1)} %get-tuple-element.117), channel_id=1, source_target_pairs={{0,2},{1,3},{2,0},{3,1},{4,6},{5,7},{6,4},{7,5},{8,10},{9,11},{10,... | collective-permute-start | bytes 1572872 | tf_op jit(solution)/shard_map/ppermute | solution.py:325
  143.4 13.4 %collective-permute-start.35 = (bf16[64,4096]{1,0:T(8,128)(2,1)S(1)}, bf16[64,4096]{1,0:T(8,128)(2,1)}, u32[]{:S(2)}, u32[]{:S(2)}) collective-permute-start(bf16[64,4096]{1,0:T(8,128)(2,1)S(1)} %collective-permute-done.26), channel_id=1, source_target_pairs={{0,8},{1,9},{2,10},{3,11},{8,16},{9,17},{10,18},{11,19},{16,24},{1... | collective-permute-start | bytes 1572872 | tf_op jit(solution)/shard_map/ppermute | solution.py:305
  144.4 13.0 %collective-permute-start.37 = (bf16[64,4096]{1,0:T(8,128)(2,1)S(1)}, bf16[64,4096]{1,0:T(8,128)(2,1)}, u32[]{:S(2)}, u32[]{:S(2)}) collective-permute-start(bf16[64,4096]{1,0:T(8,128)(2,1)S(1)} %collective-permute-done.27), channel_id=1, source_target_pairs={{8,0},{9,1},{10,2},{11,3},{16,8},{17,9},{18,10},{19,11},{24,16},{2... | collective-permute-start | bytes 1572872 | tf_op jit(solution)/shard_map/ppermute | solution.py:305
  156.7 12.3 %collective-permute-start.36 = (bf16[64,4096]{1,0:T(8,128)(2,1)}, bf16[64,4096]{1,0:T(8,128)(2,1)}, u32[]{:S(2)}, u32[]{:S(2)}) collective-permute-start(bf16[64,4096]{1,0:T(8,128)(2,1)} %collective-permute-done.35), channel_id=1, source_target_pairs={{0,1},{1,0},{2,3},{3,2},{4,5},{5,4},{6,7},{7,6},{8,9},{9,8},{10,11... | collective-permute-start | bytes 1572872 | tf_op jit(solution)/shard_map/ppermute | solution.py:306
  157.4 11.7 %collective-permute-start.38 = (bf16[64,4096]{1,0:T(8,128)(2,1)}, bf16[64,4096]{1,0:T(8,128)(2,1)}, u32[]{:S(2)}, u32[]{:S(2)}) collective-permute-start(bf16[64,4096]{1,0:T(8,128)(2,1)} %collective-permute-done.37), channel_id=1, source_target_pairs={{0,1},{1,0},{2,3},{3,2},{4,5},{5,4},{6,7},{7,6},{8,9},{9,8},{10,11... | collective-permute-start | bytes 1572872 | tf_op jit(solution)/shard_map/ppermute | solution.py:306
  200.8 18.8 %collective-permute-start.43 = (bf16[1,8,128,128]{3,2,1,0:T(8,128)(2,1)S(1)}, bf16[1,8,128,128]{3,2,1,0:T(8,128)(2,1)S(1)}, u32[]{:S(2)}, u32[]{:S(2)}) collective-permute-start(bf16[1,8,128,128]{3,2,1,0:T(8,128)(2,1)S(1)} %dynamic-slice_convert_fusion), channel_id=1, source_target_pairs={{0,2},{1,3},{2,0},{3,1},{4,6},{5,7},{6,4},{7,5},{8,10},{9,11},{10,... | collective-permute-start | bytes 786440 | tf_op jit(solution)/shard_map/ppermute | solution.py:83
  201.9 23.3 %collective-permute-start.41 = (bf16[128,4096]{0,1:T(8,128)(2,1)S(1)}, bf16[128,4096]{0,1:T(8,128)(2,1)S(1)}, u32[]{:S(2)}, u32[]{:S(2)}) collective-permute-start(bf16[128,4096]{0,1:T(8,128)(2,1)S(1)} %fusion.17), channel_id=1, source_target_pairs={{1,0},{2,1},{3,2},{4,3},{5,4},{6,5},{7,6},{8,7},{9,8},{10,9},{11,1... | collective-permute-start | bytes 3145736 | tf_op jit(solution)/shard_map/ppermute | solution.py:346
  221.0 22.0 %collective-permute-start.40 = (bf16[128,4096]{1,0:T(8,128)(2,1)S(1)}, bf16[128,4096]{1,0:T(8,128)(2,1)S(1)}, u32[]{:S(2)}, u32[]{:S(2)}) collective-permute-start(bf16[128,4096]{1,0:T(8,128)(2,1)S(1)} %copy-done.29), channel_id=1, source_target_pairs={{0,2},{1,3},{2,0},{3,1},{4,6},{5,7},{6,4},{7,5},{8,10},{9,11},{10,... | collective-permute-start | bytes 3145736 | tf_op jit(solution)/shard_map/ppermute | solution.py:333
  229.1 17.7 %collective-permute-start.46 = (bf16[1,128,128]{2,1,0:T(8,128)(2,1)S(1)}, bf16[1,128,128]{2,1,0:T(8,128)(2,1)S(1)}, u32[]{:S(2)}, u32[]{:S(2)}) collective-permute-start(bf16[1,128,128]{2,1,0:T(8,128)(2,1)S(1)} %dynamic-slice_convert_fusion.2), channel_id=1, source_target_pairs={{0,16},{1,17},{2,18},{3,19},{4,20},{5,21},{6,22},{7,23},{8,24},{9,... | collective-permute-start | bytes 98312 | tf_op jit(solution)/shard_map/ppermute | solution.py:83
  (81 other events, 475.0 us)
